TPU v7x, 32 devices: a whole 2x2x4 slice. The times are simulated.
32 devices in a mesh: sec: 2 (over core), seq: 8 (over z, x), tp: 2 (over y).
Axes of the slice: x: 2, y: 2, z: 4, core: 2. Of those that a mesh axis runs over, the one named last changes fastest.
Arguments:
- hidden_rows: bfloat16 [2, 512, 5120], P('sec', 'seq'), may hold values from -10 to 10
- carried: bfloat16 [2, 512, 5120], P('sec', 'seq'), may hold values from -6 to 6
- query_weight: bfloat16 [2, 5120, 4096], P('sec', 'seq', 'tp'), may hold values from -6 to 6
- response_cache: bfloat16 [2, 512, 2048], P('sec', 'seq', 'tp'), may hold values from -8.375 to 8.375
- prompt_cache: bfloat16 [2, 8, 16384, 2048], P('sec', None, 'seq', 'tp'), may hold values from -5 to 5
- prompt_lengths: int32 [8], replicated, may hold values from 1 to 16384, 81920 in all
- response_lengths: int32 [2, 8], replicated, may hold values from 1 to 64, 320 in all within a row
- block_prompts: int32 [2, 8, 1], replicated, may hold values from 0 to 7
Outputs:
- attended: bfloat16 [2, 512, 4096], P('sec', 'seq', 'tp')
All inputs are finite; a program needn't handle non-finite values.
Results may differ from a plain program's by a relative error of at most 0.0096.
Values may be sent and summed in bfloat16 or wider, within the bound.
No kernel may reach another device: no remote copies, remote signals or barrier semaphores. Data moves between devices by JAX's collectives and lax.ppermute only.
A program may use at most 192 MiB of HBM per device.

v0:
```python
import math

import jax
import jax.numpy as jnp
from jax import lax
from jax.sharding import PartitionSpec as P

H = 32
KVH = 8
HD = 128


NEG_FILL = -1e30


def from_behind(value, axis, steps):
    count = lax.axis_size(axis)
    first, last = (max(0, -steps), min(count, count - steps))
    return lax.ppermute(value, axis, [(source, source + steps) for source in range(first, last)])


def partial_attend(queries, key_rows, value_rows, key_valid):
    score_scale = queries.shape[-1] ** (-0.5)
    scores = (
        jnp.einsum("rgqd,kgd->rgqk", queries, key_rows, preferred_element_type=jnp.float32)
        * score_scale
    )
    key_mask = key_valid[:, None, None, :]
    row_peak = jnp.max(jnp.where(key_mask, scores, NEG_FILL), axis=-1)
    weights = jnp.where(key_mask, jnp.exp(scores - row_peak[..., None]), 0.0).astype(jnp.bfloat16)
    row_total = jnp.sum(weights.astype(jnp.float32), axis=-1)
    row_sum = jnp.einsum("rgqk,kgd->rgqd", weights, value_rows, preferred_element_type=jnp.float32)
    return (row_peak, row_total, row_sum)


def shards(
    hidden_rows,
    carried,
    query_weight,
    response_cache,
    prompt_cache,
    prompt_lengths,
    response_lengths,
    block_prompts,
):
    section = lax.axis_index("sec")
    shard_index = lax.axis_index("seq")
    shard_count = lax.axis_size("seq")
    rows = hidden_rows.shape[1]
    local_kv = response_cache.shape[2] // (2 * HD)
    ratio = H // KVH
    handed = from_behind(carried, "sec", 1)
    inputs = (hidden_rows[0].astype(jnp.float32) + handed[0].astype(jnp.float32)).astype(
        jnp.bfloat16
    )
    projected = jnp.dot(
        inputs,
        lax.all_gather(query_weight[0], "seq", axis=0, tiled=True),
        preferred_element_type=jnp.float32,
    )
    queries = projected.astype(jnp.bfloat16).reshape(rows, local_kv, ratio, HD)
    own_cache = response_cache[0].reshape(rows, local_kv, 2, HD)
    order = jnp.arange(rows, dtype=jnp.int32)
    causal = order[:, None] >= order[None, :]
    own_part = partial_attend(queries, own_cache[:, :, 0], own_cache[:, :, 1], causal)
    section_prompts = lax.dynamic_index_in_dim(block_prompts, section, 0, keepdims=False)[:, 0]
    section_lengths = lax.dynamic_index_in_dim(response_lengths, section, 0, keepdims=False)
    my_length = section_lengths[shard_index]
    prompt_tiles = prompt_cache[0]
    tile_len = prompt_tiles.shape[1]
    gathered = lax.all_gather(queries, "seq", axis=0, tiled=True)
    group = math.gcd(shard_count, 4)
    grouped_queries = gathered.reshape(shard_count // group, group, rows, local_kv, ratio, HD)
    grouped_prompts = section_prompts.reshape(shard_count // group, group)
    positions = shard_index * tile_len + jnp.arange(tile_len, dtype=jnp.int32)

    def tile_parts(tile_inputs):
        group_queries, group_prompts = tile_inputs
        group_cache = jnp.take(prompt_tiles, group_prompts, axis=0).reshape(
            group, tile_len, local_kv, 2, HD
        )
        key_valid = (positions[None, :] < prompt_lengths[group_prompts][:, None])[:, None, :]
        return jax.vmap(partial_attend)(
            group_queries, group_cache[:, :, :, 0], group_cache[:, :, :, 1], key_valid
        )

    parts = lax.map(tile_parts, (grouped_queries, grouped_prompts))
    peaks = parts[0].reshape((shard_count,) + parts[0].shape[2:])
    totals = parts[1].reshape((shard_count,) + parts[1].shape[2:])
    sums = parts[2].reshape((shard_count,) + parts[2].shape[2:])
    returned = (
        lax.all_to_all(peaks, "seq", split_axis=0, concat_axis=0, tiled=True),
        lax.all_to_all(totals, "seq", split_axis=0, concat_axis=0, tiled=True),
        lax.all_to_all(sums, "seq", split_axis=0, concat_axis=0, tiled=True),
    )
    row_peak = jnp.maximum(own_part[0], jnp.max(returned[0], axis=0))
    own_scale = jnp.exp(own_part[0] - row_peak)
    far_scale = jnp.exp(returned[0] - row_peak[None])
    merged = (
        row_peak,
        own_part[1] * own_scale + jnp.sum(returned[1] * far_scale, axis=0),
        own_part[2] * own_scale[..., None] + jnp.sum(returned[2] * far_scale[..., None], axis=0),
    )
    output = merged[2] / merged[1][..., None]
    output = jnp.where((order < my_length)[:, None, None, None], output, 0.0)
    return output.reshape(1, rows, local_kv * ratio * HD).astype(jnp.bfloat16)


def solution(mesh):
    placed = (
        P("sec", "seq", None),
        P("sec", "seq", None),
        P("sec", "seq", "tp"),
        P("sec", "seq", "tp"),
        P("sec", None, "seq", "tp"),
        P(),
        P(),
        P(),
    )
    return jax.shard_map(
        shards, mesh=mesh, in_specs=placed, out_specs=P("sec", "seq", "tp"), check_vma=False
    )
```

profile of v0, /device:TPU:0, one launch (start us, length us, event | category | flops | bytes accessed | tf_op | source)
XLA Modules:
  0.0 935.1 jit_solution(12797706329737312130)
XLA Ops:
  6.5 0.7 all-gather.6.cloned.1.call-update
  7.3 2.4 collective-permute-start
  9.7 1.9 collective-permute-done
  11.6 401.8 %all-gather.6.cloned.1.call-done = bf16[1,5120,2048]{2,1,0:T(8,128)(2,1)} async-done(((bf16[1,640,2048]{2,1,0:T(8,128)(2,1)}), bf16[1,5120,2048]{2,1,0:T(8,128)(2,1)}) %all-gather.6.cloned.1.call-update) | async-done | bytes 20971536 | tf_op jit(solution)/shard_map/all_gather | solution.py:58
  413.4 10.9 %fusion.14 = bf16[64,2048]{1,0:T(8,128)(2,1)S(1)} fusion(bf16[1,5120,2048]{2,1,0:T(8,128)(2,1)} %all-gather.6.cloned.1.call-done, bf16[1,64,5120]{2,1,0:T(8,128)(2,1)S(1)} %collective-permute-done, bf16[1,64,5120]{2,1,0:T(8,128)(2,1)} %param.10), kind=kOutput, calls=%fused_computation.36 | convolution fusion | flops 1343619072 | bytes 22544384 | tf_op jit(solution)/shard_map/dot_general | solution.py:56
  424.6 0.8 copy.22
  425.5 49.2 %all-gather.4.cloned.1.call-done = bf16[512,4,4,128]{3,0,2,1:T(8,128)(2,1)} async-done(((bf16[64,4,4,128]{3,0,2,1:T(8,128)(2,1)}), bf16[512,4,4,128]{3,0,2,1:T(8,128)(2,1)}) %all-gather.4.cloned.1.call-update) | async-done | bytes 2097168 | tf_op jit(solution)/shard_map/all_gather | solution.py:71
  474.8 334.1 %while.15 = (s32[]{:T(128)}, f32[2,4,64,4,4]{2,4,3,1,0:T(4,128)S(1)}, f32[2,4,64,4,4]{2,4,3,1,0:T(4,128)S(1)}, f32[2,4,64,4,4,128]{5,2,4,3,1,0:T(8,128)}, s32[2,...) while((s32[]{:T(128)}, ...), condition=%wide.region_4.5_spmd.clone, body=%wide.region_1.4_spmd.clone.sunk | while | flops 4462742528 | bytes 364107072 | solution.py:87
  475.0 17.5 %fusion.35 = (bf16[8,768,1024]{2,1,0:T(8,128)(2,1)}, bf16[8,768,1024]{2,1,0:T(8,128)(2,1)}) fusion(bf16[8,2048,1024]{2,1,0:T(8,128)(2,1)} %get-tuple-element.223), kind=kLoop, calls=%fused_computation.61.clone.1 | loop fusion | bytes 50331648 | tf_op jit(solution)/shard_map/while/body/eval_jaxpr/jit(_take)/gather | solution.py:79
  492.5 8.2 gather_fusion.2
  500.8 8.2 gather_fusion.3
  508.9 7.6 mini-gather-slice.13
  516.5 6.2 gather_fusion.1
  522.7 13.6 %pad_maximum_fusion.2 = bf16[4,2048,1024]{2,1,0:T(8,128)(2,1)} fusion(bf16[4,512,1024]{2,1,0:T(8,128)(2,1)} %gather_fusion.1, bf16[4,768,1024]{2,1,0:T(8,128)(2,1)} %gather_fusion.2, bf16[4,768,1024]{2,1,0:T(8,128)(2,1)} %gather_fusion.3), kind=kLoop, calls=%fused_computation.12.clone.1 | loop fusion | flops 50331648 | bytes 33554432 | tf_op jit(solution)/shard_map/while
  536.3 21.9 %copy.54 = bf16[4,2048,1024]{1,2,0:T(8,128)(2,1)} copy(bf16[4,2048,1024]{2,1,0:T(8,128)(2,1)} %pad_maximum_fusion.2) | data formatting | bytes 33554432 | tf_op jit(solution)/shard_map/while
  558.2 21.7 %copy.55 = bf16[4,2048,4,2,128]{4,1,2,0,3:T(8,128)(2,1)} copy(bf16[4,2048,4,2,128]{1,4,3,2,0:T(8,128)(2,1)} %bitcast.129) | data formatting | bytes 33554432 | tf_op jit(solution)/shard_map/while/body/eval_jaxpr/jit(_take)/gather | solution.py:79
  579.9 14.3 %broadcast_select_fusion.2 = bf16[4,2048,4,2,128]{4,1,2,0,3:T(8,128)(2,1)} fusion(bf16[4,2048,4,2,128]{4,1,2,0,3:T(8,128)(2,1)} %copy.55, pred[4]{0:T(512)(128)(4,1)S(1)} %compare_and_fusion.2), kind=kLoop, calls=%fused_computation.13.clone.1 | loop fusion | flops 8388608 | bytes 33554436 | tf_op jit(solution)/shard_map/while/body/eval_jaxpr/jit(_take)/select_n | solution.py:79
  594.1 0.6 gather_fusion
  594.9 15.4 %fusion.36 = (f32[4,64,4,4]{1,3,2,0:T(4,128)S(1)}, f32[4,4,2048,64,4]{2,3,4,1,0:T(8,128)}) fusion(pred[4,2048]{1,0:T(4,128)(4,1)S(1)} %broadcast_compare_fusion.2, bf16[4,2048,4,2,128]{4,1,2,0,3:T(8,128)(2,1)} %broadcast_select_fusion.2, bf16[2,4,64,4,4,128]{5,2,1,0,4,3:T(8,128)(2,1)S(1)} %copy-done.6, s32[]{:T(128)} %get-tuple-element.207), kind=kOutput, calls=%fused_computation.7.clone.1 | convolution fusion | flops 2172645376 | bytes 43016704 | tf_op jit(solution)/shard_map/while/body/eval_jaxpr/vmap(rgqd,kgd->rgqk)/dot_general | solution.py:25
  610.3 16.9 %bitcast_dynamic-update-slice_fusion.6 = f32[2,4,64,4,4,128]{5,2,4,3,1,0:T(8,128)} fusion(f32[2,4,64,4,4,128]{5,2,4,3,1,0:T(8,128)} %get-tuple-element.210, s32[]{:T(128)} %get-tuple-element.207, bf16[4,2048,4,2,128]{4,1,2,0,3:T(8,128)(2,1)} %broadcast_select_fusion.2, f32[4,4,2048,64,4]{2,3,4,1,0:T(8,128)} %get-tuple-element.194, ...), kind=kOutput, calls=%fused_computation.18.clone.1 | convolution fusion | flops 2181038080 | bytes 44065280 | tf_op jit(solution)/shard_map/while/body/eval_jaxpr/vmap(rgqk,kgd->rgqd)/dot_general | solution.py:32
  627.3 14.6 %convert_reduce_fusion.3 = f32[4,64,4,4]{1,3,2,0:T(4,128)S(1)} fusion(f32[4,64,4,4]{1,3,2,0:T(4,128)S(1)} %get-tuple-element.193, f32[4,4,2048,64,4]{2,3,4,1,0:T(8,128)} %get-tuple-element.194, pred[4,2048]{1,0:T(4,128)(4,1)S(1)} %broadcast_compare_fusion.2), kind=kLoop, calls=%fused_computation.11.clone.1 | loop fusion | flops 50327552 | bytes 33595392 | tf_op jit(solution)/shard_map/while/body/eval_jaxpr/vmap()/reduce_sum | solution.py:31
  642.0 17.5 %fusion.35 = (bf16[8,768,1024]{2,1,0:T(8,128)(2,1)}, bf16[8,768,1024]{2,1,0:T(8,128)(2,1)}) fusion(bf16[8,2048,1024]{2,1,0:T(8,128)(2,1)} %get-tuple-element.223), kind=kLoop, calls=%fused_computation.61.clone.1 | loop fusion | bytes 50331648 | tf_op jit(solution)/shard_map/while/body/eval_jaxpr/jit(_take)/gather | solution.py:79
  659.5 8.2 gather_fusion.2
  667.7 8.2 gather_fusion.3
  675.9 7.6 mini-gather-slice.13
  683.5 6.2 gather_fusion.1
  689.7 13.6 %pad_maximum_fusion.2 = bf16[4,2048,1024]{2,1,0:T(8,128)(2,1)} fusion(bf16[4,512,1024]{2,1,0:T(8,128)(2,1)} %gather_fusion.1, bf16[4,768,1024]{2,1,0:T(8,128)(2,1)} %gather_fusion.2, bf16[4,768,1024]{2,1,0:T(8,128)(2,1)} %gather_fusion.3), kind=kLoop, calls=%fused_computation.12.clone.1 | loop fusion | flops 50331648 | bytes 33554432 | tf_op jit(solution)/shard_map/while
  703.3 21.9 %copy.54 = bf16[4,2048,1024]{1,2,0:T(8,128)(2,1)} copy(bf16[4,2048,1024]{2,1,0:T(8,128)(2,1)} %pad_maximum_fusion.2) | data formatting | bytes 33554432 | tf_op jit(solution)/shard_map/while
  725.1 21.7 %copy.55 = bf16[4,2048,4,2,128]{4,1,2,0,3:T(8,128)(2,1)} copy(bf16[4,2048,4,2,128]{1,4,3,2,0:T(8,128)(2,1)} %bitcast.129) | data formatting | bytes 33554432 | tf_op jit(solution)/shard_map/while/body/eval_jaxpr/jit(_take)/gather | solution.py:79
  746.8 14.3 %broadcast_select_fusion.2 = bf16[4,2048,4,2,128]{4,1,2,0,3:T(8,128)(2,1)} fusion(bf16[4,2048,4,2,128]{4,1,2,0,3:T(8,128)(2,1)} %copy.55, pred[4]{0:T(512)(128)(4,1)S(1)} %compare_and_fusion.2), kind=kLoop, calls=%fused_computation.13.clone.1 | loop fusion | flops 8388608 | bytes 33554436 | tf_op jit(solution)/shard_map/while/body/eval_jaxpr/jit(_take)/select_n | solution.py:79
  761.1 0.6 gather_fusion
  761.8 15.4 %fusion.36 = (f32[4,64,4,4]{1,3,2,0:T(4,128)S(1)}, f32[4,4,2048,64,4]{2,3,4,1,0:T(8,128)}) fusion(pred[4,2048]{1,0:T(4,128)(4,1)S(1)} %broadcast_compare_fusion.2, bf16[4,2048,4,2,128]{4,1,2,0,3:T(8,128)(2,1)} %broadcast_select_fusion.2, bf16[2,4,64,4,4,128]{5,2,1,0,4,3:T(8,128)(2,1)S(1)} %copy-done.6, s32[]{:T(128)} %get-tuple-element.207), kind=kOutput, calls=%fused_computation.7.clone.1 | convolution fusion | flops 2172645376 | bytes 43016704 | tf_op jit(solution)/shard_map/while/body/eval_jaxpr/vmap(rgqd,kgd->rgqk)/dot_general | solution.py:25
  777.3 16.9 %bitcast_dynamic-update-slice_fusion.6 = f32[2,4,64,4,4,128]{5,2,4,3,1,0:T(8,128)} fusion(f32[2,4,64,4,4,128]{5,2,4,3,1,0:T(8,128)} %get-tuple-element.210, s32[]{:T(128)} %get-tuple-element.207, bf16[4,2048,4,2,128]{4,1,2,0,3:T(8,128)(2,1)} %broadcast_select_fusion.2, f32[4,4,2048,64,4]{2,3,4,1,0:T(8,128)} %get-tuple-element.194, ...), kind=kOutput, calls=%fused_computation.18.clone.1 | convolution fusion | flops 2181038080 | bytes 44065280 | tf_op jit(solution)/shard_map/while/body/eval_jaxpr/vmap(rgqk,kgd->rgqd)/dot_general | solution.py:32
  794.2 14.6 %convert_reduce_fusion.3 = f32[4,64,4,4]{1,3,2,0:T(4,128)S(1)} fusion(f32[4,64,4,4]{1,3,2,0:T(4,128)S(1)} %get-tuple-element.193, f32[4,4,2048,64,4]{2,3,4,1,0:T(8,128)} %get-tuple-element.194, pred[4,2048]{1,0:T(4,128)(4,1)S(1)} %broadcast_compare_fusion.2), kind=kLoop, calls=%fused_computation.11.clone.1 | loop fusion | flops 50327552 | bytes 33595392 | tf_op jit(solution)/shard_map/while/body/eval_jaxpr/vmap()/reduce_sum | solution.py:31
  808.9 0.7 reshape.193
  809.6 3.3 all-to-all-start
  813.1 6.5 all-to-all-done
  819.6 9.0 all_to_all.15
  828.7 4.8 all-to-all-start.1
  833.5 0.6 dynamic_slice.17
  834.1 0.6 iota_compare_fusion.1
  835.0 1.3 select_reduce_fusion
  836.5 0.5 broadcast.107
  837.0 0.7 reduce.4
  837.9 0.7 reduce.5
  838.8 85.1 %all-to-all-done.1 = f32[8,64,4,4,128]{4,1,3,2,0:T(8,128)} async-done(((f32[8,64,4,4,128]{4,1,3,2,0:T(8,128)}), f32[8,64,4,4,128]{4,1,3,2,0:T(8,128)}, u32[]{:S(2)}, u32[]{:S(2)}) %all-to-all-start.1) | async-done | bytes 4194336 | tf_op jit(solution)/shard_map/all_to_all | solution.py:94
  923.8 2.9 multiply_reduce_fusion
  927.4 0.9 convert_element_type.51
  (50 shorter events, 2.1 us)
Async XLA Ops:
  6.5 418.9 %copy-start = (s32[2,8,1]{1,2,0:T(1,128)S(1)}, s32[2,8,1]{1,2,0:T(1,128)}, u32[]{:S(2)}) copy-start(s32[2,8,1]{1,2,0:T(1,128)} %param.17) | copy-start | bytes 196
  6.5 406.9 %all-gather.6.cloned.1.call-start = ((), (), s32[]{:S(2)}) async-start(), calls=%async_computation.4 | async-start | bytes 23592960 | tf_op jit(solution)/shard_map/all_gather | solution.py:58
  7.3 467.5 %copy-start.2 = (s32[8]{0:T(128)S(1)}, s32[8]{0:T(128)}, u32[]{:S(2)}) copy-start(s32[8]{0:T(128)} %param.15) | copy-start | bytes 100
  7.3 467.5 %all-gather.4.cloned.1.call-start = ((), (), s32[]{:S(2)}) async-start(), calls=%async_computation.3 | async-start | bytes 2359296 | tf_op jit(solution)/shard_map/all_gather | solution.py:71
  7.3 4.3 collective-permute-start
  424.5 50.2 %copy-start.3 = (bf16[64,4,4,128]{3,2,1,0:T(4,128)(2,1)}, bf16[64,4,4,128]{3,2,1,0:T(4,128)(2,1)S(1)}, u32[]{:S(2)}) copy-start(bf16[64,4,4,128]{3,2,1,0:T(4,128)(2,1)S(1)} %reshape.135) | copy-start | bytes 786436
  474.8 358.7 %copy-start.4 = (bf16[1,64,1024]{2,1,0:T(8,128)(2,1)S(1)}, bf16[1,64,1024]{2,1,0:T(8,128)(2,1)}, u32[]{:S(2)}) copy-start(bf16[1,64,1024]{2,1,0:T(8,128)(2,1)} %param.13) | copy-start | bytes 393220
  474.8 358.8 %copy-start.5 = (s32[2,8]{1,0:T(2,128)S(1)}, s32[2,8]{1,0:T(2,128)}, u32[]{:S(2)}) copy-start(s32[2,8]{1,0:T(2,128)} %param.16) | copy-start | bytes 196
  579.9 15.0 %copy-start.6 = (bf16[2,4,64,4,4,128]{5,2,1,0,4,3:T(8,128)(2,1)S(1)}, bf16[2,4,64,4,4,128]{5,2,1,0,4,3:T(8,128)(2,1)}, u32[]{:S(2)}) copy-start(bf16[2,4,64,4,4,128]{5,2,1,0,4,3:T(8,128)(2,1)} %get-tuple-element.224) | copy-start | bytes 6291460 | tf_op jit(solution)/shard_map/while
  746.8 15.0 %copy-start.6 = (bf16[2,4,64,4,4,128]{5,2,1,0,4,3:T(8,128)(2,1)S(1)}, bf16[2,4,64,4,4,128]{5,2,1,0,4,3:T(8,128)(2,1)}, u32[]{:S(2)}) copy-start(bf16[2,4,64,4,4,128]{5,2,1,0,4,3:T(8,128)(2,1)} %get-tuple-element.224) | copy-start | bytes 6291460 | tf_op jit(solution)/shard_map/while
  808.9 119.4 %copy-start.1 = (s32[2,8,1]{1,2,0:T(1,128)S(1)}, s32[2,8,1]{1,2,0:T(1,128)}, u32[]{:S(2)}) copy-start(s32[2,8,1]{1,2,0:T(1,128)} %param.17) | copy-start | bytes 196
  809.6 10.0 %all-to-all-start = ((f32[8,1,1024]{2,1,0:T(1,128)}), f32[8,1,1024]{2,1,0:T(1,128)S(1)}, u32[]{:S(2)}, u32[]{:S(2)}) async-start(f32[8,1,1024]{2,1,0:T(1,128)} %reshape.193), calls=%async_computation | async-start | bytes 65536 | tf_op jit(solution)/shard_map/all_to_all | solution.py:92
  828.7 95.2 %all-to-all-start.1 = ((f32[8,64,4,4,128]{4,1,3,2,0:T(8,128)}), f32[8,64,4,4,128]{4,1,3,2,0:T(8,128)}, u32[]{:S(2)}, u32[]{:S(2)}) async-start(f32[8,64,4,4,128]{4,1,3,2,0:T(8,128)} %bitcast.131), calls=%async_computation.1 | async-start | bytes 8388608 | tf_op jit(solution)/shard_map/all_to_all | solution.py:94
Sparse Core Ops, SparseCore 0:
  8.9 404.4 all-gather.5
  425.5 49.2 all-gather.3
where the time goes:
time: 939 us; the launch traced here: 935 us
  waiting for transfers between devices  545 us (58%)
  local copies, waits for them, and re-layouts  188 us (20%)
  other arithmetic  90.4 us (10%)
  matrix products  77.5 us (8%)
  between operations  13.6 us (1%)
  starting transfers between devices  10.5 us (1%)
    all_gather x1, waiting for transfers between devices, shards(): lax.all_gather(query_weight[0], 'seq', axis=0, tiled=True)  402 us
    gather x12, local copies, waits for them, and re-layouts, tile_parts(): jnp.take(prompt_tiles, group_prompts, axis=0)  139 us
    all_to_all x1, waiting for transfers between devices, shards(): lax.all_to_all(sums, 'seq', split_axis=0, concat_axis=0, tiled=True)  85.1 us
    all_gather x1, waiting for transfers between devices, shards(): gathered = lax.all_gather(queries, 'seq', axis=0, tiled=True)  49.2 us
    while x6, local copies, waits for them, and re-layouts  43.7 us
    dot_general x3, matrix products, partial_attend(): jnp.einsum('rgqk,kgd->rgqd', weights, value_rows, preferred_element_type=...  34.4 us
    dot_general x3, matrix products, partial_attend(): jnp.einsum('rgqd,kgd->rgqk', queries, key_rows, preferred_element_type=jn...  32.2 us
    reduce_sum x3, other arithmetic, partial_attend(): row_total = jnp.sum(weights.astype(jnp.float32), axis=-1)  29.4 us
  transfers between devices with their start and end apart: 5, of which 5 were waited for; matrix products, arithmetic and copies ran while one was open for 1% of the time, Pallas kernels for 0%

commit v1 on v0

v1 whole, which is shorter than its diff:
```python
import functools
import math

import jax
import jax.numpy as jnp
from jax import lax
from jax.experimental import pallas as pl
from jax.experimental.pallas import tpu as pltpu
from jax.sharding import PartitionSpec as P

HD = 128
GR = 4
NEG = -1e30
LOG2E = 1.4426950408889634
CHUNK = 512
EXTRA = 128
VMEM = 56 * 1024 * 1024


def from_behind(value, axis, steps):
    count = lax.axis_size(axis)
    first, last = (max(0, -steps), min(count, count - steps))
    return lax.ppermute(value, axis, [(source, source + steps) for source in range(first, last)])


def dot_nt(a, b):
    return lax.dot_general(a, b, (((1,), (1,)), ((), ())), preferred_element_type=jnp.float32)


def project_kernel(nb, bl, packed, meta, x_ref, w_ref, out_ref, xp_ref):
    @pl.when(pl.program_id(0) == 0)
    def _():
        total = jnp.zeros(xp_ref.shape, jnp.float32)
        offset = jnp.int32(0)
        place = lax.broadcasted_iota(jnp.int32, (packed, bl), 0)
        order = lax.broadcasted_iota(jnp.int32, (packed, bl), 1)
        parts = []
        for b in range(nb):
            length = meta[b]
            pick = (place == order + offset) & (order < length)
            parts.append(jnp.where(pick, 1.0, 0.0).astype(jnp.bfloat16))
            offset = offset + length
        pick = jnp.concatenate(parts, axis=1)
        total = jnp.dot(pick, x_ref[...], preferred_element_type=jnp.float32)
        xp_ref[...] = total.astype(jnp.bfloat16)

    out_ref[...] = jnp.dot(xp_ref[...], w_ref[...], preferred_element_type=jnp.float32)


def project(lengths, x, w, nb, bl, packed):
    k, cols = w.shape
    tile = min(512, cols)
    return pl.pallas_call(
        functools.partial(project_kernel, nb, bl, packed),
        grid_spec=pltpu.PrefetchScalarGridSpec(
            num_scalar_prefetch=1,
            grid=(cols // tile,),
            in_specs=[
                pl.BlockSpec((nb * bl, k), lambda j, m: (0, 0)),
                pl.BlockSpec((k, tile), lambda j, m: (0, j)),
            ],
            out_specs=pl.BlockSpec((packed, tile), lambda j, m: (0, j)),
            scratch_shapes=[pltpu.VMEM((packed, k), jnp.bfloat16)],
        ),
        out_shape=jax.ShapeDtypeStruct((packed, cols), jnp.float32),
        compiler_params=pltpu.CompilerParams(vmem_limit_bytes=VMEM),
        cost_estimate=pl.CostEstimate(
            flops=2 * packed * k * cols, bytes_accessed=2 * k * cols + 4 * packed * cols,
            transcendentals=0,
        ),
        name="project",
    )(lengths, x, w)


def attend_kernel(nb, bl, packed, tile_len, heads, meta, q_ref, kv_ref, own_ref, o_ref,
                  q32_ref, s_ref, acc_ref, m_ref):
    b = pl.program_id(0)
    valid = meta[nb + b]
    offset = meta[2 * nb + b]
    mine = meta[3 * nb] == b
    m_rows = GR * bl
    c2 = LOG2E / math.sqrt(HD)
    chunk = min(CHUNK, tile_len)
    ones_of = lambda rows: jnp.ones((rows, HD), jnp.bfloat16)

    @pl.when(b == 0)
    def _():
        q32_ref[:packed, :] = q_ref[...].astype(jnp.float32)
        q32_ref[packed:, :] = jnp.zeros((bl + 8, q32_ref.shape[1]), jnp.float32)

    lane = lax.broadcasted_iota(jnp.int32, (bl, EXTRA), 1)
    lse_tile = jnp.zeros((bl, EXTRA), jnp.float32)
    rest = offset % 8
    window = q32_ref[pl.ds(pl.multiple_of(offset - rest, 8), bl + 8), :]
    window = pltpu.roll(window, jnp.where(rest == 0, 0, bl + 8 - rest), 0)
    queries = window[:bl].astype(jnp.bfloat16)
    for g in range(heads):
        q = jnp.concatenate(
            [queries[:, (g * GR + r) * HD:(g * GR + r + 1) * HD] for r in range(GR)], axis=0
        )
        keys = pl.ds(g * 2 * HD, HD)
        vals = pl.ds(g * 2 * HD + HD, HD)

        @pl.when(valid == tile_len)
        def _():
            s = dot_nt(q, kv_ref[0, 0, :, keys]) * c2
            m = jnp.max(s, axis=1, keepdims=True)
            p = jnp.exp2(s - m).astype(jnp.bfloat16)
            v = jnp.concatenate([kv_ref[0, 0, :, vals], ones_of(tile_len)], axis=1)
            acc_ref[...] = jnp.dot(p, v, preferred_element_type=jnp.float32)
            m_ref[...] = jnp.broadcast_to(m, m_ref.shape)

        @pl.when(valid < tile_len)
        def _():
            count = (valid + chunk - 1) // chunk
            acc_ref[...] = jnp.zeros_like(acc_ref)
            m_ref[...] = jnp.full_like(m_ref, NEG)

            def scores(c, carry):
                at = pl.multiple_of(c * chunk, chunk)
                s = dot_nt(q, kv_ref[0, 0, pl.ds(at, chunk), keys]) * c2
                here = lax.broadcasted_iota(jnp.int32, s.shape, 1) + at
                s = jnp.where(here < valid, s, NEG)
                s_ref[c] = s
                m_ref[...] = jnp.maximum(m_ref[...], jnp.max(s, axis=1, keepdims=True))
                return carry

            lax.fori_loop(0, count, scores, 0)

            def sums(c, carry):
                at = pl.multiple_of(c * chunk, chunk)
                s = s_ref[c]
                here = lax.broadcasted_iota(jnp.int32, s.shape, 1) + at
                p = jnp.where(here < valid, jnp.exp2(s - m_ref[:, :1]), 0.0).astype(jnp.bfloat16)
                v = jnp.concatenate([kv_ref[0, 0, pl.ds(at, chunk), vals], ones_of(chunk)], axis=1)
                acc_ref[...] += jnp.dot(p, v, preferred_element_type=jnp.float32)
                return carry

            lax.fori_loop(0, count, sums, 0)

        @pl.when(mine)
        def _():
            s = dot_nt(q, own_ref[:, keys]) * c2
            row = lax.broadcasted_iota(jnp.int32, s.shape, 0) % bl
            col = lax.broadcasted_iota(jnp.int32, s.shape, 1)
            seen = col <= row
            s = jnp.where(seen, s, NEG)
            before = m_ref[:, :1]
            m = jnp.maximum(before, jnp.max(s, axis=1, keepdims=True))
            p = jnp.where(seen, jnp.exp2(s - m), 0.0).astype(jnp.bfloat16)
            v = jnp.concatenate([own_ref[:, vals], ones_of(bl)], axis=1)
            acc_ref[...] = acc_ref[...] * jnp.exp2(before - m) + jnp.dot(
                p, v, preferred_element_type=jnp.float32
            )
            m_ref[...] = jnp.broadcast_to(m, m_ref.shape)

        total = acc_ref[:, HD:]
        some = total > 0.0
        safe = jnp.where(some, total, 1.0)
        out = (acc_ref[:, :HD] / safe).astype(jnp.bfloat16)
        lse = jnp.where(some, m_ref[...] + jnp.log2(safe), NEG)
        for r in range(GR):
            h = g * GR + r
            o_ref[0, :, h * HD:(h + 1) * HD] = out[r * bl:(r + 1) * bl]
            lse_tile = jnp.where(lane == h, lse[r * bl:(r + 1) * bl], lse_tile)
    high = lse_tile.astype(jnp.bfloat16)
    rest = lse_tile - high.astype(jnp.float32)
    mid = rest.astype(jnp.bfloat16)
    low = (rest - mid.astype(jnp.float32)).astype(jnp.bfloat16)
    base = heads * GR * HD
    o_ref[0, :, base:base + EXTRA] = high
    o_ref[0, :, base + EXTRA:base + 2 * EXTRA] = mid
    o_ref[0, :, base + 2 * EXTRA:base + 3 * EXTRA] = low


def attend(meta, q, cache, own, nb, bl, first, heads):
    packed, cols = q.shape
    tile_len = cache.shape[2]
    chunk = min(CHUNK, tile_len)
    width = heads * GR * HD + 3 * EXTRA
    return pl.pallas_call(
        functools.partial(attend_kernel, nb, bl, packed, tile_len, heads),
        grid_spec=pltpu.PrefetchScalarGridSpec(
            num_scalar_prefetch=1,
            grid=(nb,),
            in_specs=[
                pl.BlockSpec((packed, cols), lambda b, m: (0, 0)),
                pl.BlockSpec(
                    (1, 1, tile_len, heads * 2 * HD), lambda b, m: (0, m[b], 0, first // heads)
                ),
                pl.BlockSpec((bl, heads * 2 * HD), lambda b, m: (0, first // heads)),
            ],
            out_specs=pl.BlockSpec((1, bl, width), lambda b, m: (b, 0, 0)),
            scratch_shapes=[
                pltpu.VMEM((packed + bl + 8, cols), jnp.float32),
                pltpu.VMEM((tile_len // chunk, GR * bl, chunk), jnp.float32),
                pltpu.VMEM((GR * bl, 2 * HD), jnp.float32),
                pltpu.VMEM((GR * bl, HD), jnp.float32),
            ],
        ),
        out_shape=jax.ShapeDtypeStruct((nb, bl, width), jnp.bfloat16),
        compiler_params=pltpu.CompilerParams(vmem_limit_bytes=VMEM),
        cost_estimate=pl.CostEstimate(
            flops=4 * nb * bl * cols * tile_len,
            bytes_accessed=2 * nb * tile_len * heads * 2 * HD,
            transcendentals=nb * bl * heads * GR * tile_len,
        ),
        name="attend",
    )(meta, q, cache, own)


def shards(
    hidden_rows,
    carried,
    query_weight,
    response_cache,
    prompt_cache,
    prompt_lengths,
    response_lengths,
    block_prompts,
):
    section = lax.axis_index("sec")
    shard = lax.axis_index("seq")
    nb = lax.axis_size("seq")
    bl = hidden_rows.shape[1]
    local_kv = response_cache.shape[2] // (2 * HD)
    packed = nb * bl * 5 // 8
    share = packed // nb
    tile_len = prompt_cache.shape[2]
    cols = query_weight.shape[2]
    lengths = lax.dynamic_index_in_dim(response_lengths, section, 0, keepdims=False)
    prompts = lax.dynamic_index_in_dim(block_prompts, section, 0, keepdims=False)[:, 0]
    valid = jnp.clip(prompt_lengths[prompts] - shard * tile_len, 0, tile_len)
    offsets = jnp.cumsum(lengths) - lengths
    meta = jnp.concatenate([prompts, valid, offsets, shard[None]]).astype(jnp.int32)

    handed = from_behind(carried, "sec", 1)
    inputs = (hidden_rows[0].astype(jnp.float32) + handed[0].astype(jnp.float32)).astype(
        jnp.bfloat16
    )
    depth = query_weight.shape[1]
    slices = inputs.reshape(bl, nb, depth).transpose(1, 0, 2)
    x = lax.all_to_all(slices, "seq", split_axis=0, concat_axis=0, tiled=True)
    part = project(lengths, x.reshape(nb * bl, depth), query_weight[0], nb, bl, packed)
    part = (part * 0.125).astype(jnp.float16).reshape(nb, share, cols)
    part = lax.all_to_all(part, "seq", split_axis=0, concat_axis=0, tiled=True)
    mine = (jnp.sum(part.astype(jnp.float32), axis=0) * 8.0).astype(jnp.bfloat16)
    queries = lax.all_gather(mine, "seq", axis=0, tiled=True)
    out = attend(meta, queries, prompt_cache, response_cache[0], nb, bl, 0, local_kv)
    back = lax.all_to_all(out, "seq", split_axis=0, concat_axis=0, tiled=True)
    heads = local_kv * GR
    base = heads * HD
    terms = back[:, :, base:].astype(jnp.float32).reshape(nb, bl, 3, EXTRA)[:, :, :, :heads]
    lse = terms[:, :, 0] + terms[:, :, 1] + terms[:, :, 2]
    weight = jnp.exp2(lse - jnp.max(lse, axis=0, keepdims=True))
    weight = weight / jnp.sum(weight, axis=0, keepdims=True)
    values = back[:, :, :base].reshape(nb, bl, heads, HD).astype(jnp.float32)
    output = jnp.sum(values * weight[..., None], axis=0)
    order = jnp.arange(bl, dtype=jnp.int32)
    output = jnp.where((order < lengths[shard])[:, None, None], output, 0.0)
    return output.reshape(1, bl, base).astype(jnp.bfloat16)


def solution(mesh):
    placed = (
        P("sec", "seq", None),
        P("sec", "seq", None),
        P("sec", "seq", "tp"),
        P("sec", "seq", "tp"),
        P("sec", None, "seq", "tp"),
        P(),
        P(),
        P(),
    )
    return jax.shard_map(
        shards, mesh=mesh, in_specs=placed, out_specs=P("sec", "seq", "tp"), check_vma=False
    )
```

time: 939 us -> 262 us (0.28)
  waiting for transfers between devices: 545 us -> 114 us
  local copies, waits for them, and re-layouts: 188 us -> 12 us
  other arithmetic: 90.4 us -> 11.6 us
  matrix products: 77.5 us -> 0 us
  Pallas kernels: 0 us -> 60.8 us
  blocking collectives: 9.05 us -> 35 us
    all_gather x2 -> x1, waiting for transfers between devices: 451 us -> 40 us  [shards(): queries = lax.all_gather(mine, 'seq', axis=0, tiled=True)]
    gather x14 -> x1, local copies, waits for them, and re-layouts: 140 us -> 0.64 us  [shards(): valid = jnp.clip(prompt_lengths[prompts] - shard * tile_len, 0, tile_len)]
    dot_general x7 -> x0, matrix products: 77.5 us -> none  [the longest x3 34.4 us: partial_attend(): jnp.einsum('rgqk,kgd->rgqd', weights, value_rows, preferred_element_type=...]
    pallas_call x0 -> x2, Pallas kernels: none -> 60.8 us  [the longest x1 54.6 us: attend(): pl.pallas_call(functools.partial(attend_kernel, nb, bl, packed, tile_len,...]
    while x6 -> x0, local copies, waits for them, and re-layouts: 43.7 us -> none
    reduce_sum x5 -> x3, other arithmetic: 32.3 us -> 3.22 us  [the longest x1 2.91 us: shards(): output = jnp.sum(values * weight[..., None], axis=0)]
    select_n x4 -> x1, other arithmetic: 28.6 us -> 0.01 us  [shards(): valid = jnp.clip(prompt_lengths[prompts] - shard * tile_len, 0, tile_len)]
    while x2 -> x0, other arithmetic: 27.2 us -> none
  transfers between devices with their start and end apart: 5 -> 4, of which waited for: 5 -> 4; matrix products, arithmetic and copies ran while one was open for 1% -> 1% of each run, Pallas kernels for 0% -> 0%
where the time goes in v1:
time: 262 us; the launch traced here: 260 us
  waiting for transfers between devices  114 us (44%)
  Pallas kernels  60.8 us (23%)
  blocking collectives  35 us (13%)
  between operations  13.6 us (5%)
  starting transfers between devices  13 us (5%)
  local copies, waits for them, and re-layouts  12 us (5%)
  other arithmetic  11.6 us (4%)
    all_to_all x1, waiting for transfers between devices, shards(): back = lax.all_to_all(out, 'seq', split_axis=0, concat_axis=0, tiled=True)  55.2 us
    pallas_call x1, Pallas kernels, attend(): pl.pallas_call(functools.partial(attend_kernel, nb, bl, packed, tile_len,...  54.6 us
    all_gather x1, waiting for transfers between devices, shards(): queries = lax.all_gather(mine, 'seq', axis=0, tiled=True)  40 us
    all_to_all x1, blocking collectives, shards(): part = lax.all_to_all(part, 'seq', split_axis=0, concat_axis=0, tiled=True)  35 us
    all_to_all x1, waiting for transfers between devices, shards(): x = lax.all_to_all(slices, 'seq', split_axis=0, concat_axis=0, tiled=True)  17 us
    mul x2, local copies, waits for them, and re-layouts, shards(): output = jnp.sum(values * weight[..., None], axis=0)  7.46 us
    all_to_all x1, starting transfers between devices, shards(): x = lax.all_to_all(slices, 'seq', split_axis=0, concat_axis=0, tiled=True)  6.65 us
    pallas_call x1, Pallas kernels, project(): pl.pallas_call(functools.partial(project_kernel, nb, bl, packed), grid_sp...  6.14 us
  transfers between devices with their start and end apart: 4, of which 4 were waited for; matrix products, arithmetic and copies ran while one was open for 1% of the time, Pallas kernels for 0%

profile of v1, /device:TPU:0, one launch (start us, length us, event | category | flops | bytes accessed | tf_op | source)
XLA Modules:
  0.0 260.0 jit_solution(3624381493174076867)
XLA Ops:
  6.5 0.0 copy-start
  6.5 0.0 copy-start.2
  6.5 2.5 collective-permute-start
  9.1 1.9 collective-permute-done
  10.9 1.3 add_convert_fusion
  12.2 0.1 copy.11
  12.3 0.9 copy.13
  13.2 6.6 %all-to-all-start = ((bf16[8,64,640]{2,1,0:T(8,128)(2,1)}), bf16[8,64,640]{2,1,0:T(8,128)(2,1)S(1)}, u32[]{:S(2)}, u32[]{:S(2)}) async-start(bf16[8,64,640]{2,1,0:T(8,128)(2,1)} %bitcast.31), calls=%async_computation | async-start | bytes 1310720 | tf_op jit(solution)/shard_map/all_to_all | solution.py:243
  19.9 0.0 all-gather.2.cloned.1.call-start
  19.9 0.0 copy-done.2
  19.9 0.2 reduce-window.9
  20.1 0.5 bitcast_subtract_fusion
  20.6 17.0 %all-to-all-done = bf16[8,64,640]{2,1,0:T(8,128)(2,1)S(1)} async-done(((bf16[8,64,640]{2,1,0:T(8,128)(2,1)}), bf16[8,64,640]{2,1,0:T(8,128)(2,1)S(1)}, u32[]{:S(2)}, u32[]{:S(2)}) %all-to-all-start) | async-done | bytes 655392 | tf_op jit(solution)/shard_map/all_to_all | solution.py:243
  37.7 0.0 copy-start.1
  37.7 0.8 copy-done.1
  38.5 6.1 %project.1 = f32[320,2048]{1,0:T(8,128)} custom-call(s32[8]{0:T(128)} %get-tuple-element.8.meta, bf16[512,640]{1,0:T(8,128)(2,1)} %bitcast.33, bf16[640,2048]{1,0:T(8,128)(2,1)} %bitcast.34), custom_call_target="tpu_custom_call" | custom-call | flops 838860800 | bytes 5242880 | tf_op jit(solution)/shard_map/project/pallas_call | solution.py:53
  44.7 2.0 multiply_convert_fusion
  46.7 0.0 copy-start.3
  46.7 35.0 %all_to_all.15 = f16[8,40,2048]{2,1,0:T(8,128)(2,1)S(1)} all-to-all(f16[8,40,2048]{2,1,0:T(8,128)(2,1)S(1)} %bitcast.32), channel_id=1, replica_groups=mesh['sec'=2,'seq'=8,'tp'=2] {'seq'}, dimensions={0} | all-to-all | bytes 2621440 | tf_op jit(solution)/shard_map/all_to_all | solution.py:246
  81.6 0.2 convert_reduce_fusion
  81.9 0.7 multiply_convert_fusion.1
  82.6 0.0 all-gather.2.cloned.1.call-update
  82.6 0.0 copy-done.3
  82.6 0.0 copy-done
  82.6 0.6 gather_fusion
  83.3 0.6 pad_add_fusion.meta
  83.9 40.0 %all-gather.2.cloned.1.call-done.q_ref = bf16[320,2048]{1,0:T(8,128)(2,1)} async-done(((bf16[40,2048]{1,0:T(8,128)(2,1)}), bf16[320,2048]{1,0:T(8,128)(2,1)}) %all-gather.2.cloned.1.call-update) | async-done | bytes 1310736 | tf_op jit(solution)/shard_map/all_gather | solution.py:248
  123.9 54.6 %attend.1 = bf16[8,64,2432]{2,1,0:T(8,128)(2,1)} custom-call(s32[25]{0:T(128)} %pad_add_fusion.meta, bf16[320,2048]{1,0:T(8,128)(2,1)} %all-gather.2.cloned.1.call-done.q_ref, bf16[1,8,2048,1024]{3,2,1,0:T(8,128)(2,1)} %kv_ref.1, bf16[64,1024]{1,0:T(8,128)(2,1)} %bitcast.39), custom_call_target="tpu_custom_call" | custom-call | flops 8589934592 | bytes 33554432 | tf_op jit(solution)/shard_map/attend/pallas_call | solution.py:181
  178.5 3.8 %all-to-all-start.2 = ((bf16[8,64,2432]{2,1,0:T(8,128)(2,1)}), bf16[8,64,2432]{2,1,0:T(8,128)(2,1)S(1)}, u32[]{:S(2)}, u32[]{:S(2)}) async-start(bf16[8,64,2432]{2,1,0:T(8,128)(2,1)} %attend.1), calls=%async_computation.2 | async-start | bytes 4980736 | tf_op jit(solution)/shard_map/all_to_all | solution.py:250
  182.3 0.6 dynamic_slice.11
  182.9 0.6 iota_compare_fusion
  183.6 55.2 %all-to-all-done.2 = bf16[8,64,2432]{2,1,0:T(8,128)(2,1)S(1)} async-done(((bf16[8,64,2432]{2,1,0:T(8,128)(2,1)}), bf16[8,64,2432]{2,1,0:T(8,128)(2,1)S(1)}, u32[]{:S(2)}, u32[]{:S(2)}) %all-to-all-start.2) | async-done | bytes 2490400 | tf_op jit(solution)/shard_map/all_to_all | solution.py:250
  238.7 0.9 slice_convert_fusion
  239.7 1.4 reshape.147
  241.1 0.7 fusion.7
  241.8 0.1 fusion.2
  241.9 0.1 fusion.1
  241.9 2.6 mul.31
  244.5 4.9 %mul.32 = f32[8,64,2048]{2,1,0:T(8,128)} reshape(f32[8,64,16,128]{3,2,1,0:T(8,128)} %mul.31) | data formatting | bytes 8388608 | tf_op jit(solution)/shard_map/mul | solution.py:258
  249.4 2.9 %multiply_reduce_fusion = bf16[64,2048]{1,0:T(8,128)(2,1)S(1)} fusion(f32[8,64,2048]{2,1,0:T(8,128)} %mul.32, bf16[8,64,2432]{2,1,0:T(8,128)(2,1)S(1)} %all-to-all-done.2), kind=kLoop, calls=%fused_computation.1 | loop fusion | flops 3014656 | bytes 6553600 | tf_op jit(solution)/shard_map/reduce_sum | solution.py:258
  252.3 0.8 fusion
  (5 shorter events, 0.0 us)
Async XLA Ops:
  6.5 76.1 %copy-start = (s32[8]{0:T(128)S(1)}, s32[8]{0:T(128)}, u32[]{:S(2)}) copy-start(s32[8]{0:T(128)} %param.13) | copy-start | bytes 100
  6.5 13.4 %copy-start.2 = (s32[2,8]{1,0:T(2,128)S(1)}, s32[2,8]{1,0:T(2,128)}, u32[]{:S(2)}) copy-start(s32[2,8]{1,0:T(2,128)} %param.14) | copy-start | bytes 196
  6.5 4.4 %collective-permute-start = (bf16[1,64,5120]{2,1,0:T(8,128)(2,1)}, bf16[1,64,5120]{2,1,0:T(8,128)(2,1)S(1)}, u32[]{:S(2)}, u32[]{:S(2)}) collective-permute-start(bf16[1,64,5120]{2,1,0:T(8,128)(2,1)} %param.9), channel_id=1, source_target_pairs={{0,16},{1,17},{2,18},{3,19},{4,20},{5,21},{6,22},{7,23},{8,24},{9,... | collective-permute-start | bytes 1966088 | tf_op jit(solution)/shard_map/ppermute | solution.py:23
  13.2 24.5 %all-to-all-start = ((bf16[8,64,640]{2,1,0:T(8,128)(2,1)}), bf16[8,64,640]{2,1,0:T(8,128)(2,1)S(1)}, u32[]{:S(2)}, u32[]{:S(2)}) async-start(bf16[8,64,640]{2,1,0:T(8,128)(2,1)} %bitcast.31), calls=%async_computation | async-start | bytes 1310720 | tf_op jit(solution)/shard_map/all_to_all | solution.py:243
  19.9 104.0 %all-gather.2.cloned.1.call-start = ((), (), s32[]{:S(2)}) async-start(), calls=%async_computation.3 | async-start | bytes 1474560 | tf_op jit(solution)/shard_map/all_gather | solution.py:248
  37.7 0.8 copy-start.1
  46.7 35.9 %copy-start.3 = (s32[2,8,1]{1,2,0:T(1,128)S(1)}, s32[2,8,1]{1,2,0:T(1,128)}, u32[]{:S(2)}) copy-start(s32[2,8,1]{1,2,0:T(1,128)} %param.15) | copy-start | bytes 196
  178.5 60.2 %all-to-all-start.2 = ((bf16[8,64,2432]{2,1,0:T(8,128)(2,1)}), bf16[8,64,2432]{2,1,0:T(8,128)(2,1)S(1)}, u32[]{:S(2)}, u32[]{:S(2)}) async-start(bf16[8,64,2432]{2,1,0:T(8,128)(2,1)} %attend.1), calls=%async_computation.2 | async-start | bytes 4980736 | tf_op jit(solution)/shard_map/all_to_all | solution.py:250
Sparse Core Ops, SparseCore 0:
  82.7 41.1 all-gather.1

commit v2 on v0

v2 whole, which is shorter than its diff:
```python
import functools
import math

import jax
import jax.numpy as jnp
from jax import lax
from jax.experimental import pallas as pl
from jax.experimental.pallas import tpu as pltpu
from jax.sharding import PartitionSpec as P

HD = 128
GR = 4
NEG = -1e30
LOG2E = 1.4426950408889634
CHUNK = 512
LONG = 1024
ROUND = 16
EXTRA = 128
SLOT = 32
BIG = 2.0 ** 100
MIB = 1024 * 1024


def dot_nt(a, b):
    return lax.dot_general(a, b, (((1,), (1,)), ((), ())), preferred_element_type=jnp.float32)


class Grid:
    def __init__(self, count):
        self.n = count
        self.xs = 1 << ((count.bit_length() - 1) // 2)
        self.zs = count // self.xs

    def owner(self, shard, kx, kz):
        z, x = shard // self.xs, shard % self.xs
        return (z ^ kz) * self.xs + (x ^ kx)

    def swap(self, value, kx, kz):
        pairs = [(s, self.owner(s, kx, kz)) for s in range(self.n)]
        return lax.ppermute(value, "seq", pairs)


def split_kernel(grid, depth, place, hidden_ref, handed_ref, *out_refs):
    for kx in range(grid.xs):
        for kz in range(grid.zs):
            at = pl.multiple_of(grid.owner(place[1], kx, kz) * depth, HD)
            total = hidden_ref[0, :, pl.ds(at, depth)].astype(jnp.float32) + handed_ref[
                0, :, pl.ds(at, depth)
            ].astype(jnp.float32)
            out_refs[kx * grid.zs + kz][...] = total.astype(jnp.bfloat16)


def split(grid, place, hidden, handed, depth):
    bl = hidden.shape[1]
    if depth % HD:
        total = (hidden[0].astype(jnp.float32) + handed[0].astype(jnp.float32)).astype(jnp.bfloat16)
        return [
            lax.dynamic_slice_in_dim(total, grid.owner(place[1], kx, kz) * depth, depth, 1)
            for kx in range(grid.xs) for kz in range(grid.zs)
        ]
    whole = pl.BlockSpec(hidden.shape, lambda i, *m: (0, 0, 0))
    return pl.pallas_call(
        functools.partial(split_kernel, grid, depth),
        grid_spec=pltpu.PrefetchScalarGridSpec(
            num_scalar_prefetch=1,
            grid=(1,),
            in_specs=[whole, whole],
            out_specs=[pl.BlockSpec((bl, depth), lambda i, *m: (0, 0))] * grid.n,
        ),
        out_shape=[jax.ShapeDtypeStruct((bl, depth), jnp.bfloat16)] * grid.n,
        compiler_params=pltpu.CompilerParams(vmem_limit_bytes=16 * MIB),
        name="split",
    )(place, hidden, handed)


def project_kernel(grid, bl, share, place, lengths, *refs):
    x_refs, (w_ref, out_ref, xp_ref, starts) = refs[:grid.n], refs[grid.n:]

    @pl.when(pl.program_id(0) == 0)
    def _():
        section, shard = place[0], place[1]
        offset = jnp.int32(0)
        for b in range(grid.n):
            starts[b] = offset
            offset = offset + lengths[section, b]
        lane = lax.broadcasted_iota(jnp.int32, (8, grid.n * bl), 1)
        target = jnp.full(lane.shape, -1, jnp.int32)
        owners = [
            grid.owner(shard, kx, kz) for kx in range(grid.xs) for kz in range(grid.zs)
        ]
        for k, b in enumerate(owners):
            order = lane - k * bl
            used = (order >= 0) & (order < lengths[section, b])
            target = jnp.where(used, order + starts[b], target)
        row = lax.broadcasted_iota(jnp.int32, (share, grid.n * bl), 0)
        target = jnp.broadcast_to(target[:1], row.shape)
        picks = [jnp.where(row + b * share == target, 1.0, 0.0) for b in owners]
        pick = jnp.concatenate(picks, axis=0).astype(jnp.bfloat16)
        x = jnp.concatenate([ref[...] for ref in x_refs], axis=0)
        chosen = jnp.dot(pick, x, preferred_element_type=jnp.float32)
        xp_ref[...] = chosen.astype(jnp.bfloat16)

    result = jnp.dot(xp_ref[...], w_ref[...], preferred_element_type=jnp.float32)
    out_ref[...] = result.reshape(out_ref.shape)


def project(grid, place, lengths, xs, w, bl, share, chunks):
    k, cols = w.shape
    rows = grid.n * share
    tile = cols // chunks
    shape = (chunks, grid.xs, grid.zs * share, tile)
    return pl.pallas_call(
        functools.partial(project_kernel, grid, bl, share),
        grid_spec=pltpu.PrefetchScalarGridSpec(
            num_scalar_prefetch=2,
            grid=(chunks,),
            in_specs=[pl.BlockSpec((bl, k), lambda j, *m: (0, 0))] * grid.n
            + [pl.BlockSpec((k, tile), lambda j, *m: (0, j))],
            out_specs=pl.BlockSpec((1,) + shape[1:], lambda j, *m: (j, 0, 0, 0)),
            scratch_shapes=[
                pltpu.VMEM((rows, k), jnp.bfloat16), pltpu.SMEM((grid.n,), jnp.int32)
            ],
        ),
        out_shape=jax.ShapeDtypeStruct(shape, jnp.float32),
        compiler_params=pltpu.CompilerParams(vmem_limit_bytes=32 * MIB),
        cost_estimate=pl.CostEstimate(
            flops=2 * rows * k * cols, bytes_accessed=2 * k * cols + 4 * rows * cols,
            transcendentals=0,
        ),
        name="project",
    )(place, lengths, *xs, w)


def encode(lse):
    lane = lax.broadcasted_iota(jnp.int32, lse.shape, 1)
    high = lse.astype(jnp.bfloat16).astype(jnp.float32)
    rest = lse - high
    mid = rest.astype(jnp.bfloat16).astype(jnp.float32)
    low = rest - mid
    return jnp.where(lane < SLOT, high, jnp.where(lane < 2 * SLOT, mid, low)).astype(jnp.bfloat16)


def decode(tile):
    terms = tile.astype(jnp.float32)
    return terms + pltpu.roll(terms, EXTRA - SLOT, 1) + pltpu.roll(terms, EXTRA - 2 * SLOT, 1)


def merge(values, lses, heads):
    bl = lses[0].shape[0]
    lane = lax.broadcasted_iota(jnp.int32, lses[0].shape, 1)
    peak = functools.reduce(jnp.maximum, lses)
    weights = [jnp.exp2(lse - peak) for lse in lses]
    total = functools.reduce(jnp.add, weights)
    weights = [weight / total for weight in weights]
    merged = peak + jnp.log2(total)
    out = []
    spread = jnp.zeros((bl, EXTRA), jnp.float32)
    for h in range(heads):
        terms = [
            jnp.broadcast_to(weight[:, h:h + 1], (bl, HD)) * value(h).astype(jnp.float32)
            for weight, value in zip(weights, values)
        ]
        out.append(functools.reduce(jnp.add, terms))
        spread = jnp.where(lane % SLOT == h, merged[:, h:h + 1], spread)
    return out, spread


def attend_kernel(grid, kx, bl, share, heads, tile_len, *refs):
    place, lengths, prompts, prompt_lengths = refs[:4]
    refs = refs[4:]
    near_ref, refs = refs[0], refs[1:]
    far_refs, refs = refs[:grid.xs - 1], refs[grid.xs - 1:]
    kv_refs, refs = refs[:heads], refs[heads:]
    own_ref, refs = refs[0], refs[1:]
    met = grid.xs - 1 if kx == 0 else 0
    met_refs, refs = refs[:met], refs[met:]
    outs = grid.zs if kx == 0 else 1
    out_refs, refs = refs[:outs], refs[outs:]
    q32_ref, acc_ref, m_ref = refs

    step = pl.program_id(0)
    section, shard = place[0], place[1]
    rows = grid.n * share
    block = grid.owner(shard, kx, step)
    offset = jnp.int32(0)
    for b in range(grid.n):
        offset = offset + jnp.where(b < block, lengths[section, b], 0)
    valid = jnp.clip(
        prompt_lengths[prompts[section, block]] - shard * tile_len, 0, tile_len
    )
    c2 = LOG2E / math.sqrt(HD)
    chunk = min(CHUNK, tile_len)
    width = heads * GR * HD

    @pl.when(step == 0)
    def _():
        for fx in range(grid.xs):
            for fz in range(grid.zs):
                source = near_ref if fx == 0 else far_refs[fx - 1]
                at = pl.multiple_of(grid.owner(shard, fx, fz) * share, 8)
                q32_ref[pl.ds(at, share), :] = source[fz].astype(jnp.float32)
        q32_ref[rows:, :] = jnp.zeros((bl + 8, width), jnp.float32)

    rest = offset % 8
    window = q32_ref[pl.ds(pl.multiple_of(offset - rest, 8), bl + 8), :]
    window = pltpu.roll(window, jnp.where(rest == 0, 0, bl + 8 - rest), 0)
    queries = window[:bl].astype(jnp.bfloat16)

    def group(g, used):
        return jnp.concatenate(
            [queries[:used, (g * GR + r) * HD:(g * GR + r + 1) * HD] for r in range(GR)], axis=0
        )

    def with_ones(v):
        return jnp.concatenate([v, jnp.ones(v.shape, jnp.bfloat16)], axis=1)

    def sums(p, v):
        return jnp.dot(p, with_ones(v), preferred_element_type=jnp.float32)

    def keys(g, at, size):
        return kv_refs[g][0, 0, pl.ds(at, size), :HD]

    def vals(g, at, size):
        return kv_refs[g][0, 0, pl.ds(at, size), HD:]

    def put(g, used, acc, m):
        m = jnp.broadcast_to(m, (GR * used, HD))
        for r in range(GR):
            acc_ref[g, r * bl:r * bl + used] = acc[r * used:(r + 1) * used]
            m_ref[g, r * bl:r * bl + used] = m[r * used:(r + 1) * used]

    def update(g, s, seen, v):
        s = jnp.where(seen, s, NEG)
        before = m_ref[g][:, :1]
        m = jnp.maximum(before, jnp.max(s, axis=1, keepdims=True))
        p = jnp.where(seen, jnp.exp2((s - m) * c2), 0.0).astype(jnp.bfloat16)
        acc_ref[g] = acc_ref[g] * jnp.exp2((before - m) * c2) + sums(p, v)
        m_ref[g] = jnp.broadcast_to(m, m_ref.shape[1:])

    def exact():
        acc_ref[...] = jnp.zeros_like(acc_ref)
        m_ref[...] = jnp.full_like(m_ref, NEG)

        def one(c, carry):
            at = pl.multiple_of(c * chunk, chunk)
            for g in range(heads):
                s = dot_nt(group(g, bl), keys(g, at, chunk))
                here = lax.broadcasted_iota(jnp.int32, s.shape, 1) + at
                update(g, s, here < valid, vals(g, at, chunk))
            return carry

        lax.fori_loop(0, (valid + chunk - 1) // chunk, one, 0)

    length = lengths[section, block]
    acc_ref[...] = jnp.zeros_like(acc_ref)
    m_ref[...] = jnp.full_like(m_ref, NEG)

    long = min(LONG, tile_len)
    for used in range(ROUND, bl + 1, ROUND):
        @pl.when((valid == tile_len) & (length <= used) & (length > used - ROUND))
        def _(used=used):
            items = [(g, c) for g in range(heads) for c in range(tile_len // long)]
            q = [group(g, used) for g in range(heads)]
            peaks = [None] * heads
            accs = [None] * heads
            ahead = dot_nt(q[0], keys(0, 0, long))
            for i, (g, c) in enumerate(items):
                s = ahead
                if i + 1 < len(items):
                    ng, nc = items[i + 1]
                    ahead = dot_nt(q[ng], keys(ng, nc * long, long))
                if c == 0:
                    peaks[g] = jnp.max(s, axis=1, keepdims=True)
                p = jnp.exp2((s - peaks[g]) * c2).astype(jnp.bfloat16)
                part = sums(p, vals(g, c * long, long))
                accs[g] = part if c == 0 else accs[g] + part
            for g in range(heads):
                put(g, used, accs[g], peaks[g])

    @pl.when((valid < tile_len) & (valid > 0))
    def _():
        def scores(g, at):
            s = dot_nt(group(g, bl), keys(g, at, chunk))
            here = lax.broadcasted_iota(jnp.int32, s.shape, 1) + at
            return jnp.where(here < valid, s, NEG)

        for g in range(heads):
            s = scores(g, 0)
            m = jnp.max(s, axis=1, keepdims=True)
            p = jnp.exp2((s - m) * c2).astype(jnp.bfloat16)
            put(g, bl, sums(p, vals(g, 0, chunk)), m)

        def one(c, carry):
            at = pl.multiple_of(c * chunk, chunk)
            for g in range(heads):
                p = jnp.exp2((scores(g, at) - m_ref[g][:, :1]) * c2).astype(jnp.bfloat16)
                acc_ref[g] += sums(p, vals(g, at, chunk))
            return carry

        lax.fori_loop(1, (valid + chunk - 1) // chunk, one, 0)

    top = jnp.where(acc_ref[:, :, HD:] < BIG, 0.0, 1.0)

    @pl.when(jnp.max(top) > 0.5)
    def _():
        exact()

    if kx == 0:
        @pl.when(step == 0)
        def _():
            for g in range(heads):
                base = g * 2 * HD
                s = dot_nt(group(g, bl), own_ref[:, base:base + HD])
                row = lax.broadcasted_iota(jnp.int32, s.shape, 0) % bl
                col = lax.broadcasted_iota(jnp.int32, s.shape, 1)
                update(g, s, col <= row, own_ref[:, base + HD:base + 2 * HD])

    lane = lax.broadcasted_iota(jnp.int32, (bl, EXTRA), 1)
    lse_tile = jnp.zeros((bl, EXTRA), jnp.float32)
    parts = []
    for g in range(heads):
        total = acc_ref[g][:, HD:]
        some = total > 0.0
        safe = jnp.where(some, total, 1.0)
        out = acc_ref[g][:, :HD] / safe
        lse = jnp.where(some, m_ref[g] * c2 + jnp.log2(safe), NEG)
        for r in range(GR):
            h = g * GR + r
            parts.append(out[r * bl:(r + 1) * bl])
            lse_tile = jnp.where(lane % SLOT == h, lse[r * bl:(r + 1) * bl], lse_tile)
    if met:
        values = [lambda h: parts[h]]
        lses = [lse_tile]
        for met_ref in met_refs:
            values.append(lambda h, met_ref=met_ref: met_ref[0, :, h * HD:(h + 1) * HD])
            lses.append(decode(met_ref[0, :, width:]))
        parts, lse_tile = merge(values, lses, heads * GR)
    terms = encode(lse_tile)

    def write(out_ref, lead):
        for h in range(heads * GR):
            out_ref[lead + (slice(None), slice(h * HD, (h + 1) * HD))] = parts[h].astype(
                jnp.bfloat16
            )
        out_ref[lead + (slice(None), slice(width, width + EXTRA))] = terms

    if kx == 0:
        for kz in range(grid.zs):
            @pl.when(step == kz)
            def _():
                write(out_refs[kz], ())
    else:
        write(out_refs[0], (0,))


def attend(grid, kx, place, lengths, prompts, prompt_lengths, near, fars, cache, own, mets, first,
           heads):
    zs, share, cols = near.shape
    bl = own.shape[0]
    tile_len = cache.shape[2]
    width = heads * GR * HD + EXTRA

    def cache_at(head):
        def index(i, place, lengths, prompts, prompt_lengths):
            section, shard = place[0], place[1]
            at = prompts[section, grid.owner(shard, kx, 0)]
            for kz in range(1, zs):
                prompt = prompts[section, grid.owner(shard, kx, kz)]
                here = (kz <= i) & (prompt_lengths[prompt] > shard * tile_len)
                at = jnp.where(here, prompt, at)
            return (0, at, 0, first + head)

        return pl.BlockSpec((1, 1, tile_len, 2 * HD), index)

    piece = jax.ShapeDtypeStruct((bl, width), jnp.bfloat16)
    if kx == 0:
        out_shape = [piece] * zs
        out_specs = [pl.BlockSpec((bl, width), lambda i, *m: (0, 0))] * zs
    else:
        out_shape = jax.ShapeDtypeStruct((zs, bl, width), jnp.bfloat16)
        out_specs = pl.BlockSpec((1, bl, width), lambda i, *m: (i, 0, 0))
    return pl.pallas_call(
        functools.partial(attend_kernel, grid, kx, bl, share, heads, tile_len),
        grid_spec=pltpu.PrefetchScalarGridSpec(
            num_scalar_prefetch=4,
            grid=(zs,),
            in_specs=[pl.BlockSpec((zs, share, cols), lambda i, *m: (0, 0, 0))] * grid.xs
            + [cache_at(head) for head in range(heads)]
            + [pl.BlockSpec((bl, heads * 2 * HD), lambda i, *m: (0, first // heads))]
            + [pl.BlockSpec((1, bl, width), lambda i, *m: (i, 0, 0))] * len(mets),
            out_specs=out_specs,
            scratch_shapes=[
                pltpu.VMEM((grid.n * share + bl + 8, cols), jnp.float32),
                pltpu.VMEM((heads, GR * bl, 2 * HD), jnp.float32),
                pltpu.VMEM((heads, GR * bl, HD), jnp.float32),
            ],
        ),
        out_shape=out_shape,
        compiler_params=pltpu.CompilerParams(vmem_limit_bytes=40 * MIB),
        cost_estimate=pl.CostEstimate(
            flops=8 * zs * bl * cols * tile_len,
            bytes_accessed=2 * zs * tile_len * heads * 2 * HD,
            transcendentals=zs * bl * heads * GR * tile_len,
        ),
        name="attend",
    )(place, lengths, prompts, prompt_lengths, near, *fars, *([cache] * heads), own, *mets)


def finish_kernel(chunks, zs, heads, bl, place, lengths, *refs):
    out_ref = refs[-1]
    length = lengths[place[0], place[1]]
    row = lax.broadcasted_iota(jnp.int32, (bl, HD), 0)
    width = heads * GR * HD
    for c in range(chunks):
        pieces = refs[c * zs:(c + 1) * zs]
        values = [lambda h, ref=ref: ref[:, h * HD:(h + 1) * HD] for ref in pieces]
        lses = [decode(ref[:, width:]) for ref in pieces]
        parts, _ = merge(values, lses, heads * GR)
        for h in range(heads * GR):
            at = c * width + h * HD
            out_ref[0, :, at:at + HD] = jnp.where(row < length, parts[h], 0.0).astype(jnp.bfloat16)


def finish(place, lengths, pieces, chunks, zs, heads):
    bl = pieces[0].shape[0]
    cols = chunks * heads * GR * HD
    return pl.pallas_call(
        functools.partial(finish_kernel, chunks, zs, heads, bl),
        grid_spec=pltpu.PrefetchScalarGridSpec(
            num_scalar_prefetch=2,
            grid=(1,),
            in_specs=[pl.BlockSpec(piece.shape, lambda i, *m: (0, 0)) for piece in pieces],
            out_specs=pl.BlockSpec((1, bl, cols), lambda i, *m: (0, 0, 0)),
        ),
        out_shape=jax.ShapeDtypeStruct((1, bl, cols), jnp.bfloat16),
        compiler_params=pltpu.CompilerParams(vmem_limit_bytes=16 * MIB),
        name="finish",
    )(place, lengths, *pieces)


def shards(
    hidden_rows,
    carried,
    query_weight,
    response_cache,
    prompt_cache,
    prompt_lengths,
    response_lengths,
    block_prompts,
):
    grid = Grid(lax.axis_size("seq"))
    bl = hidden_rows.shape[1]
    local_kv = response_cache.shape[2] // (2 * HD)
    share = bl * 5 // 8
    chunks = 2 if local_kv % 2 == 0 else 1
    heads = local_kv // chunks
    part_cols = heads * GR * HD
    place = jnp.stack([lax.axis_index("sec"), lax.axis_index("seq")]).astype(jnp.int32)
    prompts = block_prompts[:, :, 0]

    handed = lax.ppermute(carried, "sec", [(0, 1)])
    depth = query_weight.shape[1]
    slices = split(grid, place, hidden_rows, handed, depth)
    x = [grid.swap(piece, k // grid.zs, k % grid.zs) if k else piece for k, piece in enumerate(slices)]
    part = project(grid, place, response_lengths, x, query_weight[0], bl, share, chunks)
    part = part.reshape(chunks, grid.xs, grid.zs, share, part_cols)

    def narrow(value):
        return (value * 0.125).astype(jnp.float16)

    def widen(value):
        return value.astype(jnp.float32) * 8.0

    def after(value, done):
        return lax.optimization_barrier((value, done))[0]

    def sum_x(c, done):
        parts = [part[c, kx] for kx in range(grid.xs)]
        got = [grid.swap(after(narrow(parts[kx]), done), kx, 0) for kx in range(1, grid.xs)]
        return functools.reduce(jnp.add, [parts[0]] + [widen(value) for value in got]), got

    def sum_z(held, done):
        got = [grid.swap(after(narrow(held[kz]), done), 0, kz) for kz in range(1, grid.zs)]
        total = functools.reduce(jnp.add, [held[0]] + [widen(value) for value in got])
        return total.astype(jnp.bfloat16)

    def gather_z(mine):
        return [mine] + [grid.swap(mine, 0, kz) for kz in range(1, grid.zs)]

    def gather_x(near):
        return [near] + [grid.swap(near, kx, 0) for kx in range(1, grid.xs)]

    def call(c, kx, queries, mets):
        return attend(
            grid, kx, place, response_lengths, prompts, prompt_lengths, queries[0], queries[1:],
            prompt_cache, response_cache[0], mets, c * heads, heads,
        )

    queries = [None] * chunks
    sent = [[] for _ in range(chunks)]
    held, got = sum_x(0, ())
    mine = sum_z(held, ())
    column = gather_z(mine)
    near = jnp.stack(column)
    if chunks > 1:
        held, _ = sum_x(1, got)
        mine = sum_z(held, column)
    queries[0] = gather_x(near)
    if chunks > 1:
        column = gather_z(mine)
        queries[0][0] = after(queries[0][0], mine)
    for kx in range(1, grid.xs):
        out = call(0, kx, queries[0], [])
        sent[0].append(grid.swap(out, kx, 0))
    if chunks > 1:
        near = jnp.stack(after(column, out))
        queries[1] = gather_x(near)
        queries[0][0] = after(queries[0][0], near)
        for kx in range(1, grid.xs):
            sent[1].append(None)
    pieces = []
    for c in range(chunks):
        if c:
            for kx in range(1, grid.xs):
                sent[c][kx - 1] = grid.swap(call(c, kx, queries[c], []), kx, 0)
        held = call(c, 0, queries[c], sent[c])
        pieces.append(held[0])
        pieces.extend(grid.swap(held[kz], 0, kz) for kz in range(1, grid.zs))
    return finish(place, response_lengths, pieces, chunks, grid.zs, heads)


def solution(mesh):
    placed = (
        P("sec", "seq", None),
        P("sec", "seq", None),
        P("sec", "seq", "tp"),
        P("sec", "seq", "tp"),
        P("sec", None, "seq", "tp"),
        P(),
        P(),
        P(),
    )
    return jax.shard_map(
        shards, mesh=mesh, in_specs=placed, out_specs=P("sec", "seq", "tp"), check_vma=False
    )
```

time: 939 us -> 151 us (0.16)
  waiting for transfers between devices: 545 us -> 47 us
  local copies, waits for them, and re-layouts: 188 us -> 3.52 us
  other arithmetic: 90.4 us -> 0.7 us
  matrix products: 77.5 us -> 0 us
  Pallas kernels: 0 us -> 46.4 us
  starting transfers between devices: 10.5 us -> 53.5 us
  between operations: 13.6 us -> 0.19 us
    all_gather x2 -> x0, waiting for transfers between devices: 451 us -> none  [the longest x1 402 us: shards(): lax.all_gather(query_weight[0], 'seq', axis=0, tiled=True)]
    gather x14 -> x0, local copies, waits for them, and re-layouts: 140 us -> none  [the longest x12 139 us: tile_parts(): jnp.take(prompt_tiles, group_prompts, axis=0)]
    all_to_all x2 -> x0, waiting for transfers between devices: 91.6 us -> none  [the longest x1 85.1 us: shards(): lax.all_to_all(sums, 'seq', split_axis=0, concat_axis=0, tiled=True)]
    dot_general x7 -> x0, matrix products: 77.5 us -> none  [the longest x3 34.4 us: partial_attend(): jnp.einsum('rgqk,kgd->rgqd', weights, value_rows, preferred_element_type=...]
    ppermute x1 -> x32, starting transfers between devices: 2.4 us -> 53.5 us  [the longest x31 51.1 us: swap(): return lax.ppermute(value, 'seq', pairs)]
    pallas_call x0 -> x7, Pallas kernels: none -> 46.4 us  [the longest x4 40.7 us: attend(): pl.pallas_call(functools.partial(attend_kernel, grid, kx, bl, share, head...]
    ppermute x1 -> x32, waiting for transfers between devices: 1.88 us -> 47 us  [the longest x31 45.2 us: swap(): return lax.ppermute(value, 'seq', pairs)]
    while x6 -> x0, local copies, waits for them, and re-layouts: 43.7 us -> none
  transfers between devices with their start and end apart: 5 -> 32, of which waited for: 5 -> 17; matrix products, arithmetic and copies ran while one was open for 1% -> 0% of each run, Pallas kernels for 0% -> 27%
where the time goes in v2:
time: 151 us
  starting transfers between devices  53.5 us (35%)
  waiting for transfers between devices  47 us (31%)
  Pallas kernels  46.4 us (31%)
  local copies, waits for them, and re-layouts  3.52 us (2%)
    ppermute x31, starting transfers between devices, swap(): return lax.ppermute(value, 'seq', pairs)  51.1 us
    ppermute x31, waiting for transfers between devices, swap(): return lax.ppermute(value, 'seq', pairs)  45.2 us
    pallas_call x4, Pallas kernels, attend(): pl.pallas_call(functools.partial(attend_kernel, grid, kx, bl, share, head...  40.7 us
    unnamed x14, local copies, waits for them, and re-layouts  3.52 us
  transfers between devices with their start and end apart: 32, of which 17 were waited for; matrix products, arithmetic and copies ran while one was open for 0% of the time, Pallas kernels for 27%

profile of v2, /device:TPU:0, one launch (start us, length us, event | category | flops | bytes accessed | tf_op | source)
XLA Modules:
  0.0 151.2 jit_solution(3836861396992767865)
XLA Ops:
  0.0 2.4 %collective-permute-start = (bf16[1,64,5120]{2,1,0:T(8,128)(2,1)}, bf16[1,64,5120]{2,1,0:T(8,128)(2,1)S(1)}, u32[]{:S(2)}, u32[]{:S(2)}) collective-permute-start(bf16[1,64,5120]{2,1,0:T(8,128)(2,1)} %param.9), channel_id=1, source_target_pairs={{0,16},{1,17},{2,18},{3,19},{4,20},{5,21},{6,22},{7,23},{8,24},{9,... | collective-permute-start | bytes 1966088 | tf_op jit(solution)/shard_map/ppermute | solution.py:461
  2.5 1.8 %collective-permute-done.handed_ref = bf16[1,64,5120]{2,1,0:T(8,128)(2,1)S(1)} collective-permute-done((bf16[1,64,5120]{2,1,0:T(8,128)(2,1)}, bf16[1,64,5120]{2,1,0:T(8,128)(2,1)S(1)}, u32[]{:S(2)}, u32[]{:S(2)}) %collective-permute-start) | collective-permute-done | bytes 655392 | tf_op jit(solution)/shard_map/ppermute | solution.py:461
  4.3 1.1 copy-done.2
  5.4 0.7 split.1
  6.1 2.5 %collective-permute-start.1 = (bf16[64,640]{1,0:T(8,128)(2,1)S(1)}, bf16[64,640]{1,0:T(8,128)(2,1)S(1)}, u32[]{:S(2)}, u32[]{:S(2)}) collective-permute-start(bf16[64,640]{1,0:T(8,128)(2,1)S(1)} %get-tuple-element.32), channel_id=1, source_target_pairs={{0,4},{2,6},{4,0},{6,2},{8,12},{10,14},{12,8},{14,10},{1,5},{3,7},... | collective-permute-start | bytes 245768 | tf_op jit(solution)/shard_map/ppermute | solution.py:40
  8.6 2.6 %collective-permute-start.2 = (bf16[64,640]{1,0:T(8,128)(2,1)S(1)}, bf16[64,640]{1,0:T(8,128)(2,1)S(1)}, u32[]{:S(2)}, u32[]{:S(2)}) collective-permute-start(bf16[64,640]{1,0:T(8,128)(2,1)S(1)} %get-tuple-element.33), channel_id=1, source_target_pairs={{0,8},{2,10},{4,12},{6,14},{8,0},{10,2},{12,4},{14,6},{1,9},{3,11}... | collective-permute-start | bytes 245768 | tf_op jit(solution)/shard_map/ppermute | solution.py:40
  11.2 1.7 %collective-permute-start.4 = (bf16[64,640]{1,0:T(8,128)(2,1)S(1)}, bf16[64,640]{1,0:T(8,128)(2,1)S(1)}, u32[]{:S(2)}, u32[]{:S(2)}) collective-permute-start(bf16[64,640]{1,0:T(8,128)(2,1)S(1)} %get-tuple-element.35), channel_id=1, source_target_pairs={{0,2},{2,0},{4,6},{6,4},{8,10},{10,8},{12,14},{14,12},{1,3},{3,1},... | collective-permute-start | bytes 245768 | tf_op jit(solution)/shard_map/ppermute | solution.py:40
  12.9 0.6 collective-permute-start.5
  13.5 4.4 %collective-permute-start.6 = (bf16[64,640]{1,0:T(8,128)(2,1)S(1)}, bf16[64,640]{1,0:T(8,128)(2,1)S(1)}, u32[]{:S(2)}, u32[]{:S(2)}) collective-permute-start(bf16[64,640]{1,0:T(8,128)(2,1)S(1)} %get-tuple-element.37), channel_id=1, source_target_pairs={{0,10},{2,8},{4,14},{6,12},{8,2},{10,0},{12,6},{14,4},{1,11},{3,9}... | collective-permute-start | bytes 245768 | tf_op jit(solution)/shard_map/ppermute | solution.py:40
  17.9 4.1 %collective-permute-start.7 = (bf16[64,640]{1,0:T(8,128)(2,1)S(1)}, bf16[64,640]{1,0:T(8,128)(2,1)S(1)}, u32[]{:S(2)}, u32[]{:S(2)}) collective-permute-start(bf16[64,640]{1,0:T(8,128)(2,1)S(1)} %get-tuple-element.38), channel_id=1, source_target_pairs={{0,14},{2,12},{4,10},{6,8},{8,6},{10,4},{12,2},{14,0},{1,15},{3,13... | collective-permute-start | bytes 245768 | tf_op jit(solution)/shard_map/ppermute | solution.py:40
  22.0 3.9 %collective-permute-done.6.refs_6_ = bf16[64,640]{1,0:T(8,128)(2,1)S(1)} collective-permute-done((bf16[64,640]{1,0:T(8,128)(2,1)S(1)}, bf16[64,640]{1,0:T(8,128)(2,1)S(1)}, u32[]{:S(2)}, u32[]{:S(2)}) %collective-permute-start.6) | collective-permute-done | bytes 81952 | tf_op jit(solution)/shard_map/ppermute | solution.py:40
  26.0 1.7 %copy-done = bf16[1,640,2048]{2,1,0:T(8,128)(2,1)S(1)} copy-done((bf16[1,640,2048]{2,1,0:T(8,128)(2,1)S(1)}, bf16[1,640,2048]{2,1,0:T(8,128)(2,1)}, u32[]{:S(2)}) %copy-start) | copy-done | bytes 2621464
  27.7 0.7 copy-done.3
  28.4 2.6 %project.1 = f32[2,2,160,1024]{3,2,1,0:T(8,128)S(1)} custom-call(s32[2]{0:T(128)S(1)} %pad_add_fusion.place.refs_0_, s32[2,8]{1,0:T(2,128)S(1)} %copy-done.3, bf16[64,640]{1,0:T(8,128)(2,1)S(1)} %get-tuple-element.31.refs_0_, bf16[64,640]{1,0:T(8,128)(2,1)S(1)} %collective-permute-done.1.refs_1_, bf16[64,640]{1,0:T(8,128)(2,1)S(1)} %collective-permute-done.2.refs_2_, ...), custom_call_target="tpu_custom_call" | custom-call | flops 838860800 | bytes 5242880 | tf_op jit(solution)/shard_map/project/pallas_call | solution.py:112
  31.1 0.6 collective-permute-start.8
  31.7 7.3 %collective-permute-done.8 = f16[4,40,1024]{2,1,0:T(8,128)(2,1)S(1)} collective-permute-done((f16[4,40,1024]{2,1,0:T(8,128)(2,1)S(1)}, f16[4,40,1024]{2,1,0:T(8,128)(2,1)S(1)}, u32[]{:S(2)}, u32[]{:S(2)}) %collective-permute-start.8) | collective-permute-done | bytes 327712 | tf_op jit(solution)/shard_map/ppermute | solution.py:40
  39.0 0.6 collective-permute-start.15
  39.6 6.5 %collective-permute-done.15 = f16[4,40,1024]{2,1,0:T(8,128)(2,1)S(1)} collective-permute-done((f16[4,40,1024]{2,1,0:T(8,128)(2,1)S(1)}, f16[4,40,1024]{2,1,0:T(8,128)(2,1)S(1)}, u32[]{:S(2)}, u32[]{:S(2)}) %collective-permute-start.15) | collective-permute-done | bytes 327712 | tf_op jit(solution)/shard_map/ppermute | solution.py:40
  46.4 3.3 %collective-permute-start.11 = (f16[40,1024]{1,0:T(8,128)(2,1)S(1)}, f16[40,1024]{1,0:T(8,128)(2,1)S(1)}, u32[]{:S(2)}, u32[]{:S(2)}) collective-permute-start(f16[40,1024]{1,0:T(8,128)(2,1)S(1)} %get-tuple-element.65), channel_id=1, source_target_pairs={{0,12},{2,14},{4,8},{6,10},{8,4},{10,6},{12,0},{14,2},{1,13},{3,15... | collective-permute-start | bytes 245768 | tf_op jit(solution)/shard_map/ppermute | solution.py:40
  49.7 1.4 collective-permute-start.9
  51.1 1.0 collective-permute-start.10
  52.1 1.6 %collective-permute-done.11 = f16[40,1024]{1,0:T(8,128)(2,1)S(1)} collective-permute-done((f16[40,1024]{1,0:T(8,128)(2,1)S(1)}, f16[40,1024]{1,0:T(8,128)(2,1)S(1)}, u32[]{:S(2)}, u32[]{:S(2)}) %collective-permute-start.11) | collective-permute-done | bytes 81952 | tf_op jit(solution)/shard_map/ppermute | solution.py:40
  53.7 0.7 collective-permute-done.9
  54.4 3.2 %collective-permute-done.10 = f16[40,1024]{1,0:T(8,128)(2,1)S(1)} collective-permute-done((f16[40,1024]{1,0:T(8,128)(2,1)S(1)}, f16[40,1024]{1,0:T(8,128)(2,1)S(1)}, u32[]{:S(2)}, u32[]{:S(2)}) %collective-permute-start.10) | collective-permute-done | bytes 81952 | tf_op jit(solution)/shard_map/ppermute | solution.py:40
  57.7 2.6 %collective-permute-start.14 = (bf16[40,1024]{1,0:T(8,128)(2,1)S(1)}, bf16[40,1024]{1,0:T(8,128)(2,1)S(1)}, u32[]{:S(2)}, u32[]{:S(2)}) collective-permute-start(bf16[40,1024]{1,0:T(8,128)(2,1)S(1)} %fusion.19), channel_id=1, source_target_pairs={{0,12},{2,14},{4,8},{6,10},{8,4},{10,6},{12,0},{14,2},{1,13},{3,15... | collective-permute-start | bytes 245768 | tf_op jit(solution)/shard_map/ppermute | solution.py:40
  60.2 1.9 %collective-permute-start.12 = (bf16[40,1024]{1,0:T(8,128)(2,1)S(1)}, bf16[40,1024]{1,0:T(8,128)(2,1)S(1)}, u32[]{:S(2)}, u32[]{:S(2)}) collective-permute-start(bf16[40,1024]{1,0:T(8,128)(2,1)S(1)} %fusion.19), channel_id=1, source_target_pairs={{0,4},{2,6},{4,0},{6,2},{8,12},{10,14},{12,8},{14,10},{1,5},{3,7},... | collective-permute-start | bytes 245768 | tf_op jit(solution)/shard_map/ppermute | solution.py:40
  62.1 1.9 %collective-permute-done.14 = bf16[40,1024]{1,0:T(8,128)(2,1)S(1)} collective-permute-done((bf16[40,1024]{1,0:T(8,128)(2,1)S(1)}, bf16[40,1024]{1,0:T(8,128)(2,1)S(1)}, u32[]{:S(2)}, u32[]{:S(2)}) %collective-permute-start.14) | collective-permute-done | bytes 81952 | tf_op jit(solution)/shard_map/ppermute | solution.py:40
  64.0 1.8 %collective-permute-done.13 = bf16[40,1024]{1,0:T(8,128)(2,1)S(1)} collective-permute-done((bf16[40,1024]{1,0:T(8,128)(2,1)S(1)}, bf16[40,1024]{1,0:T(8,128)(2,1)S(1)}, u32[]{:S(2)}, u32[]{:S(2)}) %collective-permute-start.13) | collective-permute-done | bytes 81952 | tf_op jit(solution)/shard_map/ppermute | solution.py:40
  66.8 1.2 collective-permute-start.16
  68.0 2.4 %collective-permute-start.17 = (f16[40,1024]{1,0:T(8,128)(2,1)S(1)}, f16[40,1024]{1,0:T(8,128)(2,1)S(1)}, u32[]{:S(2)}, u32[]{:S(2)}) collective-permute-start(f16[40,1024]{1,0:T(8,128)(2,1)S(1)} %get-tuple-element.41), channel_id=1, source_target_pairs={{0,8},{2,10},{4,12},{6,14},{8,0},{10,2},{12,4},{14,6},{1,9},{3,11}... | collective-permute-start | bytes 245768 | tf_op jit(solution)/shard_map/ppermute | solution.py:40
  70.4 0.9 collective-permute-start.18
  71.3 6.0 %collective-permute-done.17 = f16[40,1024]{1,0:T(8,128)(2,1)S(1)} collective-permute-done((f16[40,1024]{1,0:T(8,128)(2,1)S(1)}, f16[40,1024]{1,0:T(8,128)(2,1)S(1)}, u32[]{:S(2)}, u32[]{:S(2)}) %collective-permute-start.17) | collective-permute-done | bytes 81952 | tf_op jit(solution)/shard_map/ppermute | solution.py:40
  77.6 3.4 %collective-permute-start.21 = (bf16[40,1024]{1,0:T(8,128)(2,1)S(1)}, bf16[40,1024]{1,0:T(8,128)(2,1)S(1)}, u32[]{:S(2)}, u32[]{:S(2)}) collective-permute-start(bf16[40,1024]{1,0:T(8,128)(2,1)S(1)} %fusion.12), channel_id=1, source_target_pairs={{0,12},{2,14},{4,8},{6,10},{8,4},{10,6},{12,0},{14,2},{1,13},{3,15... | collective-permute-start | bytes 245768 | tf_op jit(solution)/shard_map/ppermute | solution.py:40
  81.3 0.7 collective-permute-start.19
  82.1 8.9 %attend.4 = bf16[4,64,1152]{2,1,0:T(8,128)(2,1)S(1)} custom-call(s32[2]{0:T(128)S(1)} %pad_add_fusion.place.refs_0_, s32[2,8]{1,0:T(2,128)S(1)} %copy-done.4, s32[2,8]{1,0:T(2,128)S(1)} %bitcast.65, s32[8]{0:T(128)S(1)} %copy-done.6, bf16[4,40,1024]{2,1,0:T(8,128)(2,1)S(1)} %pad_maximum_fusion.refs_4_, ...), custom_call_target="tpu_custom_call" | custom-call | flops 4294967296 | bytes 8388608 | tf_op jit(solution)/shard_map/attend/pallas_call | solution.py:382
  91.1 2.0 %collective-permute-start.27 = (bf16[4,40,1024]{2,1,0:T(8,128)(2,1)S(1)}, bf16[4,40,1024]{2,1,0:T(8,128)(2,1)S(1)}, u32[]{:S(2)}, u32[]{:S(2)}) collective-permute-start(bf16[4,40,1024]{2,1,0:T(8,128)(2,1)S(1)} %pad_maximum_fusion.1.refs_4_), channel_id=1, source_target_pairs={{0,2},{2,0},{4,6},{6,4},{8,10},{10,8},{12,14},{14,12},{1,3},{3,1},... | collective-permute-start | bytes 983048 | tf_op jit(solution)/shard_map/ppermute | solution.py:40
  93.2 5.1 %collective-permute-done.27.refs_5_ = bf16[4,40,1024]{2,1,0:T(8,128)(2,1)S(1)} collective-permute-done((bf16[4,40,1024]{2,1,0:T(8,128)(2,1)S(1)}, bf16[4,40,1024]{2,1,0:T(8,128)(2,1)S(1)}, u32[]{:S(2)}, u32[]{:S(2)}) %collective-permute-start.27) | collective-permute-done | bytes 327712 | tf_op jit(solution)/shard_map/ppermute | solution.py:40
  98.3 9.1 %attend.6 = bf16[4,64,1152]{2,1,0:T(8,128)(2,1)S(1)} custom-call(s32[2]{0:T(128)S(1)} %pad_add_fusion.place.refs_0_, s32[2,8]{1,0:T(2,128)S(1)} %copy-done.4, s32[2,8]{1,0:T(2,128)S(1)} %bitcast.66, s32[8]{0:T(128)S(1)} %copy-done.6, bf16[4,40,1024]{2,1,0:T(8,128)(2,1)S(1)} %pad_maximum_fusion.1.refs_4_, ...), custom_call_target="tpu_custom_call" | custom-call | flops 4294967296 | bytes 8388608 | tf_op jit(solution)/shard_map/attend/pallas_call | solution.py:382
  107.4 2.8 %collective-permute-start.28 = (bf16[4,64,1152]{2,1,0:T(8,128)(2,1)S(1)}, bf16[4,64,1152]{2,1,0:T(8,128)(2,1)S(1)}, u32[]{:S(2)}, u32[]{:S(2)}) collective-permute-start(bf16[4,64,1152]{2,1,0:T(8,128)(2,1)S(1)} %attend.6), channel_id=1, source_target_pairs={{0,2},{2,0},{4,6},{6,4},{8,10},{10,8},{12,14},{14,12},{1,3},{3,1},... | collective-permute-start | bytes 1769480 | tf_op jit(solution)/shard_map/ppermute | solution.py:40
  110.4 11.4 %attend.5 = (bf16[64,1152]{1,0:T(8,128)(2,1)S(1)}, bf16[64,1152]{1,0:T(8,128)(2,1)S(1)}, bf16[64,1152]{1,0:T(8,128)(2,1)S(1)}, bf16[64,1152]{1,0:T(8,128)(2,1)S(1)}) custom-call(s32[2]{0:T(128)S(1)} %pad_add_fusion.place.refs_0_, s32[2,8]{1,0:T(2,128)S(1)} %copy-done.4, s32[2,8]{1,0:T(2,128)S(1)} %bitcast.67, s32[8]{0:T(128)S(1)} %copy-done.6, ...), custom_call_target="tpu_custom_call" | custom-call | flops 4294967296 | bytes 8388608 | tf_op jit(solution)/shard_map/attend/pallas_call | solution.py:382
  121.7 2.6 %collective-permute-start.24 = (bf16[64,1152]{1,0:T(8,128)(2,1)S(1)}, bf16[64,1152]{1,0:T(8,128)(2,1)S(1)}, u32[]{:S(2)}, u32[]{:S(2)}) collective-permute-start(bf16[64,1152]{1,0:T(8,128)(2,1)S(1)} %get-tuple-element.50), channel_id=1, source_target_pairs={{0,4},{2,6},{4,0},{6,2},{8,12},{10,14},{12,8},{14,10},{1,5},{3,7},... | collective-permute-start | bytes 442376 | tf_op jit(solution)/shard_map/ppermute | solution.py:40
  124.3 2.4 %collective-permute-start.26 = (bf16[64,1152]{1,0:T(8,128)(2,1)S(1)}, bf16[64,1152]{1,0:T(8,128)(2,1)S(1)}, u32[]{:S(2)}, u32[]{:S(2)}) collective-permute-start(bf16[64,1152]{1,0:T(8,128)(2,1)S(1)} %get-tuple-element.52), channel_id=1, source_target_pairs={{0,12},{2,14},{4,8},{6,10},{8,4},{10,6},{12,0},{14,2},{1,13},{3,15... | collective-permute-start | bytes 442376 | tf_op jit(solution)/shard_map/ppermute | solution.py:40
  126.8 11.4 %attend.7 = (bf16[64,1152]{1,0:T(8,128)(2,1)S(1)}, bf16[64,1152]{1,0:T(8,128)(2,1)S(1)}, bf16[64,1152]{1,0:T(8,128)(2,1)S(1)}, bf16[64,1152]{1,0:T(8,128)(2,1)S(1)}) custom-call(s32[2]{0:T(128)S(1)} %pad_add_fusion.place.refs_0_, s32[2,8]{1,0:T(2,128)S(1)} %copy-done.4, s32[2,8]{1,0:T(2,128)S(1)} %bitcast.68, s32[8]{0:T(128)S(1)} %copy-done.6, ...), custom_call_target="tpu_custom_call" | custom-call | flops 4294967296 | bytes 8388608 | tf_op jit(solution)/shard_map/attend/pallas_call | solution.py:382
  138.2 1.8 %collective-permute-start.29 = (bf16[64,1152]{1,0:T(8,128)(2,1)S(1)}, bf16[64,1152]{1,0:T(8,128)(2,1)S(1)}, u32[]{:S(2)}, u32[]{:S(2)}) collective-permute-start(bf16[64,1152]{1,0:T(8,128)(2,1)S(1)} %get-tuple-element.54), channel_id=1, source_target_pairs={{0,4},{2,6},{4,0},{6,2},{8,12},{10,14},{12,8},{14,10},{1,5},{3,7},... | collective-permute-start | bytes 442376 | tf_op jit(solution)/shard_map/ppermute | solution.py:40
  139.9 2.7 %collective-permute-start.31 = (bf16[64,1152]{1,0:T(8,128)(2,1)S(1)}, bf16[64,1152]{1,0:T(8,128)(2,1)S(1)}, u32[]{:S(2)}, u32[]{:S(2)}) collective-permute-start(bf16[64,1152]{1,0:T(8,128)(2,1)S(1)} %get-tuple-element.56), channel_id=1, source_target_pairs={{0,12},{2,14},{4,8},{6,10},{8,4},{10,6},{12,0},{14,2},{1,13},{3,15... | collective-permute-start | bytes 442376 | tf_op jit(solution)/shard_map/ppermute | solution.py:40
  142.6 0.7 collective-permute-done.29.refs_5_
  143.4 5.5 %collective-permute-done.30.refs_6_ = bf16[64,1152]{1,0:T(8,128)(2,1)S(1)} collective-permute-done((bf16[64,1152]{1,0:T(8,128)(2,1)S(1)}, bf16[64,1152]{1,0:T(8,128)(2,1)S(1)}, u32[]{:S(2)}, u32[]{:S(2)}) %collective-permute-start.30) | collective-permute-done | bytes 147488 | tf_op jit(solution)/shard_map/ppermute | solution.py:40
  148.9 2.3 %finish.1 = bf16[1,64,2048]{2,1,0:T(8,128)(2,1)} custom-call(s32[2]{0:T(128)S(1)} %pad_add_fusion.place.refs_0_, s32[2,8]{1,0:T(2,128)S(1)} %copy-done.4, bf16[64,1152]{1,0:T(8,128)(2,1)S(1)} %get-tuple-element.49.refs_0_, bf16[64,1152]{1,0:T(8,128)(2,1)S(1)} %collective-permute-done.24.refs_1_, bf16[64,1152]{1,0:T(8,128)(2,1)S(1)} %collective-permute-done.25.refs_2_, ...), custom_call_target="tpu_custom_call" | custom-call | tf_op jit(solution)/shard_map/finish/pallas_call | solution.py:427
  (46 shorter events, 2.5 us)
Async XLA Ops:
  0.0 4.3 %collective-permute-start = (bf16[1,64,5120]{2,1,0:T(8,128)(2,1)}, bf16[1,64,5120]{2,1,0:T(8,128)(2,1)S(1)}, u32[]{:S(2)}, u32[]{:S(2)}) collective-permute-start(bf16[1,64,5120]{2,1,0:T(8,128)(2,1)} %param.9), channel_id=1, source_target_pairs={{0,16},{1,17},{2,18},{3,19},{4,20},{5,21},{6,22},{7,23},{8,24},{9,... | collective-permute-start | bytes 1966088 | tf_op jit(solution)/shard_map/ppermute | solution.py:461
  4.3 1.1 copy-start.2
  6.1 7.4 %collective-permute-start.1 = (bf16[64,640]{1,0:T(8,128)(2,1)S(1)}, bf16[64,640]{1,0:T(8,128)(2,1)S(1)}, u32[]{:S(2)}, u32[]{:S(2)}) collective-permute-start(bf16[64,640]{1,0:T(8,128)(2,1)S(1)} %get-tuple-element.32), channel_id=1, source_target_pairs={{0,4},{2,6},{4,0},{6,2},{8,12},{10,14},{12,8},{14,10},{1,5},{3,7},... | collective-permute-start | bytes 245768 | tf_op jit(solution)/shard_map/ppermute | solution.py:40
  8.6 9.4 %collective-permute-start.2 = (bf16[64,640]{1,0:T(8,128)(2,1)S(1)}, bf16[64,640]{1,0:T(8,128)(2,1)S(1)}, u32[]{:S(2)}, u32[]{:S(2)}) collective-permute-start(bf16[64,640]{1,0:T(8,128)(2,1)S(1)} %get-tuple-element.33), channel_id=1, source_target_pairs={{0,8},{2,10},{4,12},{6,14},{8,0},{10,2},{12,4},{14,6},{1,9},{3,11}... | collective-permute-start | bytes 245768 | tf_op jit(solution)/shard_map/ppermute | solution.py:40
  11.1 10.9 %collective-permute-start.3 = (bf16[64,640]{1,0:T(8,128)(2,1)S(1)}, bf16[64,640]{1,0:T(8,128)(2,1)S(1)}, u32[]{:S(2)}, u32[]{:S(2)}) collective-permute-start(bf16[64,640]{1,0:T(8,128)(2,1)S(1)} %get-tuple-element.34), channel_id=1, source_target_pairs={{0,12},{2,14},{4,8},{6,10},{8,4},{10,6},{12,0},{14,2},{1,13},{3,15... | collective-permute-start | bytes 245768 | tf_op jit(solution)/shard_map/ppermute | solution.py:40
  11.2 10.9 %collective-permute-start.4 = (bf16[64,640]{1,0:T(8,128)(2,1)S(1)}, bf16[64,640]{1,0:T(8,128)(2,1)S(1)}, u32[]{:S(2)}, u32[]{:S(2)}) collective-permute-start(bf16[64,640]{1,0:T(8,128)(2,1)S(1)} %get-tuple-element.35), channel_id=1, source_target_pairs={{0,2},{2,0},{4,6},{6,4},{8,10},{10,8},{12,14},{14,12},{1,3},{3,1},... | collective-permute-start | bytes 245768 | tf_op jit(solution)/shard_map/ppermute | solution.py:40
  12.9 9.2 %collective-permute-start.5 = (bf16[64,640]{1,0:T(8,128)(2,1)S(1)}, bf16[64,640]{1,0:T(8,128)(2,1)S(1)}, u32[]{:S(2)}, u32[]{:S(2)}) collective-permute-start(bf16[64,640]{1,0:T(8,128)(2,1)S(1)} %get-tuple-element.36), channel_id=1, source_target_pairs={{0,6},{2,4},{4,2},{6,0},{8,14},{10,12},{12,10},{14,8},{1,7},{3,5},... | collective-permute-start | bytes 245768 | tf_op jit(solution)/shard_map/ppermute | solution.py:40
  13.5 12.4 %collective-permute-start.6 = (bf16[64,640]{1,0:T(8,128)(2,1)S(1)}, bf16[64,640]{1,0:T(8,128)(2,1)S(1)}, u32[]{:S(2)}, u32[]{:S(2)}) collective-permute-start(bf16[64,640]{1,0:T(8,128)(2,1)S(1)} %get-tuple-element.37), channel_id=1, source_target_pairs={{0,10},{2,8},{4,14},{6,12},{8,2},{10,0},{12,6},{14,4},{1,11},{3,9}... | collective-permute-start | bytes 245768 | tf_op jit(solution)/shard_map/ppermute | solution.py:40
  17.9 8.0 %collective-permute-start.7 = (bf16[64,640]{1,0:T(8,128)(2,1)S(1)}, bf16[64,640]{1,0:T(8,128)(2,1)S(1)}, u32[]{:S(2)}, u32[]{:S(2)}) collective-permute-start(bf16[64,640]{1,0:T(8,128)(2,1)S(1)} %get-tuple-element.38), channel_id=1, source_target_pairs={{0,14},{2,12},{4,10},{6,8},{8,6},{10,4},{12,2},{14,0},{1,15},{3,13... | collective-permute-start | bytes 245768 | tf_op jit(solution)/shard_map/ppermute | solution.py:40
  26.0 1.7 %copy-start = (bf16[1,640,2048]{2,1,0:T(8,128)(2,1)S(1)}, bf16[1,640,2048]{2,1,0:T(8,128)(2,1)}, u32[]{:S(2)}) copy-start(bf16[1,640,2048]{2,1,0:T(8,128)(2,1)} %param.10) | copy-start | bytes 7864324
  27.7 0.7 copy-start.3
  31.1 7.9 %collective-permute-start.8 = (f16[4,40,1024]{2,1,0:T(8,128)(2,1)S(1)}, f16[4,40,1024]{2,1,0:T(8,128)(2,1)S(1)}, u32[]{:S(2)}, u32[]{:S(2)}) collective-permute-start(f16[4,40,1024]{2,1,0:T(8,128)(2,1)S(1)} %get-tuple-element.60), channel_id=1, source_target_pairs={{0,2},{2,0},{4,6},{6,4},{8,10},{10,8},{12,14},{14,12},{1,3},{3,1},... | collective-permute-start | bytes 983048 | tf_op jit(solution)/shard_map/ppermute | solution.py:40
  39.0 43.1 %copy-start.1 = (bf16[1,64,1024]{2,1,0:T(8,128)(2,1)S(1)}, bf16[1,64,1024]{2,1,0:T(8,128)(2,1)}, u32[]{:S(2)}) copy-start(bf16[1,64,1024]{2,1,0:T(8,128)(2,1)} %param.11) | copy-start | bytes 393220
  39.0 43.1 %copy-start.4 = (s32[2,8]{1,0:T(2,128)S(1)}, s32[2,8]{1,0:T(2,128)}, u32[]{:S(2)}) copy-start(s32[2,8]{1,0:T(2,128)} %lengths.3) | copy-start | bytes 196
  39.0 43.1 %copy-start.5 = (s32[2,8,1]{1,2,0:T(1,128)S(1)}, s32[2,8,1]{1,2,0:T(1,128)}, u32[]{:S(2)}) copy-start(s32[2,8,1]{1,2,0:T(1,128)} %param.15) | copy-start | bytes 196
  39.0 43.1 %copy-start.6 = (s32[8]{0:T(128)S(1)}, s32[8]{0:T(128)}, u32[]{:S(2)}) copy-start(s32[8]{0:T(128)} %refs_3_.7) | copy-start | bytes 100
  39.0 7.1 %collective-permute-start.15 = (f16[4,40,1024]{2,1,0:T(8,128)(2,1)S(1)}, f16[4,40,1024]{2,1,0:T(8,128)(2,1)S(1)}, u32[]{:S(2)}, u32[]{:S(2)}) collective-permute-start(f16[4,40,1024]{2,1,0:T(8,128)(2,1)S(1)} %get-tuple-element.39), channel_id=1, source_target_pairs={{0,2},{2,0},{4,6},{6,4},{8,10},{10,8},{12,14},{14,12},{1,3},{3,1},... | collective-permute-start | bytes 983048 | tf_op jit(solution)/shard_map/ppermute | solution.py:40
  46.4 7.3 %collective-permute-start.11 = (f16[40,1024]{1,0:T(8,128)(2,1)S(1)}, f16[40,1024]{1,0:T(8,128)(2,1)S(1)}, u32[]{:S(2)}, u32[]{:S(2)}) collective-permute-start(f16[40,1024]{1,0:T(8,128)(2,1)S(1)} %get-tuple-element.65), channel_id=1, source_target_pairs={{0,12},{2,14},{4,8},{6,10},{8,4},{10,6},{12,0},{14,2},{1,13},{3,15... | collective-permute-start | bytes 245768 | tf_op jit(solution)/shard_map/ppermute | solution.py:40
  49.7 4.6 %collective-permute-start.9 = (f16[40,1024]{1,0:T(8,128)(2,1)S(1)}, f16[40,1024]{1,0:T(8,128)(2,1)S(1)}, u32[]{:S(2)}, u32[]{:S(2)}) collective-permute-start(f16[40,1024]{1,0:T(8,128)(2,1)S(1)} %get-tuple-element.64), channel_id=1, source_target_pairs={{0,4},{2,6},{4,0},{6,2},{8,12},{10,14},{12,8},{14,10},{1,5},{3,7},... | collective-permute-start | bytes 245768 | tf_op jit(solution)/shard_map/ppermute | solution.py:40
  51.1 6.5 %collective-permute-start.10 = (f16[40,1024]{1,0:T(8,128)(2,1)S(1)}, f16[40,1024]{1,0:T(8,128)(2,1)S(1)}, u32[]{:S(2)}, u32[]{:S(2)}) collective-permute-start(f16[40,1024]{1,0:T(8,128)(2,1)S(1)} %get-tuple-element.66), channel_id=1, source_target_pairs={{0,8},{2,10},{4,12},{6,14},{8,0},{10,2},{12,4},{14,6},{1,9},{3,11}... | collective-permute-start | bytes 245768 | tf_op jit(solution)/shard_map/ppermute | solution.py:40
  57.7 6.3 %collective-permute-start.14 = (bf16[40,1024]{1,0:T(8,128)(2,1)S(1)}, bf16[40,1024]{1,0:T(8,128)(2,1)S(1)}, u32[]{:S(2)}, u32[]{:S(2)}) collective-permute-start(bf16[40,1024]{1,0:T(8,128)(2,1)S(1)} %fusion.19), channel_id=1, source_target_pairs={{0,12},{2,14},{4,8},{6,10},{8,4},{10,6},{12,0},{14,2},{1,13},{3,15... | collective-permute-start | bytes 245768 | tf_op jit(solution)/shard_map/ppermute | solution.py:40
  60.2 5.6 %collective-permute-start.13 = (bf16[40,1024]{1,0:T(8,128)(2,1)S(1)}, bf16[40,1024]{1,0:T(8,128)(2,1)S(1)}, u32[]{:S(2)}, u32[]{:S(2)}) collective-permute-start(bf16[40,1024]{1,0:T(8,128)(2,1)S(1)} %fusion.19), channel_id=1, source_target_pairs={{0,8},{2,10},{4,12},{6,14},{8,0},{10,2},{12,4},{14,6},{1,9},{3,11}... | collective-permute-start | bytes 245768 | tf_op jit(solution)/shard_map/ppermute | solution.py:40
  60.2 6.0 %collective-permute-start.12 = (bf16[40,1024]{1,0:T(8,128)(2,1)S(1)}, bf16[40,1024]{1,0:T(8,128)(2,1)S(1)}, u32[]{:S(2)}, u32[]{:S(2)}) collective-permute-start(bf16[40,1024]{1,0:T(8,128)(2,1)S(1)} %fusion.19), channel_id=1, source_target_pairs={{0,4},{2,6},{4,0},{6,2},{8,12},{10,14},{12,8},{14,10},{1,5},{3,7},... | collective-permute-start | bytes 245768 | tf_op jit(solution)/shard_map/ppermute | solution.py:40
  66.2 15.8 %collective-permute-start.22 = (bf16[4,40,1024]{2,1,0:T(8,128)(2,1)S(1)}, bf16[4,40,1024]{2,1,0:T(8,128)(2,1)S(1)}, u32[]{:S(2)}, u32[]{:S(2)}) collective-permute-start(bf16[4,40,1024]{2,1,0:T(8,128)(2,1)S(1)} %pad_maximum_fusion.refs_4_), channel_id=1, source_target_pairs={{0,2},{2,0},{4,6},{6,4},{8,10},{10,8},{12,14},{14,12},{1,3},{3,1},... | collective-permute-start | bytes 983048 | tf_op jit(solution)/shard_map/ppermute | solution.py:40
  66.8 4.5 %collective-permute-start.16 = (f16[40,1024]{1,0:T(8,128)(2,1)S(1)}, f16[40,1024]{1,0:T(8,128)(2,1)S(1)}, u32[]{:S(2)}, u32[]{:S(2)}) collective-permute-start(f16[40,1024]{1,0:T(8,128)(2,1)S(1)} %get-tuple-element.40), channel_id=1, source_target_pairs={{0,4},{2,6},{4,0},{6,2},{8,12},{10,14},{12,8},{14,10},{1,5},{3,7},... | collective-permute-start | bytes 245768 | tf_op jit(solution)/shard_map/ppermute | solution.py:40
  68.0 9.3 %collective-permute-start.17 = (f16[40,1024]{1,0:T(8,128)(2,1)S(1)}, f16[40,1024]{1,0:T(8,128)(2,1)S(1)}, u32[]{:S(2)}, u32[]{:S(2)}) collective-permute-start(f16[40,1024]{1,0:T(8,128)(2,1)S(1)} %get-tuple-element.41), channel_id=1, source_target_pairs={{0,8},{2,10},{4,12},{6,14},{8,0},{10,2},{12,4},{14,6},{1,9},{3,11}... | collective-permute-start | bytes 245768 | tf_op jit(solution)/shard_map/ppermute | solution.py:40
  70.4 7.2 %collective-permute-start.18 = (f16[40,1024]{1,0:T(8,128)(2,1)S(1)}, f16[40,1024]{1,0:T(8,128)(2,1)S(1)}, u32[]{:S(2)}, u32[]{:S(2)}) collective-permute-start(f16[40,1024]{1,0:T(8,128)(2,1)S(1)} %get-tuple-element.42), channel_id=1, source_target_pairs={{0,12},{2,14},{4,8},{6,10},{8,4},{10,6},{12,0},{14,2},{1,13},{3,15... | collective-permute-start | bytes 245768 | tf_op jit(solution)/shard_map/ppermute | solution.py:40
  77.6 13.4 %collective-permute-start.21 = (bf16[40,1024]{1,0:T(8,128)(2,1)S(1)}, bf16[40,1024]{1,0:T(8,128)(2,1)S(1)}, u32[]{:S(2)}, u32[]{:S(2)}) collective-permute-start(bf16[40,1024]{1,0:T(8,128)(2,1)S(1)} %fusion.12), channel_id=1, source_target_pairs={{0,12},{2,14},{4,8},{6,10},{8,4},{10,6},{12,0},{14,2},{1,13},{3,15... | collective-permute-start | bytes 245768 | tf_op jit(solution)/shard_map/ppermute | solution.py:40
  81.0 10.0 %collective-permute-start.20 = (bf16[40,1024]{1,0:T(8,128)(2,1)S(1)}, bf16[40,1024]{1,0:T(8,128)(2,1)S(1)}, u32[]{:S(2)}, u32[]{:S(2)}) collective-permute-start(bf16[40,1024]{1,0:T(8,128)(2,1)S(1)} %fusion.12), channel_id=1, source_target_pairs={{0,8},{2,10},{4,12},{6,14},{8,0},{10,2},{12,4},{14,6},{1,9},{3,11}... | collective-permute-start | bytes 245768 | tf_op jit(solution)/shard_map/ppermute | solution.py:40
  81.3 9.7 %collective-permute-start.19 = (bf16[40,1024]{1,0:T(8,128)(2,1)S(1)}, bf16[40,1024]{1,0:T(8,128)(2,1)S(1)}, u32[]{:S(2)}, u32[]{:S(2)}) collective-permute-start(bf16[40,1024]{1,0:T(8,128)(2,1)S(1)} %fusion.12), channel_id=1, source_target_pairs={{0,4},{2,6},{4,0},{6,2},{8,12},{10,14},{12,8},{14,10},{1,5},{3,7},... | collective-permute-start | bytes 245768 | tf_op jit(solution)/shard_map/ppermute | solution.py:40
  91.1 7.2 %collective-permute-start.27 = (bf16[4,40,1024]{2,1,0:T(8,128)(2,1)S(1)}, bf16[4,40,1024]{2,1,0:T(8,128)(2,1)S(1)}, u32[]{:S(2)}, u32[]{:S(2)}) collective-permute-start(bf16[4,40,1024]{2,1,0:T(8,128)(2,1)S(1)} %pad_maximum_fusion.1.refs_4_), channel_id=1, source_target_pairs={{0,2},{2,0},{4,6},{6,4},{8,10},{10,8},{12,14},{14,12},{1,3},{3,1},... | collective-permute-start | bytes 983048 | tf_op jit(solution)/shard_map/ppermute | solution.py:40
  93.1 17.2 %collective-permute-start.23 = (bf16[4,64,1152]{2,1,0:T(8,128)(2,1)S(1)}, bf16[4,64,1152]{2,1,0:T(8,128)(2,1)S(1)}, u32[]{:S(2)}, u32[]{:S(2)}) collective-permute-start(bf16[4,64,1152]{2,1,0:T(8,128)(2,1)S(1)} %attend.4), channel_id=1, source_target_pairs={{0,2},{2,0},{4,6},{6,4},{8,10},{10,8},{12,14},{14,12},{1,3},{3,1},... | collective-permute-start | bytes 1769480 | tf_op jit(solution)/shard_map/ppermute | solution.py:40
  107.4 19.3 %collective-permute-start.28 = (bf16[4,64,1152]{2,1,0:T(8,128)(2,1)S(1)}, bf16[4,64,1152]{2,1,0:T(8,128)(2,1)S(1)}, u32[]{:S(2)}, u32[]{:S(2)}) collective-permute-start(bf16[4,64,1152]{2,1,0:T(8,128)(2,1)S(1)} %attend.6), channel_id=1, source_target_pairs={{0,2},{2,0},{4,6},{6,4},{8,10},{10,8},{12,14},{14,12},{1,3},{3,1},... | collective-permute-start | bytes 1769480 | tf_op jit(solution)/shard_map/ppermute | solution.py:40
  121.7 18.2 %collective-permute-start.24 = (bf16[64,1152]{1,0:T(8,128)(2,1)S(1)}, bf16[64,1152]{1,0:T(8,128)(2,1)S(1)}, u32[]{:S(2)}, u32[]{:S(2)}) collective-permute-start(bf16[64,1152]{1,0:T(8,128)(2,1)S(1)} %get-tuple-element.50), channel_id=1, source_target_pairs={{0,4},{2,6},{4,0},{6,2},{8,12},{10,14},{12,8},{14,10},{1,5},{3,7},... | collective-permute-start | bytes 442376 | tf_op jit(solution)/shard_map/ppermute | solution.py:40
  124.3 18.3 %collective-permute-start.25 = (bf16[64,1152]{1,0:T(8,128)(2,1)S(1)}, bf16[64,1152]{1,0:T(8,128)(2,1)S(1)}, u32[]{:S(2)}, u32[]{:S(2)}) collective-permute-start(bf16[64,1152]{1,0:T(8,128)(2,1)S(1)} %get-tuple-element.51), channel_id=1, source_target_pairs={{0,8},{2,10},{4,12},{6,14},{8,0},{10,2},{12,4},{14,6},{1,9},{3,11}... | collective-permute-start | bytes 442376 | tf_op jit(solution)/shard_map/ppermute | solution.py:40
  124.3 18.3 %collective-permute-start.26 = (bf16[64,1152]{1,0:T(8,128)(2,1)S(1)}, bf16[64,1152]{1,0:T(8,128)(2,1)S(1)}, u32[]{:S(2)}, u32[]{:S(2)}) collective-permute-start(bf16[64,1152]{1,0:T(8,128)(2,1)S(1)} %get-tuple-element.52), channel_id=1, source_target_pairs={{0,12},{2,14},{4,8},{6,10},{8,4},{10,6},{12,0},{14,2},{1,13},{3,15... | collective-permute-start | bytes 442376 | tf_op jit(solution)/shard_map/ppermute | solution.py:40
  138.2 5.2 %collective-permute-start.29 = (bf16[64,1152]{1,0:T(8,128)(2,1)S(1)}, bf16[64,1152]{1,0:T(8,128)(2,1)S(1)}, u32[]{:S(2)}, u32[]{:S(2)}) collective-permute-start(bf16[64,1152]{1,0:T(8,128)(2,1)S(1)} %get-tuple-element.54), channel_id=1, source_target_pairs={{0,4},{2,6},{4,0},{6,2},{8,12},{10,14},{12,8},{14,10},{1,5},{3,7},... | collective-permute-start | bytes 442376 | tf_op jit(solution)/shard_map/ppermute | solution.py:40
  139.9 9.0 %collective-permute-start.30 = (bf16[64,1152]{1,0:T(8,128)(2,1)S(1)}, bf16[64,1152]{1,0:T(8,128)(2,1)S(1)}, u32[]{:S(2)}, u32[]{:S(2)}) collective-permute-start(bf16[64,1152]{1,0:T(8,128)(2,1)S(1)} %get-tuple-element.55), channel_id=1, source_target_pairs={{0,8},{2,10},{4,12},{6,14},{8,0},{10,2},{12,4},{14,6},{1,9},{3,11}... | collective-permute-start | bytes 442376 | tf_op jit(solution)/shard_map/ppermute | solution.py:40
  139.9 8.9 %collective-permute-start.31 = (bf16[64,1152]{1,0:T(8,128)(2,1)S(1)}, bf16[64,1152]{1,0:T(8,128)(2,1)S(1)}, u32[]{:S(2)}, u32[]{:S(2)}) collective-permute-start(bf16[64,1152]{1,0:T(8,128)(2,1)S(1)} %get-tuple-element.56), channel_id=1, source_target_pairs={{0,12},{2,14},{4,8},{6,10},{8,4},{10,6},{12,0},{14,2},{1,13},{3,15... | collective-permute-start | bytes 442376 | tf_op jit(solution)/shard_map/ppermute | solution.py:40

commit v3 on v2

--- a/solution.py
+++ b/solution.py
@@ -73,8 +73,70 @@
     )(place, hidden, handed)
 
 
+def fetch_kernel(chunk, width, first, place, prompts, prompt_lengths, cache_ref, *refs):
+    plain = (len(refs) - 3) // 2
+    sources, (kv_ref, *copies), (kv_sem, sem) = refs[:plain], refs[plain:-2], refs[-2:]
+    count, tile_len = kv_ref.shape[:2]
+    section, shard = place[0], place[1]
+    moves = [
+        (None, pltpu.make_async_copy(source, copy, sem.at[i]))
+        for i, (source, copy) in enumerate(zip(sources, copies))
+    ]
+    for p in range(count if first is not None else 0):
+        asked = prompts[section, 0] == p
+        for b in range(1, prompts.shape[1]):
+            asked = asked | (prompts[section, b] == p)
+        for c in range(tile_len // chunk):
+            at = pl.ds(c * chunk, chunk)
+            needed = asked & (prompt_lengths[p] > shard * tile_len + c * chunk)
+            moves.append((needed, pltpu.make_async_copy(
+                cache_ref.at[0, p, at, pl.ds(first * width, width)], kv_ref.at[p, at],
+                kv_sem.at[p, c],
+            )))
+    for needed, move in moves:
+        if needed is None:
+            move.start()
+        else:
+            pl.when(needed)(move.start)
+    for needed, move in moves:
+        if needed is None:
+            move.wait()
+        else:
+            pl.when(needed)(move.wait)
+
+
+def fetch(place, prompts, prompt_lengths, cache, width, first, plain):
+    count, tile_len = cache.shape[1:3]
+    chunk = min(CHUNK, tile_len)
+    shape = (count, tile_len, width) if first is not None else (1, 16, HD)
+    anywhere, near = pl.BlockSpec(memory_space=pltpu.HBM), pl.BlockSpec(memory_space=pltpu.VMEM)
+    size = math.prod(shape) + sum(math.prod(array.shape) for array in plain)
+    return pl.pallas_call(
+        functools.partial(fetch_kernel, chunk, width, first),
+        grid_spec=pltpu.PrefetchScalarGridSpec(
+            num_scalar_prefetch=3,
+            grid=(1,),
+            in_specs=[anywhere] * (1 + len(plain)),
+            out_specs=[near] * (1 + len(plain)),
+            scratch_shapes=[
+                pltpu.SemaphoreType.DMA((count, tile_len // chunk)),
+                pltpu.SemaphoreType.DMA((len(plain) + 1,)),
+            ],
+        ),
+        out_shape=[pltpu.VMEM(shape, cache.dtype)]
+        + [pltpu.VMEM(array.shape, array.dtype) for array in plain],
+        compiler_params=pltpu.CompilerParams(vmem_limit_bytes=4 * MIB),
+        cost_estimate=pl.CostEstimate(flops=0, bytes_accessed=2 * size, transcendentals=0),
+        name="fetch",
+    )(
+        place, prompts, prompt_lengths,
+        *[pltpu.with_memory_space_constraint(array, pltpu.HBM) for array in (cache, *plain)],
+    )
+
+
 def project_kernel(grid, bl, share, place, lengths, *refs):
-    x_refs, (w_ref, out_ref, xp_ref, starts) = refs[:grid.n], refs[grid.n:]
+    x_refs, w_ref, refs = refs[:grid.n], refs[grid.n], refs[grid.n + 1:]
+    out_refs, (xp_ref, starts) = refs[:-2], refs[-2:]
 
     @pl.when(pl.program_id(0) == 0)
     def _():
@@ -100,29 +162,35 @@
         chosen = jnp.dot(pick, x, preferred_element_type=jnp.float32)
         xp_ref[...] = chosen.astype(jnp.bfloat16)
 
-    result = jnp.dot(xp_ref[...], w_ref[...], preferred_element_type=jnp.float32)
-    out_ref[...] = result.reshape(out_ref.shape)
+    result = jnp.dot(xp_ref[...], w_ref[0], preferred_element_type=jnp.float32)
+    rows = grid.zs * share
+    for i, out_ref in enumerate(out_refs):
+        chunk, kx = i // grid.xs, i % grid.xs
+
+        @pl.when(pl.program_id(0) == chunk)
+        def _(out_ref=out_ref, kx=kx):
+            out_ref[...] = result[kx * rows:(kx + 1) * rows]
 
 
 def project(grid, place, lengths, xs, w, bl, share, chunks):
-    k, cols = w.shape
+    k, cols = w.shape[1:]
     rows = grid.n * share
     tile = cols // chunks
-    shape = (chunks, grid.xs, grid.zs * share, tile)
+    piece = (grid.zs * share, tile)
     return pl.pallas_call(
         functools.partial(project_kernel, grid, bl, share),
         grid_spec=pltpu.PrefetchScalarGridSpec(
             num_scalar_prefetch=2,
             grid=(chunks,),
             in_specs=[pl.BlockSpec((bl, k), lambda j, *m: (0, 0))] * grid.n
-            + [pl.BlockSpec((k, tile), lambda j, *m: (0, j))],
-            out_specs=pl.BlockSpec((1,) + shape[1:], lambda j, *m: (j, 0, 0, 0)),
+            + [pl.BlockSpec((1, k, tile), lambda j, *m: (0, 0, j))],
+            out_specs=[pl.BlockSpec(piece, lambda j, *m: (0, 0))] * (chunks * grid.xs),
             scratch_shapes=[
                 pltpu.VMEM((rows, k), jnp.bfloat16), pltpu.SMEM((grid.n,), jnp.int32)
             ],
         ),
-        out_shape=jax.ShapeDtypeStruct(shape, jnp.float32),
-        compiler_params=pltpu.CompilerParams(vmem_limit_bytes=32 * MIB),
+        out_shape=[jax.ShapeDtypeStruct(piece, jnp.float32)] * (chunks * grid.xs),
+        compiler_params=pltpu.CompilerParams(vmem_limit_bytes=20 * MIB),
         cost_estimate=pl.CostEstimate(
             flops=2 * rows * k * cols, bytes_accessed=2 * k * cols + 4 * rows * cols,
             transcendentals=0,
@@ -170,7 +238,7 @@
     refs = refs[4:]
     near_ref, refs = refs[0], refs[1:]
     far_refs, refs = refs[:grid.xs - 1], refs[grid.xs - 1:]
-    kv_refs, refs = refs[:heads], refs[heads:]
+    kv_ref, refs = refs[0], refs[1:]
     own_ref, refs = refs[0], refs[1:]
     met = grid.xs - 1 if kx == 0 else 0
     met_refs, refs = refs[:met], refs[met:]
@@ -185,9 +253,8 @@
     offset = jnp.int32(0)
     for b in range(grid.n):
         offset = offset + jnp.where(b < block, lengths[section, b], 0)
-    valid = jnp.clip(
-        prompt_lengths[prompts[section, block]] - shard * tile_len, 0, tile_len
-    )
+    prompt = prompts[section, block]
+    valid = jnp.clip(prompt_lengths[prompt] - shard * tile_len, 0, tile_len)
     c2 = LOG2E / math.sqrt(HD)
     chunk = min(CHUNK, tile_len)
     width = heads * GR * HD
@@ -218,10 +285,10 @@
         return jnp.dot(p, with_ones(v), preferred_element_type=jnp.float32)
 
     def keys(g, at, size):
-        return kv_refs[g][0, 0, pl.ds(at, size), :HD]
+        return kv_ref[prompt, pl.ds(at, size), pl.ds(g * 2 * HD, HD)]
 
     def vals(g, at, size):
-        return kv_refs[g][0, 0, pl.ds(at, size), HD:]
+        return kv_ref[prompt, pl.ds(at, size), pl.ds(g * 2 * HD + HD, HD)]
 
     def put(g, used, acc, m):
         m = jnp.broadcast_to(m, (GR * used, HD))
@@ -310,10 +377,10 @@
         def _():
             for g in range(heads):
                 base = g * 2 * HD
-                s = dot_nt(group(g, bl), own_ref[:, base:base + HD])
+                s = dot_nt(group(g, bl), own_ref[0, :, base:base + HD])
                 row = lax.broadcasted_iota(jnp.int32, s.shape, 0) % bl
                 col = lax.broadcasted_iota(jnp.int32, s.shape, 1)
-                update(g, s, col <= row, own_ref[:, base + HD:base + 2 * HD])
+                update(g, s, col <= row, own_ref[0, :, base + HD:base + 2 * HD])
 
     lane = lax.broadcasted_iota(jnp.int32, (bl, EXTRA), 1)
     lse_tile = jnp.zeros((bl, EXTRA), jnp.float32)
@@ -356,21 +423,9 @@
 def attend(grid, kx, place, lengths, prompts, prompt_lengths, near, fars, cache, own, mets, first,
            heads):
     zs, share, cols = near.shape
-    bl = own.shape[0]
-    tile_len = cache.shape[2]
+    bl = own.shape[1]
+    tile_len = cache.shape[1]
     width = heads * GR * HD + EXTRA
-
-    def cache_at(head):
-        def index(i, place, lengths, prompts, prompt_lengths):
-            section, shard = place[0], place[1]
-            at = prompts[section, grid.owner(shard, kx, 0)]
-            for kz in range(1, zs):
-                prompt = prompts[section, grid.owner(shard, kx, kz)]
-                here = (kz <= i) & (prompt_lengths[prompt] > shard * tile_len)
-                at = jnp.where(here, prompt, at)
-            return (0, at, 0, first + head)
-
-        return pl.BlockSpec((1, 1, tile_len, 2 * HD), index)
 
     piece = jax.ShapeDtypeStruct((bl, width), jnp.bfloat16)
     if kx == 0:
@@ -385,8 +440,8 @@
             num_scalar_prefetch=4,
             grid=(zs,),
             in_specs=[pl.BlockSpec((zs, share, cols), lambda i, *m: (0, 0, 0))] * grid.xs
-            + [cache_at(head) for head in range(heads)]
-            + [pl.BlockSpec((bl, heads * 2 * HD), lambda i, *m: (0, first // heads))]
+            + [pl.BlockSpec(memory_space=pltpu.VMEM)]
+            + [pl.BlockSpec((1, bl, heads * 2 * HD), lambda i, *m: (0, 0, first // heads))]
             + [pl.BlockSpec((1, bl, width), lambda i, *m: (i, 0, 0))] * len(mets),
             out_specs=out_specs,
             scratch_shapes=[
@@ -396,14 +451,14 @@
             ],
         ),
         out_shape=out_shape,
-        compiler_params=pltpu.CompilerParams(vmem_limit_bytes=40 * MIB),
+        compiler_params=pltpu.CompilerParams(vmem_limit_bytes=20 * MIB),
         cost_estimate=pl.CostEstimate(
             flops=8 * zs * bl * cols * tile_len,
             bytes_accessed=2 * zs * tile_len * heads * 2 * HD,
             transcendentals=zs * bl * heads * GR * tile_len,
         ),
         name="attend",
-    )(place, lengths, prompts, prompt_lengths, near, *fars, *([cache] * heads), own, *mets)
+    )(place, lengths, prompts, prompt_lengths, near, *fars, cache, own, *mets)
 
 
 def finish_kernel(chunks, zs, heads, bl, place, lengths, *refs):
@@ -458,12 +513,27 @@
     place = jnp.stack([lax.axis_index("sec"), lax.axis_index("seq")]).astype(jnp.int32)
     prompts = block_prompts[:, :, 0]
 
+    def after(value, done):
+        return lax.optimization_barrier((value, done))[0]
+
+    def fetched(first, plain):
+        out = fetch(
+            place, prompts, prompt_lengths, prompt_cache, heads * 2 * HD, first, plain
+        )
+        return [pltpu.with_memory_space_constraint(array, pltpu.VMEM) for array in out]
+
     handed = lax.ppermute(carried, "sec", [(0, 1)])
+    _, hidden, weight, own = fetched(None, [hidden_rows, query_weight, response_cache])
     depth = query_weight.shape[1]
-    slices = split(grid, place, hidden_rows, handed, depth)
+    if depth % HD:
+        hidden = hidden_rows
+    slices = split(grid, place, hidden, handed, depth)
     x = [grid.swap(piece, k // grid.zs, k % grid.zs) if k else piece for k, piece in enumerate(slices)]
-    part = project(grid, place, response_lengths, x, query_weight[0], bl, share, chunks)
-    part = part.reshape(chunks, grid.xs, grid.zs, share, part_cols)
+    caches = [fetched(0, [])[0]]
+    x[0] = after(x[0], caches[0])
+    part = project(grid, place, response_lengths, x, weight, bl, share, chunks)
+    part = [piece.reshape(grid.zs, share, part_cols) for piece in part]
+    part = [part[c * grid.xs:(c + 1) * grid.xs] for c in range(chunks)]
 
     def narrow(value):
         return (value * 0.125).astype(jnp.float16)
@@ -471,11 +541,8 @@
     def widen(value):
         return value.astype(jnp.float32) * 8.0
 
-    def after(value, done):
-        return lax.optimization_barrier((value, done))[0]
-
     def sum_x(c, done):
-        parts = [part[c, kx] for kx in range(grid.xs)]
+        parts = part[c]
         got = [grid.swap(after(narrow(parts[kx]), done), kx, 0) for kx in range(1, grid.xs)]
         return functools.reduce(jnp.add, [parts[0]] + [widen(value) for value in got]), got
 
@@ -493,11 +560,14 @@
     def call(c, kx, queries, mets):
         return attend(
             grid, kx, place, response_lengths, prompts, prompt_lengths, queries[0], queries[1:],
-            prompt_cache, response_cache[0], mets, c * heads, heads,
+            caches[c], own, mets, c * heads, heads,
         )
 
     queries = [None] * chunks
     sent = [[] for _ in range(chunks)]
+    if chunks > 1:
+        caches.append(fetched(1, [])[0])
+        part[0][0] = after(part[0][0], caches[1])
     held, got = sum_x(0, ())
     mine = sum_z(held, ())
     column = gather_z(mine)

time: 151 us -> 139 us (0.921)
  waiting for transfers between devices: 47 us -> 32.3 us
  Pallas kernels: 46.4 us -> 55.6 us
  starting transfers between devices: 53.5 us -> 49.1 us
  local copies, waits for them, and re-layouts: 3.52 us -> 1.34 us
    pallas_call x0 -> x3, Pallas kernels: none -> 15.2 us  [fetch(): pl.pallas_call(functools.partial(fetch_kernel, chunk, width, first), grid...]
    ppermute x31, waiting for transfers between devices: 45.2 us -> 32.3 us  [swap(): return lax.ppermute(value, 'seq', pairs)]
    pallas_call x4, Pallas kernels: 40.7 us -> 34.5 us  [attend(): pl.pallas_call(functools.partial(attend_kernel, grid, kx, bl, share, head...]
    ppermute x31, starting transfers between devices: 51.1 us -> 46.7 us  [swap(): return lax.ppermute(value, 'seq', pairs)]
    unnamed x14 -> x10, local copies, waits for them, and re-layouts: 3.52 us -> 1.34 us
    ppermute x1, waiting for transfers between devices: 1.79 us -> 0.01 us  [shards(): handed = lax.ppermute(carried, 'sec', [(0, 1)])]
  transfers between devices with their start and end apart: 32 -> 32, of which waited for: 17 -> 11; matrix products, arithmetic and copies ran while one was open for 0% -> 0% of each run, Pallas kernels for 27% -> 36%
where the time goes in v3:
time: 139 us
  Pallas kernels  55.6 us (40%)
  starting transfers between devices  49.1 us (35%)
  waiting for transfers between devices  32.3 us (23%)
    ppermute x31, starting transfers between devices, swap(): return lax.ppermute(value, 'seq', pairs)  46.7 us
    pallas_call x4, Pallas kernels, attend(): pl.pallas_call(functools.partial(attend_kernel, grid, kx, bl, share, head...  34.5 us
    ppermute x31, waiting for transfers between devices, swap(): return lax.ppermute(value, 'seq', pairs)  32.3 us
    pallas_call x3, Pallas kernels, fetch(): pl.pallas_call(functools.partial(fetch_kernel, chunk, width, first), grid...  15.2 us
  transfers between devices with their start and end apart: 32, of which 11 were waited for; matrix products, arithmetic and copies ran while one was open for 0% of the time, Pallas kernels for 36%

profile of v3, /device:TPU:0, one launch (start us, length us, event | category | flops | bytes accessed | tf_op | source)
XLA Modules:
  0.0 139.4 jit_solution(9337628081627075462)
XLA Ops:
  0.0 2.4 %collective-permute-start = (bf16[1,64,5120]{2,1,0:T(8,128)(2,1)}, bf16[1,64,5120]{2,1,0:T(8,128)(2,1)S(1)}, u32[]{:S(2)}, u32[]{:S(2)}) collective-permute-start(bf16[1,64,5120]{2,1,0:T(8,128)(2,1)} %param.9), channel_id=1, source_target_pairs={{0,16},{1,17},{2,18},{3,19},{4,20},{5,21},{6,22},{7,23},{8,24},{9,... | collective-permute-start | bytes 1966088 | tf_op jit(solution)/shard_map/ppermute | solution.py:525
  2.4 0.1 pad_add_fusion.place.refs_0_
  2.5 0.7 copy-done
  3.2 0.7 copy-done.3
  3.8 3.4 %fetch.3 = (bf16[1,16,128]{2,1,0:T(8,128)(2,1)}, bf16[1,64,5120]{2,1,0:T(8,128)(2,1)S(1)}, bf16[1,640,2048]{2,1,0:T(8,128)(2,1)S(1)}, bf16[1,64,1024]{2,1,0:T(8,128)(2,1)S(1)}) custom-call(s32[2]{0:T(128)S(1)} %pad_add_fusion.place.refs_0_, s32[2,8]{1,0:T(2,128)S(1)} %bitcast.49, s32[8]{0:T(128)S(1)} %copy-done.3, bf16[1,8,2048,1024]{3,2,1,0:T(8,128)(2,1)} %cache_ref.5, ...), custom_call_target="tpu_custom_call" | custom-call | bytes 3411968 | tf_op jit(solution)/shard_map/fetch/pallas_call | solution.py:114
  7.3 0.7 split.1
  8.0 2.5 %collective-permute-start.1 = (bf16[64,640]{1,0:T(8,128)(2,1)S(1)}, bf16[64,640]{1,0:T(8,128)(2,1)S(1)}, u32[]{:S(2)}, u32[]{:S(2)}) collective-permute-start(bf16[64,640]{1,0:T(8,128)(2,1)S(1)} %get-tuple-element.43), channel_id=1, source_target_pairs={{0,4},{2,6},{4,0},{6,2},{8,12},{10,14},{12,8},{14,10},{1,5},{3,7},... | collective-permute-start | bytes 245768 | tf_op jit(solution)/shard_map/ppermute | solution.py:40
  10.4 2.6 %collective-permute-start.2 = (bf16[64,640]{1,0:T(8,128)(2,1)S(1)}, bf16[64,640]{1,0:T(8,128)(2,1)S(1)}, u32[]{:S(2)}, u32[]{:S(2)}) collective-permute-start(bf16[64,640]{1,0:T(8,128)(2,1)S(1)} %get-tuple-element.44), channel_id=1, source_target_pairs={{0,8},{2,10},{4,12},{6,14},{8,0},{10,2},{12,4},{14,6},{1,9},{3,11}... | collective-permute-start | bytes 245768 | tf_op jit(solution)/shard_map/ppermute | solution.py:40
  13.0 1.7 %collective-permute-start.4 = (bf16[64,640]{1,0:T(8,128)(2,1)S(1)}, bf16[64,640]{1,0:T(8,128)(2,1)S(1)}, u32[]{:S(2)}, u32[]{:S(2)}) collective-permute-start(bf16[64,640]{1,0:T(8,128)(2,1)S(1)} %get-tuple-element.46), channel_id=1, source_target_pairs={{0,2},{2,0},{4,6},{6,4},{8,10},{10,8},{12,14},{14,12},{1,3},{3,1},... | collective-permute-start | bytes 245768 | tf_op jit(solution)/shard_map/ppermute | solution.py:40
  14.7 0.6 collective-permute-start.5
  15.4 4.4 %collective-permute-start.6 = (bf16[64,640]{1,0:T(8,128)(2,1)S(1)}, bf16[64,640]{1,0:T(8,128)(2,1)S(1)}, u32[]{:S(2)}, u32[]{:S(2)}) collective-permute-start(bf16[64,640]{1,0:T(8,128)(2,1)S(1)} %get-tuple-element.48), channel_id=1, source_target_pairs={{0,10},{2,8},{4,14},{6,12},{8,2},{10,0},{12,6},{14,4},{1,11},{3,9}... | collective-permute-start | bytes 245768 | tf_op jit(solution)/shard_map/ppermute | solution.py:40
  19.8 4.9 %collective-permute-start.7 = (bf16[64,640]{1,0:T(8,128)(2,1)S(1)}, bf16[64,640]{1,0:T(8,128)(2,1)S(1)}, u32[]{:S(2)}, u32[]{:S(2)}) collective-permute-start(bf16[64,640]{1,0:T(8,128)(2,1)S(1)} %get-tuple-element.49), channel_id=1, source_target_pairs={{0,14},{2,12},{4,10},{6,8},{8,6},{10,4},{12,2},{14,0},{1,15},{3,13... | collective-permute-start | bytes 245768 | tf_op jit(solution)/shard_map/ppermute | solution.py:40
  24.8 5.9 %fetch.4.refs_6_ = bf16[8,2048,512]{2,1,0:T(8,128)(2,1)S(1)} custom-call(s32[2]{0:T(128)S(1)} %pad_add_fusion.place.refs_0_, s32[2,8]{1,0:T(2,128)S(1)} %bitcast.50, s32[8]{0:T(128)S(1)} %copy-done.4, bf16[1,8,2048,1024]{3,2,1,0:T(8,128)(2,1)} %cache_ref.5), custom_call_target="tpu_custom_call" | custom-call | bytes 16777216 | tf_op jit(solution)/shard_map/fetch/pallas_call | solution.py:114
  30.7 2.7 %project.1 = (f32[160,1024]{1,0:T(8,128)S(1)}, f32[160,1024]{1,0:T(8,128)S(1)}, f32[160,1024]{1,0:T(8,128)S(1)}, f32[160,1024]{1,0:T(8,128)S(1)}) custom-call(s32[2]{0:T(128)S(1)} %pad_add_fusion.place.refs_0_, s32[2,8]{1,0:T(2,128)S(1)} %copy-done.2, bf16[64,640]{1,0:T(8,128)(2,1)S(1)} %get-tuple-element.42.refs_0_, ...), custom_call_target="tpu_custom_call" | custom-call | flops 838860800 | bytes 5242880 | tf_op jit(solution)/shard_map/project/pallas_call | solution.py:180
  33.5 0.1 collective-permute-start.8
  33.6 5.9 %fetch.5.refs_6_ = bf16[8,2048,512]{2,1,0:T(8,128)(2,1)S(1)} custom-call(s32[2]{0:T(128)S(1)} %pad_add_fusion.place.refs_0_, s32[2,8]{1,0:T(2,128)S(1)} %bitcast.51, s32[8]{0:T(128)S(1)} %copy-done.4, bf16[1,8,2048,1024]{3,2,1,0:T(8,128)(2,1)} %cache_ref.5), custom_call_target="tpu_custom_call" | custom-call | bytes 16777216 | tf_op jit(solution)/shard_map/fetch/pallas_call | solution.py:114
  39.5 2.1 %collective-permute-done.8 = f16[4,40,1024]{2,1,0:T(8,128)(2,1)S(1)} collective-permute-done((f16[4,40,1024]{2,1,0:T(8,128)(2,1)S(1)}, f16[4,40,1024]{2,1,0:T(8,128)(2,1)S(1)}, u32[]{:S(2)}, u32[]{:S(2)}) %collective-permute-start.8) | collective-permute-done | bytes 327712 | tf_op jit(solution)/shard_map/ppermute | solution.py:40
  41.6 0.1 multiply_add_fusion.1
  41.8 0.1 collective-permute-start.11
  41.9 0.1 collective-permute-start.10
  41.9 4.3 %collective-permute-start.9 = (f16[40,1024]{1,0:T(8,128)(2,1)S(1)}, f16[40,1024]{1,0:T(8,128)(2,1)S(1)}, u32[]{:S(2)}, u32[]{:S(2)}) collective-permute-start(f16[40,1024]{1,0:T(8,128)(2,1)S(1)} %get-tuple-element.78), channel_id=1, source_target_pairs={{0,4},{2,6},{4,0},{6,2},{8,12},{10,14},{12,8},{14,10},{1,5},{3,7},... | collective-permute-start | bytes 245768 | tf_op jit(solution)/shard_map/ppermute | solution.py:40
  46.4 2.3 %collective-permute-done.11 = f16[40,1024]{1,0:T(8,128)(2,1)S(1)} collective-permute-done((f16[40,1024]{1,0:T(8,128)(2,1)S(1)}, f16[40,1024]{1,0:T(8,128)(2,1)S(1)}, u32[]{:S(2)}, u32[]{:S(2)}) %collective-permute-start.11) | collective-permute-done | bytes 81952 | tf_op jit(solution)/shard_map/ppermute | solution.py:40
  48.7 2.0 %collective-permute-done.10 = f16[40,1024]{1,0:T(8,128)(2,1)S(1)} collective-permute-done((f16[40,1024]{1,0:T(8,128)(2,1)S(1)}, f16[40,1024]{1,0:T(8,128)(2,1)S(1)}, u32[]{:S(2)}, u32[]{:S(2)}) %collective-permute-start.10) | collective-permute-done | bytes 81952 | tf_op jit(solution)/shard_map/ppermute | solution.py:40
  50.8 1.9 %collective-permute-start.14 = (bf16[40,1024]{1,0:T(8,128)(2,1)S(1)}, bf16[40,1024]{1,0:T(8,128)(2,1)S(1)}, u32[]{:S(2)}, u32[]{:S(2)}) collective-permute-start(bf16[40,1024]{1,0:T(8,128)(2,1)S(1)} %fusion.13), channel_id=1, source_target_pairs={{0,12},{2,14},{4,8},{6,10},{8,4},{10,6},{12,0},{14,2},{1,13},{3,15... | collective-permute-start | bytes 245768 | tf_op jit(solution)/shard_map/ppermute | solution.py:40
  52.6 2.6 %collective-permute-start.12 = (bf16[40,1024]{1,0:T(8,128)(2,1)S(1)}, bf16[40,1024]{1,0:T(8,128)(2,1)S(1)}, u32[]{:S(2)}, u32[]{:S(2)}) collective-permute-start(bf16[40,1024]{1,0:T(8,128)(2,1)S(1)} %fusion.13), channel_id=1, source_target_pairs={{0,4},{2,6},{4,0},{6,2},{8,12},{10,14},{12,8},{14,10},{1,5},{3,7},... | collective-permute-start | bytes 245768 | tf_op jit(solution)/shard_map/ppermute | solution.py:40
  55.2 2.8 %collective-permute-done.14 = bf16[40,1024]{1,0:T(8,128)(2,1)S(1)} collective-permute-done((bf16[40,1024]{1,0:T(8,128)(2,1)S(1)}, bf16[40,1024]{1,0:T(8,128)(2,1)S(1)}, u32[]{:S(2)}, u32[]{:S(2)}) %collective-permute-start.14) | collective-permute-done | bytes 81952 | tf_op jit(solution)/shard_map/ppermute | solution.py:40
  58.0 3.2 %collective-permute-done.13 = bf16[40,1024]{1,0:T(8,128)(2,1)S(1)} collective-permute-done((bf16[40,1024]{1,0:T(8,128)(2,1)S(1)}, bf16[40,1024]{1,0:T(8,128)(2,1)S(1)}, u32[]{:S(2)}, u32[]{:S(2)}) %collective-permute-start.13) | collective-permute-done | bytes 81952 | tf_op jit(solution)/shard_map/ppermute | solution.py:40
  61.3 1.0 collective-permute-start.22
  62.3 0.1 multiply_add_fusion
  62.4 2.0 %collective-permute-start.18 = (f16[40,1024]{1,0:T(8,128)(2,1)S(1)}, f16[40,1024]{1,0:T(8,128)(2,1)S(1)}, u32[]{:S(2)}, u32[]{:S(2)}) collective-permute-start(f16[40,1024]{1,0:T(8,128)(2,1)S(1)} %get-tuple-element.59), channel_id=1, source_target_pairs={{0,12},{2,14},{4,8},{6,10},{8,4},{10,6},{12,0},{14,2},{1,13},{3,15... | collective-permute-start | bytes 245768 | tf_op jit(solution)/shard_map/ppermute | solution.py:40
  64.4 2.5 %collective-permute-start.16 = (f16[40,1024]{1,0:T(8,128)(2,1)S(1)}, f16[40,1024]{1,0:T(8,128)(2,1)S(1)}, u32[]{:S(2)}, u32[]{:S(2)}) collective-permute-start(f16[40,1024]{1,0:T(8,128)(2,1)S(1)} %get-tuple-element.57), channel_id=1, source_target_pairs={{0,4},{2,6},{4,0},{6,2},{8,12},{10,14},{12,8},{14,10},{1,5},{3,7},... | collective-permute-start | bytes 245768 | tf_op jit(solution)/shard_map/ppermute | solution.py:40
  66.9 2.7 %collective-permute-done.18 = f16[40,1024]{1,0:T(8,128)(2,1)S(1)} collective-permute-done((f16[40,1024]{1,0:T(8,128)(2,1)S(1)}, f16[40,1024]{1,0:T(8,128)(2,1)S(1)}, u32[]{:S(2)}, u32[]{:S(2)}) %collective-permute-start.18) | collective-permute-done | bytes 81952 | tf_op jit(solution)/shard_map/ppermute | solution.py:40
  69.6 2.4 %collective-permute-done.17 = f16[40,1024]{1,0:T(8,128)(2,1)S(1)} collective-permute-done((f16[40,1024]{1,0:T(8,128)(2,1)S(1)}, f16[40,1024]{1,0:T(8,128)(2,1)S(1)}, u32[]{:S(2)}, u32[]{:S(2)}) %collective-permute-start.17) | collective-permute-done | bytes 81952 | tf_op jit(solution)/shard_map/ppermute | solution.py:40
  72.1 0.1 collective-permute-start.19
  72.2 2.4 %collective-permute-start.20 = (bf16[40,1024]{1,0:T(8,128)(2,1)S(1)}, bf16[40,1024]{1,0:T(8,128)(2,1)S(1)}, u32[]{:S(2)}, u32[]{:S(2)}) collective-permute-start(bf16[40,1024]{1,0:T(8,128)(2,1)S(1)} %fusion.6), channel_id=1, source_target_pairs={{0,8},{2,10},{4,12},{6,14},{8,0},{10,2},{12,4},{14,6},{1,9},{3,11}... | collective-permute-start | bytes 245768 | tf_op jit(solution)/shard_map/ppermute | solution.py:40
  74.5 2.0 %collective-permute-start.21 = (bf16[40,1024]{1,0:T(8,128)(2,1)S(1)}, bf16[40,1024]{1,0:T(8,128)(2,1)S(1)}, u32[]{:S(2)}, u32[]{:S(2)}) collective-permute-start(bf16[40,1024]{1,0:T(8,128)(2,1)S(1)} %fusion.6), channel_id=1, source_target_pairs={{0,12},{2,14},{4,8},{6,10},{8,4},{10,6},{12,0},{14,2},{1,13},{3,15... | collective-permute-start | bytes 245768 | tf_op jit(solution)/shard_map/ppermute | solution.py:40
  76.5 7.6 %attend.4 = bf16[4,64,1152]{2,1,0:T(8,128)(2,1)S(1)} custom-call(s32[2]{0:T(128)S(1)} %pad_add_fusion.place.refs_0_, s32[2,8]{1,0:T(2,128)S(1)} %copy-done.2, s32[2,8]{1,0:T(2,128)S(1)} %bitcast.52, s32[8]{0:T(128)S(1)} %copy-done.4, bf16[4,40,1024]{2,1,0:T(8,128)(2,1)S(1)} %pad_maximum_fusion.refs_4_, ...), custom_call_target="tpu_custom_call" | custom-call | flops 4294967296 | bytes 8388608 | tf_op jit(solution)/shard_map/attend/pallas_call | solution.py:437
  84.3 2.0 %collective-permute-start.23 = (bf16[4,64,1152]{2,1,0:T(8,128)(2,1)S(1)}, bf16[4,64,1152]{2,1,0:T(8,128)(2,1)S(1)}, u32[]{:S(2)}, u32[]{:S(2)}) collective-permute-start(bf16[4,64,1152]{2,1,0:T(8,128)(2,1)S(1)} %attend.4), channel_id=1, source_target_pairs={{0,2},{2,0},{4,6},{6,4},{8,10},{10,8},{12,14},{14,12},{1,3},{3,1},... | collective-permute-start | bytes 1769480 | tf_op jit(solution)/shard_map/ppermute | solution.py:40
  86.3 8.1 %collective-permute-done.27.refs_5_ = bf16[4,40,1024]{2,1,0:T(8,128)(2,1)S(1)} collective-permute-done((bf16[4,40,1024]{2,1,0:T(8,128)(2,1)S(1)}, bf16[4,40,1024]{2,1,0:T(8,128)(2,1)S(1)}, u32[]{:S(2)}, u32[]{:S(2)}) %collective-permute-start.27) | collective-permute-done | bytes 327712 | tf_op jit(solution)/shard_map/ppermute | solution.py:40
  94.5 7.8 %attend.6 = bf16[4,64,1152]{2,1,0:T(8,128)(2,1)S(1)} custom-call(s32[2]{0:T(128)S(1)} %pad_add_fusion.place.refs_0_, s32[2,8]{1,0:T(2,128)S(1)} %copy-done.2, s32[2,8]{1,0:T(2,128)S(1)} %bitcast.53, s32[8]{0:T(128)S(1)} %copy-done.4, bf16[4,40,1024]{2,1,0:T(8,128)(2,1)S(1)} %pad_maximum_fusion.1.refs_4_, ...), custom_call_target="tpu_custom_call" | custom-call | flops 4294967296 | bytes 8388608 | tf_op jit(solution)/shard_map/attend/pallas_call | solution.py:437
  102.3 1.7 %collective-permute-done.23.refs_8_ = bf16[4,64,1152]{2,1,0:T(8,128)(2,1)S(1)} collective-permute-done((bf16[4,64,1152]{2,1,0:T(8,128)(2,1)S(1)}, bf16[4,64,1152]{2,1,0:T(8,128)(2,1)S(1)}, u32[]{:S(2)}, u32[]{:S(2)}) %collective-permute-start.23) | collective-permute-done | bytes 589856 | tf_op jit(solution)/shard_map/ppermute | solution.py:40
  104.0 9.6 %attend.5 = (bf16[64,1152]{1,0:T(8,128)(2,1)S(1)}, bf16[64,1152]{1,0:T(8,128)(2,1)S(1)}, bf16[64,1152]{1,0:T(8,128)(2,1)S(1)}, bf16[64,1152]{1,0:T(8,128)(2,1)S(1)}) custom-call(s32[2]{0:T(128)S(1)} %pad_add_fusion.place.refs_0_, s32[2,8]{1,0:T(2,128)S(1)} %copy-done.2, s32[2,8]{1,0:T(2,128)S(1)} %bitcast.54, s32[8]{0:T(128)S(1)} %copy-done.4, ...), custom_call_target="tpu_custom_call" | custom-call | flops 4294967296 | bytes 8388608 | tf_op jit(solution)/shard_map/attend/pallas_call | solution.py:437
  113.7 4.3 %collective-permute-start.26 = (bf16[64,1152]{1,0:T(8,128)(2,1)S(1)}, bf16[64,1152]{1,0:T(8,128)(2,1)S(1)}, u32[]{:S(2)}, u32[]{:S(2)}) collective-permute-start(bf16[64,1152]{1,0:T(8,128)(2,1)S(1)} %get-tuple-element.70), channel_id=1, source_target_pairs={{0,12},{2,14},{4,8},{6,10},{8,4},{10,6},{12,0},{14,2},{1,13},{3,15... | collective-permute-start | bytes 442376 | tf_op jit(solution)/shard_map/ppermute | solution.py:40
  118.0 9.6 %attend.7 = (bf16[64,1152]{1,0:T(8,128)(2,1)S(1)}, bf16[64,1152]{1,0:T(8,128)(2,1)S(1)}, bf16[64,1152]{1,0:T(8,128)(2,1)S(1)}, bf16[64,1152]{1,0:T(8,128)(2,1)S(1)}) custom-call(s32[2]{0:T(128)S(1)} %pad_add_fusion.place.refs_0_, s32[2,8]{1,0:T(2,128)S(1)} %copy-done.2, s32[2,8]{1,0:T(2,128)S(1)} %bitcast.55, s32[8]{0:T(128)S(1)} %copy-done.4, ...), custom_call_target="tpu_custom_call" | custom-call | flops 4294967296 | bytes 8388608 | tf_op jit(solution)/shard_map/attend/pallas_call | solution.py:437
  127.8 4.3 %collective-permute-start.31 = (bf16[64,1152]{1,0:T(8,128)(2,1)S(1)}, bf16[64,1152]{1,0:T(8,128)(2,1)S(1)}, u32[]{:S(2)}, u32[]{:S(2)}) collective-permute-start(bf16[64,1152]{1,0:T(8,128)(2,1)S(1)} %get-tuple-element.74), channel_id=1, source_target_pairs={{0,12},{2,14},{4,8},{6,10},{8,4},{10,6},{12,0},{14,2},{1,13},{3,15... | collective-permute-start | bytes 442376 | tf_op jit(solution)/shard_map/ppermute | solution.py:40
  132.1 2.2 %collective-permute-done.29.refs_5_ = bf16[64,1152]{1,0:T(8,128)(2,1)S(1)} collective-permute-done((bf16[64,1152]{1,0:T(8,128)(2,1)S(1)}, bf16[64,1152]{1,0:T(8,128)(2,1)S(1)}, u32[]{:S(2)}, u32[]{:S(2)}) %collective-permute-start.29) | collective-permute-done | bytes 147488 | tf_op jit(solution)/shard_map/ppermute | solution.py:40
  134.3 2.7 %collective-permute-done.30.refs_6_ = bf16[64,1152]{1,0:T(8,128)(2,1)S(1)} collective-permute-done((bf16[64,1152]{1,0:T(8,128)(2,1)S(1)}, bf16[64,1152]{1,0:T(8,128)(2,1)S(1)}, u32[]{:S(2)}, u32[]{:S(2)}) %collective-permute-start.30) | collective-permute-done | bytes 147488 | tf_op jit(solution)/shard_map/ppermute | solution.py:40
  137.0 2.4 %finish.1 = bf16[1,64,2048]{2,1,0:T(8,128)(2,1)} custom-call(s32[2]{0:T(128)S(1)} %pad_add_fusion.place.refs_0_, s32[2,8]{1,0:T(2,128)S(1)} %copy-done.2, bf16[64,1152]{1,0:T(8,128)(2,1)S(1)} %get-tuple-element.67.refs_0_, bf16[64,1152]{1,0:T(8,128)(2,1)S(1)} %collective-permute-done.24.refs_1_, bf16[64,1152]{1,0:T(8,128)(2,1)S(1)} %collective-permute-done.25.refs_2_, ...), custom_call_target="tpu_custom_call" | custom-call | tf_op jit(solution)/shard_map/finish/pallas_call | solution.py:482
  (47 shorter events, 1.0 us)
Async XLA Ops:
  0.0 7.2 %collective-permute-start = (bf16[1,64,5120]{2,1,0:T(8,128)(2,1)}, bf16[1,64,5120]{2,1,0:T(8,128)(2,1)S(1)}, u32[]{:S(2)}, u32[]{:S(2)}) collective-permute-start(bf16[1,64,5120]{2,1,0:T(8,128)(2,1)} %param.9), channel_id=1, source_target_pairs={{0,16},{1,17},{2,18},{3,19},{4,20},{5,21},{6,22},{7,23},{8,24},{9,... | collective-permute-start | bytes 1966088 | tf_op jit(solution)/shard_map/ppermute | solution.py:525
  2.5 0.7 copy-start
  3.2 0.7 copy-start.3
  3.8 20.9 %copy-start.1 = (s32[2,8,1]{1,2,0:T(1,128)S(1)}, s32[2,8,1]{1,2,0:T(1,128)}, u32[]{:S(2)}) copy-start(s32[2,8,1]{1,2,0:T(1,128)} %param.15) | copy-start | bytes 196
  3.8 20.9 %copy-start.4 = (s32[8]{0:T(128)S(1)}, s32[8]{0:T(128)}, u32[]{:S(2)}) copy-start(s32[8]{0:T(128)} %refs_3_.7) | copy-start | bytes 100
  8.0 7.4 %collective-permute-start.1 = (bf16[64,640]{1,0:T(8,128)(2,1)S(1)}, bf16[64,640]{1,0:T(8,128)(2,1)S(1)}, u32[]{:S(2)}, u32[]{:S(2)}) collective-permute-start(bf16[64,640]{1,0:T(8,128)(2,1)S(1)} %get-tuple-element.43), channel_id=1, source_target_pairs={{0,4},{2,6},{4,0},{6,2},{8,12},{10,14},{12,8},{14,10},{1,5},{3,7},... | collective-permute-start | bytes 245768 | tf_op jit(solution)/shard_map/ppermute | solution.py:40
  10.4 9.4 %collective-permute-start.2 = (bf16[64,640]{1,0:T(8,128)(2,1)S(1)}, bf16[64,640]{1,0:T(8,128)(2,1)S(1)}, u32[]{:S(2)}, u32[]{:S(2)}) collective-permute-start(bf16[64,640]{1,0:T(8,128)(2,1)S(1)} %get-tuple-element.44), channel_id=1, source_target_pairs={{0,8},{2,10},{4,12},{6,14},{8,0},{10,2},{12,4},{14,6},{1,9},{3,11}... | collective-permute-start | bytes 245768 | tf_op jit(solution)/shard_map/ppermute | solution.py:40
  13.0 17.6 %collective-permute-start.3 = (bf16[64,640]{1,0:T(8,128)(2,1)S(1)}, bf16[64,640]{1,0:T(8,128)(2,1)S(1)}, u32[]{:S(2)}, u32[]{:S(2)}) collective-permute-start(bf16[64,640]{1,0:T(8,128)(2,1)S(1)} %get-tuple-element.45), channel_id=1, source_target_pairs={{0,12},{2,14},{4,8},{6,10},{8,4},{10,6},{12,0},{14,2},{1,13},{3,15... | collective-permute-start | bytes 245768 | tf_op jit(solution)/shard_map/ppermute | solution.py:40
  13.0 17.6 %collective-permute-start.4 = (bf16[64,640]{1,0:T(8,128)(2,1)S(1)}, bf16[64,640]{1,0:T(8,128)(2,1)S(1)}, u32[]{:S(2)}, u32[]{:S(2)}) collective-permute-start(bf16[64,640]{1,0:T(8,128)(2,1)S(1)} %get-tuple-element.46), channel_id=1, source_target_pairs={{0,2},{2,0},{4,6},{6,4},{8,10},{10,8},{12,14},{14,12},{1,3},{3,1},... | collective-permute-start | bytes 245768 | tf_op jit(solution)/shard_map/ppermute | solution.py:40
  14.7 15.9 %collective-permute-start.5 = (bf16[64,640]{1,0:T(8,128)(2,1)S(1)}, bf16[64,640]{1,0:T(8,128)(2,1)S(1)}, u32[]{:S(2)}, u32[]{:S(2)}) collective-permute-start(bf16[64,640]{1,0:T(8,128)(2,1)S(1)} %get-tuple-element.47), channel_id=1, source_target_pairs={{0,6},{2,4},{4,2},{6,0},{8,14},{10,12},{12,10},{14,8},{1,7},{3,5},... | collective-permute-start | bytes 245768 | tf_op jit(solution)/shard_map/ppermute | solution.py:40
  15.4 15.3 %collective-permute-start.6 = (bf16[64,640]{1,0:T(8,128)(2,1)S(1)}, bf16[64,640]{1,0:T(8,128)(2,1)S(1)}, u32[]{:S(2)}, u32[]{:S(2)}) collective-permute-start(bf16[64,640]{1,0:T(8,128)(2,1)S(1)} %get-tuple-element.48), channel_id=1, source_target_pairs={{0,10},{2,8},{4,14},{6,12},{8,2},{10,0},{12,6},{14,4},{1,11},{3,9}... | collective-permute-start | bytes 245768 | tf_op jit(solution)/shard_map/ppermute | solution.py:40
  19.8 10.9 %copy-start.2 = (s32[2,8]{1,0:T(2,128)S(1)}, s32[2,8]{1,0:T(2,128)}, u32[]{:S(2)}) copy-start(s32[2,8]{1,0:T(2,128)} %lengths.3) | copy-start | bytes 196
  19.8 10.9 %collective-permute-start.7 = (bf16[64,640]{1,0:T(8,128)(2,1)S(1)}, bf16[64,640]{1,0:T(8,128)(2,1)S(1)}, u32[]{:S(2)}, u32[]{:S(2)}) collective-permute-start(bf16[64,640]{1,0:T(8,128)(2,1)S(1)} %get-tuple-element.49), channel_id=1, source_target_pairs={{0,14},{2,12},{4,10},{6,8},{8,6},{10,4},{12,2},{14,0},{1,15},{3,13... | collective-permute-start | bytes 245768 | tf_op jit(solution)/shard_map/ppermute | solution.py:40
  33.5 8.1 %collective-permute-start.8 = (f16[4,40,1024]{2,1,0:T(8,128)(2,1)S(1)}, f16[4,40,1024]{2,1,0:T(8,128)(2,1)S(1)}, u32[]{:S(2)}, u32[]{:S(2)}) collective-permute-start(f16[4,40,1024]{2,1,0:T(8,128)(2,1)S(1)} %bitcast.57), channel_id=1, source_target_pairs={{0,2},{2,0},{4,6},{6,4},{8,10},{10,8},{12,14},{14,12},{1,3},{3,1},... | collective-permute-start | bytes 983048 | tf_op jit(solution)/shard_map/ppermute | solution.py:40
  41.8 6.9 %collective-permute-start.11 = (f16[40,1024]{1,0:T(8,128)(2,1)S(1)}, f16[40,1024]{1,0:T(8,128)(2,1)S(1)}, u32[]{:S(2)}, u32[]{:S(2)}) collective-permute-start(f16[40,1024]{1,0:T(8,128)(2,1)S(1)} %get-tuple-element.79), channel_id=1, source_target_pairs={{0,12},{2,14},{4,8},{6,10},{8,4},{10,6},{12,0},{14,2},{1,13},{3,15... | collective-permute-start | bytes 245768 | tf_op jit(solution)/shard_map/ppermute | solution.py:40
  41.9 8.8 %collective-permute-start.10 = (f16[40,1024]{1,0:T(8,128)(2,1)S(1)}, f16[40,1024]{1,0:T(8,128)(2,1)S(1)}, u32[]{:S(2)}, u32[]{:S(2)}) collective-permute-start(f16[40,1024]{1,0:T(8,128)(2,1)S(1)} %get-tuple-element.80), channel_id=1, source_target_pairs={{0,8},{2,10},{4,12},{6,14},{8,0},{10,2},{12,4},{14,6},{1,9},{3,11}... | collective-permute-start | bytes 245768 | tf_op jit(solution)/shard_map/ppermute | solution.py:40
  41.9 8.7 %collective-permute-start.9 = (f16[40,1024]{1,0:T(8,128)(2,1)S(1)}, f16[40,1024]{1,0:T(8,128)(2,1)S(1)}, u32[]{:S(2)}, u32[]{:S(2)}) collective-permute-start(f16[40,1024]{1,0:T(8,128)(2,1)S(1)} %get-tuple-element.78), channel_id=1, source_target_pairs={{0,4},{2,6},{4,0},{6,2},{8,12},{10,14},{12,8},{14,10},{1,5},{3,7},... | collective-permute-start | bytes 245768 | tf_op jit(solution)/shard_map/ppermute | solution.py:40
  46.3 15.9 %collective-permute-start.15 = (f16[4,40,1024]{2,1,0:T(8,128)(2,1)S(1)}, f16[4,40,1024]{2,1,0:T(8,128)(2,1)S(1)}, u32[]{:S(2)}, u32[]{:S(2)}) collective-permute-start(f16[4,40,1024]{2,1,0:T(8,128)(2,1)S(1)} %bitcast.56), channel_id=1, source_target_pairs={{0,2},{2,0},{4,6},{6,4},{8,10},{10,8},{12,14},{14,12},{1,3},{3,1},... | collective-permute-start | bytes 983048 | tf_op jit(solution)/shard_map/ppermute | solution.py:40
  50.8 7.3 %collective-permute-start.14 = (bf16[40,1024]{1,0:T(8,128)(2,1)S(1)}, bf16[40,1024]{1,0:T(8,128)(2,1)S(1)}, u32[]{:S(2)}, u32[]{:S(2)}) collective-permute-start(bf16[40,1024]{1,0:T(8,128)(2,1)S(1)} %fusion.13), channel_id=1, source_target_pairs={{0,12},{2,14},{4,8},{6,10},{8,4},{10,6},{12,0},{14,2},{1,13},{3,15... | collective-permute-start | bytes 245768 | tf_op jit(solution)/shard_map/ppermute | solution.py:40
  52.6 8.6 %collective-permute-start.13 = (bf16[40,1024]{1,0:T(8,128)(2,1)S(1)}, bf16[40,1024]{1,0:T(8,128)(2,1)S(1)}, u32[]{:S(2)}, u32[]{:S(2)}) collective-permute-start(bf16[40,1024]{1,0:T(8,128)(2,1)S(1)} %fusion.13), channel_id=1, source_target_pairs={{0,8},{2,10},{4,12},{6,14},{8,0},{10,2},{12,4},{14,6},{1,9},{3,11}... | collective-permute-start | bytes 245768 | tf_op jit(solution)/shard_map/ppermute | solution.py:40
  52.6 8.6 %collective-permute-start.12 = (bf16[40,1024]{1,0:T(8,128)(2,1)S(1)}, bf16[40,1024]{1,0:T(8,128)(2,1)S(1)}, u32[]{:S(2)}, u32[]{:S(2)}) collective-permute-start(bf16[40,1024]{1,0:T(8,128)(2,1)S(1)} %fusion.13), channel_id=1, source_target_pairs={{0,4},{2,6},{4,0},{6,2},{8,12},{10,14},{12,8},{14,10},{1,5},{3,7},... | collective-permute-start | bytes 245768 | tf_op jit(solution)/shard_map/ppermute | solution.py:40
  61.3 15.3 %collective-permute-start.22 = (bf16[4,40,1024]{2,1,0:T(8,128)(2,1)S(1)}, bf16[4,40,1024]{2,1,0:T(8,128)(2,1)S(1)}, u32[]{:S(2)}, u32[]{:S(2)}) collective-permute-start(bf16[4,40,1024]{2,1,0:T(8,128)(2,1)S(1)} %pad_maximum_fusion.refs_4_), channel_id=1, source_target_pairs={{0,2},{2,0},{4,6},{6,4},{8,10},{10,8},{12,14},{14,12},{1,3},{3,1},... | collective-permute-start | bytes 983048 | tf_op jit(solution)/shard_map/ppermute | solution.py:40
  62.4 7.2 %collective-permute-start.18 = (f16[40,1024]{1,0:T(8,128)(2,1)S(1)}, f16[40,1024]{1,0:T(8,128)(2,1)S(1)}, u32[]{:S(2)}, u32[]{:S(2)}) collective-permute-start(f16[40,1024]{1,0:T(8,128)(2,1)S(1)} %get-tuple-element.59), channel_id=1, source_target_pairs={{0,12},{2,14},{4,8},{6,10},{8,4},{10,6},{12,0},{14,2},{1,13},{3,15... | collective-permute-start | bytes 245768 | tf_op jit(solution)/shard_map/ppermute | solution.py:40
  64.4 7.6 %collective-permute-start.17 = (f16[40,1024]{1,0:T(8,128)(2,1)S(1)}, f16[40,1024]{1,0:T(8,128)(2,1)S(1)}, u32[]{:S(2)}, u32[]{:S(2)}) collective-permute-start(f16[40,1024]{1,0:T(8,128)(2,1)S(1)} %get-tuple-element.58), channel_id=1, source_target_pairs={{0,8},{2,10},{4,12},{6,14},{8,0},{10,2},{12,4},{14,6},{1,9},{3,11}... | collective-permute-start | bytes 245768 | tf_op jit(solution)/shard_map/ppermute | solution.py:40
  64.4 7.6 %collective-permute-start.16 = (f16[40,1024]{1,0:T(8,128)(2,1)S(1)}, f16[40,1024]{1,0:T(8,128)(2,1)S(1)}, u32[]{:S(2)}, u32[]{:S(2)}) collective-permute-start(f16[40,1024]{1,0:T(8,128)(2,1)S(1)} %get-tuple-element.57), channel_id=1, source_target_pairs={{0,4},{2,6},{4,0},{6,2},{8,12},{10,14},{12,8},{14,10},{1,5},{3,7},... | collective-permute-start | bytes 245768 | tf_op jit(solution)/shard_map/ppermute | solution.py:40
  72.1 12.1 %collective-permute-start.19 = (bf16[40,1024]{1,0:T(8,128)(2,1)S(1)}, bf16[40,1024]{1,0:T(8,128)(2,1)S(1)}, u32[]{:S(2)}, u32[]{:S(2)}) collective-permute-start(bf16[40,1024]{1,0:T(8,128)(2,1)S(1)} %fusion.6), channel_id=1, source_target_pairs={{0,4},{2,6},{4,0},{6,2},{8,12},{10,14},{12,8},{14,10},{1,5},{3,7},... | collective-permute-start | bytes 245768 | tf_op jit(solution)/shard_map/ppermute | solution.py:40
  72.2 12.0 %collective-permute-start.20 = (bf16[40,1024]{1,0:T(8,128)(2,1)S(1)}, bf16[40,1024]{1,0:T(8,128)(2,1)S(1)}, u32[]{:S(2)}, u32[]{:S(2)}) collective-permute-start(bf16[40,1024]{1,0:T(8,128)(2,1)S(1)} %fusion.6), channel_id=1, source_target_pairs={{0,8},{2,10},{4,12},{6,14},{8,0},{10,2},{12,4},{14,6},{1,9},{3,11}... | collective-permute-start | bytes 245768 | tf_op jit(solution)/shard_map/ppermute | solution.py:40
  74.5 9.6 %collective-permute-start.21 = (bf16[40,1024]{1,0:T(8,128)(2,1)S(1)}, bf16[40,1024]{1,0:T(8,128)(2,1)S(1)}, u32[]{:S(2)}, u32[]{:S(2)}) collective-permute-start(bf16[40,1024]{1,0:T(8,128)(2,1)S(1)} %fusion.6), channel_id=1, source_target_pairs={{0,12},{2,14},{4,8},{6,10},{8,4},{10,6},{12,0},{14,2},{1,13},{3,15... | collective-permute-start | bytes 245768 | tf_op jit(solution)/shard_map/ppermute | solution.py:40
  84.2 10.2 %collective-permute-start.27 = (bf16[4,40,1024]{2,1,0:T(8,128)(2,1)S(1)}, bf16[4,40,1024]{2,1,0:T(8,128)(2,1)S(1)}, u32[]{:S(2)}, u32[]{:S(2)}) collective-permute-start(bf16[4,40,1024]{2,1,0:T(8,128)(2,1)S(1)} %pad_maximum_fusion.1.refs_4_), channel_id=1, source_target_pairs={{0,2},{2,0},{4,6},{6,4},{8,10},{10,8},{12,14},{14,12},{1,3},{3,1},... | collective-permute-start | bytes 983048 | tf_op jit(solution)/shard_map/ppermute | solution.py:40
  84.3 19.7 %collective-permute-start.23 = (bf16[4,64,1152]{2,1,0:T(8,128)(2,1)S(1)}, bf16[4,64,1152]{2,1,0:T(8,128)(2,1)S(1)}, u32[]{:S(2)}, u32[]{:S(2)}) collective-permute-start(bf16[4,64,1152]{2,1,0:T(8,128)(2,1)S(1)} %attend.4), channel_id=1, source_target_pairs={{0,2},{2,0},{4,6},{6,4},{8,10},{10,8},{12,14},{14,12},{1,3},{3,1},... | collective-permute-start | bytes 1769480 | tf_op jit(solution)/shard_map/ppermute | solution.py:40
  102.3 15.8 %collective-permute-start.28 = (bf16[4,64,1152]{2,1,0:T(8,128)(2,1)S(1)}, bf16[4,64,1152]{2,1,0:T(8,128)(2,1)S(1)}, u32[]{:S(2)}, u32[]{:S(2)}) collective-permute-start(bf16[4,64,1152]{2,1,0:T(8,128)(2,1)S(1)} %attend.6), channel_id=1, source_target_pairs={{0,2},{2,0},{4,6},{6,4},{8,10},{10,8},{12,14},{14,12},{1,3},{3,1},... | collective-permute-start | bytes 1769480 | tf_op jit(solution)/shard_map/ppermute | solution.py:40
  113.6 14.2 %collective-permute-start.24 = (bf16[64,1152]{1,0:T(8,128)(2,1)S(1)}, bf16[64,1152]{1,0:T(8,128)(2,1)S(1)}, u32[]{:S(2)}, u32[]{:S(2)}) collective-permute-start(bf16[64,1152]{1,0:T(8,128)(2,1)S(1)} %get-tuple-element.68), channel_id=1, source_target_pairs={{0,4},{2,6},{4,0},{6,2},{8,12},{10,14},{12,8},{14,10},{1,5},{3,7},... | collective-permute-start | bytes 442376 | tf_op jit(solution)/shard_map/ppermute | solution.py:40
  113.7 18.4 %collective-permute-start.25 = (bf16[64,1152]{1,0:T(8,128)(2,1)S(1)}, bf16[64,1152]{1,0:T(8,128)(2,1)S(1)}, u32[]{:S(2)}, u32[]{:S(2)}) collective-permute-start(bf16[64,1152]{1,0:T(8,128)(2,1)S(1)} %get-tuple-element.69), channel_id=1, source_target_pairs={{0,8},{2,10},{4,12},{6,14},{8,0},{10,2},{12,4},{14,6},{1,9},{3,11}... | collective-permute-start | bytes 442376 | tf_op jit(solution)/shard_map/ppermute | solution.py:40
  113.7 18.4 %collective-permute-start.26 = (bf16[64,1152]{1,0:T(8,128)(2,1)S(1)}, bf16[64,1152]{1,0:T(8,128)(2,1)S(1)}, u32[]{:S(2)}, u32[]{:S(2)}) collective-permute-start(bf16[64,1152]{1,0:T(8,128)(2,1)S(1)} %get-tuple-element.70), channel_id=1, source_target_pairs={{0,12},{2,14},{4,8},{6,10},{8,4},{10,6},{12,0},{14,2},{1,13},{3,15... | collective-permute-start | bytes 442376 | tf_op jit(solution)/shard_map/ppermute | solution.py:40
  127.6 6.6 %collective-permute-start.29 = (bf16[64,1152]{1,0:T(8,128)(2,1)S(1)}, bf16[64,1152]{1,0:T(8,128)(2,1)S(1)}, u32[]{:S(2)}, u32[]{:S(2)}) collective-permute-start(bf16[64,1152]{1,0:T(8,128)(2,1)S(1)} %get-tuple-element.72), channel_id=1, source_target_pairs={{0,4},{2,6},{4,0},{6,2},{8,12},{10,14},{12,8},{14,10},{1,5},{3,7},... | collective-permute-start | bytes 442376 | tf_op jit(solution)/shard_map/ppermute | solution.py:40
  127.7 9.3 %collective-permute-start.30 = (bf16[64,1152]{1,0:T(8,128)(2,1)S(1)}, bf16[64,1152]{1,0:T(8,128)(2,1)S(1)}, u32[]{:S(2)}, u32[]{:S(2)}) collective-permute-start(bf16[64,1152]{1,0:T(8,128)(2,1)S(1)} %get-tuple-element.73), channel_id=1, source_target_pairs={{0,8},{2,10},{4,12},{6,14},{8,0},{10,2},{12,4},{14,6},{1,9},{3,11}... | collective-permute-start | bytes 442376 | tf_op jit(solution)/shard_map/ppermute | solution.py:40
  127.8 9.2 %collective-permute-start.31 = (bf16[64,1152]{1,0:T(8,128)(2,1)S(1)}, bf16[64,1152]{1,0:T(8,128)(2,1)S(1)}, u32[]{:S(2)}, u32[]{:S(2)}) collective-permute-start(bf16[64,1152]{1,0:T(8,128)(2,1)S(1)} %get-tuple-element.74), channel_id=1, source_target_pairs={{0,12},{2,14},{4,8},{6,10},{8,4},{10,6},{12,0},{14,2},{1,13},{3,15... | collective-permute-start | bytes 442376 | tf_op jit(solution)/shard_map/ppermute | solution.py:40

commit v4 on v3

--- a/solution.py
+++ b/solution.py
@@ -73,26 +73,7 @@
     )(place, hidden, handed)
 
 
-def fetch_kernel(chunk, width, first, place, prompts, prompt_lengths, cache_ref, *refs):
-    plain = (len(refs) - 3) // 2
-    sources, (kv_ref, *copies), (kv_sem, sem) = refs[:plain], refs[plain:-2], refs[-2:]
-    count, tile_len = kv_ref.shape[:2]
-    section, shard = place[0], place[1]
-    moves = [
-        (None, pltpu.make_async_copy(source, copy, sem.at[i]))
-        for i, (source, copy) in enumerate(zip(sources, copies))
-    ]
-    for p in range(count if first is not None else 0):
-        asked = prompts[section, 0] == p
-        for b in range(1, prompts.shape[1]):
-            asked = asked | (prompts[section, b] == p)
-        for c in range(tile_len // chunk):
-            at = pl.ds(c * chunk, chunk)
-            needed = asked & (prompt_lengths[p] > shard * tile_len + c * chunk)
-            moves.append((needed, pltpu.make_async_copy(
-                cache_ref.at[0, p, at, pl.ds(first * width, width)], kv_ref.at[p, at],
-                kv_sem.at[p, c],
-            )))
+def run_moves(moves):
     for needed, move in moves:
         if needed is None:
             move.start()
@@ -105,33 +86,69 @@
             pl.when(needed)(move.wait)
 
 
-def fetch(place, prompts, prompt_lengths, cache, width, first, plain):
+def fetch_kernel(*refs):
+    count = len(refs) // 2
+    run_moves([
+        (None, pltpu.make_async_copy(refs[i], refs[count + i], refs[-1].at[i]))
+        for i in range(count)
+    ])
+
+
+def fetch(arrays):
+    anywhere, near = pl.BlockSpec(memory_space=pltpu.HBM), pl.BlockSpec(memory_space=pltpu.VMEM)
+    size = sum(math.prod(array.shape) for array in arrays)
+    out = pl.pallas_call(
+        fetch_kernel,
+        in_specs=[anywhere] * len(arrays),
+        out_specs=[near] * len(arrays),
+        scratch_shapes=[pltpu.SemaphoreType.DMA((len(arrays),))],
+        out_shape=[pltpu.VMEM(array.shape, array.dtype) for array in arrays],
+        compiler_params=pltpu.CompilerParams(vmem_limit_bytes=4 * MIB),
+        cost_estimate=pl.CostEstimate(flops=0, bytes_accessed=2 * size, transcendentals=0),
+        name="fetch",
+    )(*[pltpu.with_memory_space_constraint(array, pltpu.HBM) for array in arrays])
+    return [pltpu.with_memory_space_constraint(array, pltpu.VMEM) for array in out]
+
+
+def fetch_cache_kernel(chunk, width, first, place, prompts, prompt_lengths, cache_ref, kv_ref, sem):
+    count, tile_len = kv_ref.shape[:2]
+    section, shard = place[0], place[1]
+    moves = []
+    for p in range(count):
+        asked = prompts[section, 0] == p
+        for b in range(1, prompts.shape[1]):
+            asked = asked | (prompts[section, b] == p)
+        for c in range(tile_len // chunk):
+            at = pl.ds(c * chunk, chunk)
+            needed = asked & (prompt_lengths[p] > shard * tile_len + c * chunk)
+            moves.append((needed, pltpu.make_async_copy(
+                cache_ref.at[0, p, at, pl.ds(first * width, width)], kv_ref.at[p, at],
+                sem.at[p, c],
+            )))
+    run_moves(moves)
+
+
+def fetch_cache(place, prompts, prompt_lengths, cache, width, first):
     count, tile_len = cache.shape[1:3]
     chunk = min(CHUNK, tile_len)
-    shape = (count, tile_len, width) if first is not None else (1, 16, HD)
-    anywhere, near = pl.BlockSpec(memory_space=pltpu.HBM), pl.BlockSpec(memory_space=pltpu.VMEM)
-    size = math.prod(shape) + sum(math.prod(array.shape) for array in plain)
-    return pl.pallas_call(
-        functools.partial(fetch_kernel, chunk, width, first),
+    shape = (count, tile_len, width)
+    out = pl.pallas_call(
+        functools.partial(fetch_cache_kernel, chunk, width, first),
         grid_spec=pltpu.PrefetchScalarGridSpec(
             num_scalar_prefetch=3,
             grid=(1,),
-            in_specs=[anywhere] * (1 + len(plain)),
-            out_specs=[near] * (1 + len(plain)),
-            scratch_shapes=[
-                pltpu.SemaphoreType.DMA((count, tile_len // chunk)),
-                pltpu.SemaphoreType.DMA((len(plain) + 1,)),
-            ],
-        ),
-        out_shape=[pltpu.VMEM(shape, cache.dtype)]
-        + [pltpu.VMEM(array.shape, array.dtype) for array in plain],
+            in_specs=[pl.BlockSpec(memory_space=pltpu.HBM)],
+            out_specs=pl.BlockSpec(memory_space=pltpu.VMEM),
+            scratch_shapes=[pltpu.SemaphoreType.DMA((count, tile_len // chunk))],
+        ),
+        out_shape=pltpu.VMEM(shape, cache.dtype),
         compiler_params=pltpu.CompilerParams(vmem_limit_bytes=4 * MIB),
-        cost_estimate=pl.CostEstimate(flops=0, bytes_accessed=2 * size, transcendentals=0),
-        name="fetch",
-    )(
-        place, prompts, prompt_lengths,
-        *[pltpu.with_memory_space_constraint(array, pltpu.HBM) for array in (cache, *plain)],
-    )
+        cost_estimate=pl.CostEstimate(
+            flops=0, bytes_accessed=2 * math.prod(shape), transcendentals=0
+        ),
+        name="fetch_cache",
+    )(place, prompts, prompt_lengths, pltpu.with_memory_space_constraint(cache, pltpu.HBM))
+    return pltpu.with_memory_space_constraint(out, pltpu.VMEM)
 
 
 def project_kernel(grid, bl, share, place, lengths, *refs):
@@ -201,11 +218,13 @@
 
 def encode(lse):
     lane = lax.broadcasted_iota(jnp.int32, lse.shape, 1)
+    lse = jnp.where(lane < SLOT, lse, 0.0)
     high = lse.astype(jnp.bfloat16).astype(jnp.float32)
     rest = lse - high
     mid = rest.astype(jnp.bfloat16).astype(jnp.float32)
     low = rest - mid
-    return jnp.where(lane < SLOT, high, jnp.where(lane < 2 * SLOT, mid, low)).astype(jnp.bfloat16)
+    terms = high + pltpu.roll(mid, SLOT, 1) + pltpu.roll(low, 2 * SLOT, 1)
+    return terms.astype(jnp.bfloat16)
 
 
 def decode(tile):
@@ -213,42 +232,72 @@
     return terms + pltpu.roll(terms, EXTRA - SLOT, 1) + pltpu.roll(terms, EXTRA - 2 * SLOT, 1)
 
 
-def merge(values, lses, heads):
-    bl = lses[0].shape[0]
-    lane = lax.broadcasted_iota(jnp.int32, lses[0].shape, 1)
+def merge(refs, heads):
+    width = heads * HD
+    lses = [decode(ref[:, width:]) for ref in refs]
+    rows = lses[0].shape[0]
     peak = functools.reduce(jnp.maximum, lses)
     weights = [jnp.exp2(lse - peak) for lse in lses]
     total = functools.reduce(jnp.add, weights)
     weights = [weight / total for weight in weights]
-    merged = peak + jnp.log2(total)
     out = []
-    spread = jnp.zeros((bl, EXTRA), jnp.float32)
     for h in range(heads):
         terms = [
-            jnp.broadcast_to(weight[:, h:h + 1], (bl, HD)) * value(h).astype(jnp.float32)
-            for weight, value in zip(weights, values)
+            jnp.broadcast_to(weight[:, h:h + 1], (rows, HD))
+            * ref[:, h * HD:(h + 1) * HD].astype(jnp.float32)
+            for weight, ref in zip(weights, refs)
         ]
         out.append(functools.reduce(jnp.add, terms))
-        spread = jnp.where(lane % SLOT == h, merged[:, h:h + 1], spread)
-    return out, spread
+    return out, peak + jnp.log2(total)
+
+
+def merge_kernel(zs, heads, *refs):
+    sources, outs = refs[:-zs], refs[-zs:]
+    for kz in range(zs):
+        parts, lse = merge([ref.at[kz] for ref in sources], heads)
+        for h in range(heads):
+            outs[kz][:, h * HD:(h + 1) * HD] = parts[h].astype(jnp.bfloat16)
+        outs[kz][:, heads * HD:] = encode(lse)
+
+
+def merge_column(sources, heads):
+    zs, bl, width = sources[0].shape
+    return pl.pallas_call(
+        functools.partial(merge_kernel, zs, heads),
+        out_shape=[jax.ShapeDtypeStruct((bl, width), jnp.bfloat16)] * zs,
+        compiler_params=pltpu.CompilerParams(vmem_limit_bytes=16 * MIB),
+        name="merge",
+    )(*sources)
 
 
 def attend_kernel(grid, kx, bl, share, heads, tile_len, *refs):
     place, lengths, prompts, prompt_lengths = refs[:4]
-    refs = refs[4:]
-    near_ref, refs = refs[0], refs[1:]
-    far_refs, refs = refs[:grid.xs - 1], refs[grid.xs - 1:]
-    kv_ref, refs = refs[0], refs[1:]
-    own_ref, refs = refs[0], refs[1:]
-    met = grid.xs - 1 if kx == 0 else 0
-    met_refs, refs = refs[:met], refs[met:]
-    outs = grid.zs if kx == 0 else 1
-    out_refs, refs = refs[:outs], refs[outs:]
-    q32_ref, acc_ref, m_ref = refs
-
-    step = pl.program_id(0)
+    near_ref, far_refs = refs[4], refs[5:4 + grid.xs]
+    kv_ref, own_ref, out_ref, q32_ref, acc_ref, m_ref = refs[4 + grid.xs:]
+    shard = place[1]
+    rows = grid.n * share
+    for fx in range(grid.xs):
+        for fz in range(grid.zs):
+            source = near_ref if fx == 0 else far_refs[fx - 1]
+            at = pl.multiple_of(grid.owner(shard, fx, fz) * share, 8)
+            q32_ref[pl.ds(at, share), :] = source[fz].astype(jnp.float32)
+    q32_ref[rows:, :] = jnp.zeros((bl + 8, q32_ref.shape[1]), jnp.float32)
+    acc_ref[...] = jnp.zeros_like(acc_ref)
+    m_ref[...] = jnp.full_like(m_ref, NEG)
+
+    def one(kz, carry):
+        attend_block(
+            grid, kx, bl, heads, tile_len, kz, place, lengths, prompts, prompt_lengths,
+            kv_ref, own_ref, out_ref, q32_ref, acc_ref, m_ref,
+        )
+        return carry
+
+    lax.fori_loop(0, grid.zs, one, 0)
+
+
+def attend_block(grid, kx, bl, heads, tile_len, step, place, lengths, prompts, prompt_lengths,
+                 kv_ref, own_ref, out_ref, q32_ref, acc_ref, m_ref):
     section, shard = place[0], place[1]
-    rows = grid.n * share
     block = grid.owner(shard, kx, step)
     offset = jnp.int32(0)
     for b in range(grid.n):
@@ -259,15 +308,6 @@
     chunk = min(CHUNK, tile_len)
     width = heads * GR * HD
 
-    @pl.when(step == 0)
-    def _():
-        for fx in range(grid.xs):
-            for fz in range(grid.zs):
-                source = near_ref if fx == 0 else far_refs[fx - 1]
-                at = pl.multiple_of(grid.owner(shard, fx, fz) * share, 8)
-                q32_ref[pl.ds(at, share), :] = source[fz].astype(jnp.float32)
-        q32_ref[rows:, :] = jnp.zeros((bl + 8, width), jnp.float32)
-
     rest = offset % 8
     window = q32_ref[pl.ds(pl.multiple_of(offset - rest, 8), bl + 8), :]
     window = pltpu.roll(window, jnp.where(rest == 0, 0, bl + 8 - rest), 0)
@@ -319,8 +359,11 @@
         lax.fori_loop(0, (valid + chunk - 1) // chunk, one, 0)
 
     length = lengths[section, block]
-    acc_ref[...] = jnp.zeros_like(acc_ref)
-    m_ref[...] = jnp.full_like(m_ref, NEG)
+
+    @pl.when(valid == 0)
+    def _():
+        acc_ref[...] = jnp.zeros_like(acc_ref)
+        m_ref[...] = jnp.full_like(m_ref, NEG)
 
     long = min(LONG, tile_len)
     for used in range(ROUND, bl + 1, ROUND):
@@ -384,73 +427,40 @@
 
     lane = lax.broadcasted_iota(jnp.int32, (bl, EXTRA), 1)
     lse_tile = jnp.zeros((bl, EXTRA), jnp.float32)
-    parts = []
     for g in range(heads):
         total = acc_ref[g][:, HD:]
         some = total > 0.0
         safe = jnp.where(some, total, 1.0)
-        out = acc_ref[g][:, :HD] / safe
+        out = (acc_ref[g][:, :HD] / safe).astype(jnp.bfloat16)
         lse = jnp.where(some, m_ref[g] * c2 + jnp.log2(safe), NEG)
         for r in range(GR):
             h = g * GR + r
-            parts.append(out[r * bl:(r + 1) * bl])
-            lse_tile = jnp.where(lane % SLOT == h, lse[r * bl:(r + 1) * bl], lse_tile)
-    if met:
-        values = [lambda h: parts[h]]
-        lses = [lse_tile]
-        for met_ref in met_refs:
-            values.append(lambda h, met_ref=met_ref: met_ref[0, :, h * HD:(h + 1) * HD])
-            lses.append(decode(met_ref[0, :, width:]))
-        parts, lse_tile = merge(values, lses, heads * GR)
-    terms = encode(lse_tile)
-
-    def write(out_ref, lead):
-        for h in range(heads * GR):
-            out_ref[lead + (slice(None), slice(h * HD, (h + 1) * HD))] = parts[h].astype(
-                jnp.bfloat16
-            )
-        out_ref[lead + (slice(None), slice(width, width + EXTRA))] = terms
-
-    if kx == 0:
-        for kz in range(grid.zs):
-            @pl.when(step == kz)
-            def _():
-                write(out_refs[kz], ())
-    else:
-        write(out_refs[0], (0,))
-
-
-def attend(grid, kx, place, lengths, prompts, prompt_lengths, near, fars, cache, own, mets, first,
-           heads):
+            out_ref[step, :, h * HD:(h + 1) * HD] = out[r * bl:(r + 1) * bl]
+            lse_tile = jnp.where(lane == h, lse[r * bl:(r + 1) * bl], lse_tile)
+    out_ref[step, :, width:] = encode(lse_tile)
+
+
+def attend(grid, kx, place, lengths, prompts, prompt_lengths, near, fars, cache, own, first, heads):
     zs, share, cols = near.shape
     bl = own.shape[1]
     tile_len = cache.shape[1]
     width = heads * GR * HD + EXTRA
-
-    piece = jax.ShapeDtypeStruct((bl, width), jnp.bfloat16)
-    if kx == 0:
-        out_shape = [piece] * zs
-        out_specs = [pl.BlockSpec((bl, width), lambda i, *m: (0, 0))] * zs
-    else:
-        out_shape = jax.ShapeDtypeStruct((zs, bl, width), jnp.bfloat16)
-        out_specs = pl.BlockSpec((1, bl, width), lambda i, *m: (i, 0, 0))
     return pl.pallas_call(
         functools.partial(attend_kernel, grid, kx, bl, share, heads, tile_len),
         grid_spec=pltpu.PrefetchScalarGridSpec(
             num_scalar_prefetch=4,
-            grid=(zs,),
+            grid=(1,),
             in_specs=[pl.BlockSpec((zs, share, cols), lambda i, *m: (0, 0, 0))] * grid.xs
             + [pl.BlockSpec(memory_space=pltpu.VMEM)]
-            + [pl.BlockSpec((1, bl, heads * 2 * HD), lambda i, *m: (0, 0, first // heads))]
-            + [pl.BlockSpec((1, bl, width), lambda i, *m: (i, 0, 0))] * len(mets),
-            out_specs=out_specs,
+            + [pl.BlockSpec((1, bl, heads * 2 * HD), lambda i, *m: (0, 0, first // heads))],
+            out_specs=pl.BlockSpec((zs, bl, width), lambda i, *m: (0, 0, 0)),
             scratch_shapes=[
                 pltpu.VMEM((grid.n * share + bl + 8, cols), jnp.float32),
                 pltpu.VMEM((heads, GR * bl, 2 * HD), jnp.float32),
                 pltpu.VMEM((heads, GR * bl, HD), jnp.float32),
             ],
         ),
-        out_shape=out_shape,
+        out_shape=jax.ShapeDtypeStruct((zs, bl, width), jnp.bfloat16),
         compiler_params=pltpu.CompilerParams(vmem_limit_bytes=20 * MIB),
         cost_estimate=pl.CostEstimate(
             flops=8 * zs * bl * cols * tile_len,
@@ -458,7 +468,7 @@
             transcendentals=zs * bl * heads * GR * tile_len,
         ),
         name="attend",
-    )(place, lengths, prompts, prompt_lengths, near, *fars, cache, own, *mets)
+    )(place, lengths, prompts, prompt_lengths, near, *fars, cache, own)
 
 
 def finish_kernel(chunks, zs, heads, bl, place, lengths, *refs):
@@ -468,9 +478,7 @@
     width = heads * GR * HD
     for c in range(chunks):
         pieces = refs[c * zs:(c + 1) * zs]
-        values = [lambda h, ref=ref: ref[:, h * HD:(h + 1) * HD] for ref in pieces]
-        lses = [decode(ref[:, width:]) for ref in pieces]
-        parts, _ = merge(values, lses, heads * GR)
+        parts, _ = merge(pieces, heads * GR)
         for h in range(heads * GR):
             at = c * width + h * HD
             out_ref[0, :, at:at + HD] = jnp.where(row < length, parts[h], 0.0).astype(jnp.bfloat16)
@@ -516,21 +524,20 @@
     def after(value, done):
         return lax.optimization_barrier((value, done))[0]
 
-    def fetched(first, plain):
-        out = fetch(
-            place, prompts, prompt_lengths, prompt_cache, heads * 2 * HD, first, plain
-        )
-        return [pltpu.with_memory_space_constraint(array, pltpu.VMEM) for array in out]
+    def fetched(c):
+        return fetch_cache(place, prompts, prompt_lengths, prompt_cache, heads * 2 * HD, c)
 
     handed = lax.ppermute(carried, "sec", [(0, 1)])
-    _, hidden, weight, own = fetched(None, [hidden_rows, query_weight, response_cache])
     depth = query_weight.shape[1]
-    if depth % HD:
-        hidden = hidden_rows
+    hidden = hidden_rows if depth % HD else fetch([hidden_rows])[0]
     slices = split(grid, place, hidden, handed, depth)
-    x = [grid.swap(piece, k // grid.zs, k % grid.zs) if k else piece for k, piece in enumerate(slices)]
-    caches = [fetched(0, [])[0]]
-    x[0] = after(x[0], caches[0])
+    weight, own = fetch([query_weight, response_cache])
+    x = [slices[0]] + [None] * (grid.n - 1)
+    for kz in reversed(range(grid.zs)):
+        for kx in reversed(range(grid.xs)):
+            k = kx * grid.zs + kz
+            if k:
+                x[k] = grid.swap(slices[k], kx, kz)
     part = project(grid, place, response_lengths, x, weight, bl, share, chunks)
     part = [piece.reshape(grid.zs, share, part_cols) for piece in part]
     part = [part[c * grid.xs:(c + 1) * grid.xs] for c in range(chunks)]
@@ -557,45 +564,51 @@
     def gather_x(near):
         return [near] + [grid.swap(near, kx, 0) for kx in range(1, grid.xs)]
 
-    def call(c, kx, queries, mets):
+    def call(c, kx, queries):
         return attend(
             grid, kx, place, response_lengths, prompts, prompt_lengths, queries[0], queries[1:],
-            caches[c], own, mets, c * heads, heads,
+            caches[c], own, c * heads, heads,
         )
 
-    queries = [None] * chunks
-    sent = [[] for _ in range(chunks)]
+    def call_far(c, queries):
+        outs = [call(c, kx, queries) for kx in range(1, grid.xs)]
+        return outs, [grid.swap(out, kx + 1, 0) for kx, out in enumerate(outs)]
+
+    def send_z(merged):
+        return [merged[0]] + [grid.swap(merged[kz], 0, kz) for kz in range(1, grid.zs)]
+
+    caches = [None] * chunks
     if chunks > 1:
-        caches.append(fetched(1, [])[0])
+        caches[1] = fetched(1)
         part[0][0] = after(part[0][0], caches[1])
     held, got = sum_x(0, ())
     mine = sum_z(held, ())
     column = gather_z(mine)
-    near = jnp.stack(column)
+    caches[0] = fetched(0)
+    near = jnp.stack(after(column, caches[0]))
     if chunks > 1:
         held, _ = sum_x(1, got)
         mine = sum_z(held, column)
-    queries[0] = gather_x(near)
+    queries = gather_x(near)
     if chunks > 1:
         column = gather_z(mine)
-        queries[0][0] = after(queries[0][0], mine)
-    for kx in range(1, grid.xs):
-        out = call(0, kx, queries[0], [])
-        sent[0].append(grid.swap(out, kx, 0))
+        queries[0] = after(queries[0], mine)
+    outs, mets = call_far(0, queries)
     if chunks > 1:
-        near = jnp.stack(after(column, out))
-        queries[1] = gather_x(near)
-        queries[0][0] = after(queries[0][0], near)
-        for kx in range(1, grid.xs):
-            sent[1].append(None)
-    pieces = []
-    for c in range(chunks):
-        if c:
-            for kx in range(1, grid.xs):
-                sent[c][kx - 1] = grid.swap(call(c, kx, queries[c], []), kx, 0)
-        held = call(c, 0, queries[c], sent[c])
-        pieces.append(held[0])
-        pieces.extend(grid.swap(held[kz], 0, kz) for kz in range(1, grid.zs))
+        near = jnp.stack(after(column, outs))
+        later = gather_x(near)
+        queries[0] = after(queries[0], near)
+    held = call(0, 0, queries)
+    if chunks > 1:
+        later[0] = after(later[0], held)
+        outs, later_mets = call_far(1, later)
+        held = after(held, outs)
+    merged = merge_column([held] + mets, heads * GR)
+    pieces = send_z(merged)
+    if chunks > 1:
+        later[0] = after(later[0], merged)
+        held = call(1, 0, later)
+        pieces += send_z(merge_column([held] + later_mets, heads * GR))
     return finish(place, response_lengths, pieces, chunks, grid.zs, heads)
 
 

time: 139 us -> 129 us (0.928); the launches traced: 139 us -> 132 us
  waiting for transfers between devices: 32.3 us -> 17.2 us
  starting transfers between devices: 49.1 us -> 56.7 us
    ppermute x31, waiting for transfers between devices: 32.3 us -> 16.5 us  [swap(): return lax.ppermute(value, 'seq', pairs)]
    ppermute x31, starting transfers between devices: 46.7 us -> 54.3 us  [swap(): return lax.ppermute(value, 'seq', pairs)]
    pallas_call x4, Pallas kernels: 34.5 us -> 32.4 us  [attend(): pl.pallas_call(functools.partial(attend_kernel, grid, kx, bl, share, head...]
    pallas_call x3 -> x6, Pallas kernels: 15.2 us -> 16.6 us  [the longest x2 10.9 us: fetch_cache(): pl.pallas_call(functools.partial(fetch_cache_kernel, chunk, width, first)...]
  transfers between devices with their start and end apart: 32 -> 32, of which waited for: 11 -> 11; matrix products, arithmetic and copies ran while one was open for 0% -> 0% of each run, Pallas kernels for 36% -> 37%
where the time goes in v4:
time: 129 us; the launch traced here: 132 us
  starting transfers between devices  56.7 us (44%)
  Pallas kernels  54.8 us (42%)
  waiting for transfers between devices  17.2 us (13%)
  local copies, waits for them, and re-layouts  2.03 us (2%)
    ppermute x31, starting transfers between devices, swap(): return lax.ppermute(value, 'seq', pairs)  54.3 us
    pallas_call x4, Pallas kernels, attend(): pl.pallas_call(functools.partial(attend_kernel, grid, kx, bl, share, head...  32.4 us
    ppermute x31, waiting for transfers between devices, swap(): return lax.ppermute(value, 'seq', pairs)  16.5 us
    pallas_call x2, Pallas kernels, fetch_cache(): pl.pallas_call(functools.partial(fetch_cache_kernel, chunk, width, first)...  10.9 us
    pallas_call x2, Pallas kernels, fetch(): pl.pallas_call(fetch_kernel, in_specs=[anywhere] * len(arrays), out_specs...  2.85 us
    pallas_call x2, Pallas kernels, merge_column(): pl.pallas_call(functools.partial(merge_kernel, zs, heads), out_shape=[jax...  2.82 us
    pallas_call x1, Pallas kernels, project(): pl.pallas_call(functools.partial(project_kernel, grid, bl, share), grid_s...  2.74 us
  transfers between devices with their start and end apart: 32, of which 11 were waited for; matrix products, arithmetic and copies ran while one was open for 0% of the time, Pallas kernels for 37%

profile of v4, /device:TPU:0, one launch (start us, length us, event | category | flops | bytes accessed | tf_op | source)
XLA Modules:
  0.0 131.8 jit_solution(13767900163571990308)
XLA Ops:
  0.0 2.4 %collective-permute-start = (bf16[1,64,5120]{2,1,0:T(8,128)(2,1)}, bf16[1,64,5120]{2,1,0:T(8,128)(2,1)S(1)}, u32[]{:S(2)}, u32[]{:S(2)}) collective-permute-start(bf16[1,64,5120]{2,1,0:T(8,128)(2,1)} %param.9), channel_id=1, source_target_pairs={{0,16},{1,17},{2,18},{3,19},{4,20},{5,21},{6,22},{7,23},{8,24},{9,... | collective-permute-start | bytes 1966088 | tf_op jit(solution)/shard_map/ppermute | solution.py:530
  2.4 1.1 fetch.2.hidden_ref
  3.6 0.7 collective-permute-done.handed_ref
  4.3 0.7 split.1
  5.0 2.5 %collective-permute-start.1 = (bf16[64,640]{1,0:T(8,128)(2,1)S(1)}, bf16[64,640]{1,0:T(8,128)(2,1)S(1)}, u32[]{:S(2)}, u32[]{:S(2)}) collective-permute-start(bf16[64,640]{1,0:T(8,128)(2,1)S(1)} %get-tuple-element.46), channel_id=1, source_target_pairs={{0,4},{2,6},{4,0},{6,2},{8,12},{10,14},{12,8},{14,10},{1,5},{3,7},... | collective-permute-start | bytes 245768 | tf_op jit(solution)/shard_map/ppermute | solution.py:40
  7.5 2.6 %collective-permute-start.2 = (bf16[64,640]{1,0:T(8,128)(2,1)S(1)}, bf16[64,640]{1,0:T(8,128)(2,1)S(1)}, u32[]{:S(2)}, u32[]{:S(2)}) collective-permute-start(bf16[64,640]{1,0:T(8,128)(2,1)S(1)} %get-tuple-element.47), channel_id=1, source_target_pairs={{0,8},{2,10},{4,12},{6,14},{8,0},{10,2},{12,4},{14,6},{1,9},{3,11}... | collective-permute-start | bytes 245768 | tf_op jit(solution)/shard_map/ppermute | solution.py:40
  10.1 1.7 %collective-permute-start.4 = (bf16[64,640]{1,0:T(8,128)(2,1)S(1)}, bf16[64,640]{1,0:T(8,128)(2,1)S(1)}, u32[]{:S(2)}, u32[]{:S(2)}) collective-permute-start(bf16[64,640]{1,0:T(8,128)(2,1)S(1)} %get-tuple-element.49), channel_id=1, source_target_pairs={{0,2},{2,0},{4,6},{6,4},{8,10},{10,8},{12,14},{14,12},{1,3},{3,1},... | collective-permute-start | bytes 245768 | tf_op jit(solution)/shard_map/ppermute | solution.py:40
  11.8 0.6 collective-permute-start.5
  12.4 4.4 %collective-permute-start.6 = (bf16[64,640]{1,0:T(8,128)(2,1)S(1)}, bf16[64,640]{1,0:T(8,128)(2,1)S(1)}, u32[]{:S(2)}, u32[]{:S(2)}) collective-permute-start(bf16[64,640]{1,0:T(8,128)(2,1)S(1)} %get-tuple-element.51), channel_id=1, source_target_pairs={{0,10},{2,8},{4,14},{6,12},{8,2},{10,0},{12,6},{14,4},{1,11},{3,9}... | collective-permute-start | bytes 245768 | tf_op jit(solution)/shard_map/ppermute | solution.py:40
  16.8 4.1 %collective-permute-start.7 = (bf16[64,640]{1,0:T(8,128)(2,1)S(1)}, bf16[64,640]{1,0:T(8,128)(2,1)S(1)}, u32[]{:S(2)}, u32[]{:S(2)}) collective-permute-start(bf16[64,640]{1,0:T(8,128)(2,1)S(1)} %get-tuple-element.52), channel_id=1, source_target_pairs={{0,14},{2,12},{4,10},{6,8},{8,6},{10,4},{12,2},{14,0},{1,15},{3,13... | collective-permute-start | bytes 245768 | tf_op jit(solution)/shard_map/ppermute | solution.py:40
  20.9 1.8 %fetch.3 = (bf16[1,640,2048]{2,1,0:T(8,128)(2,1)S(1)}, bf16[1,64,1024]{2,1,0:T(8,128)(2,1)S(1)}) custom-call(bf16[1,640,2048]{2,1,0:T(8,128)(2,1)} %refs_0_.3, bf16[1,64,1024]{2,1,0:T(8,128)(2,1)} %refs_1_.5), custom_call_target="tpu_custom_call" | custom-call | bytes 2752512 | tf_op jit(solution)/shard_map/fetch/pallas_call | solution.py:100
  22.7 2.1 %collective-permute-done.6.refs_6_ = bf16[64,640]{1,0:T(8,128)(2,1)S(1)} collective-permute-done((bf16[64,640]{1,0:T(8,128)(2,1)S(1)}, bf16[64,640]{1,0:T(8,128)(2,1)S(1)}, u32[]{:S(2)}, u32[]{:S(2)}) %collective-permute-start.6) | collective-permute-done | bytes 81952 | tf_op jit(solution)/shard_map/ppermute | solution.py:40
  24.9 0.7 copy-done.2
  25.6 2.7 %project.1 = (f32[160,1024]{1,0:T(8,128)S(1)}, f32[160,1024]{1,0:T(8,128)S(1)}, f32[160,1024]{1,0:T(8,128)S(1)}, f32[160,1024]{1,0:T(8,128)S(1)}) custom-call(s32[2]{0:T(128)S(1)} %pad_add_fusion.place.refs_0_, s32[2,8]{1,0:T(2,128)S(1)} %copy-done.2, bf16[64,640]{1,0:T(8,128)(2,1)S(1)} %get-tuple-element.45.refs_0_, ...), custom_call_target="tpu_custom_call" | custom-call | flops 838860800 | bytes 5242880 | tf_op jit(solution)/shard_map/project/pallas_call | solution.py:197
  28.4 0.6 collective-permute-start.8
  29.0 0.7 copy-done
  29.7 0.7 copy-done.4
  30.3 5.5 %fetch_cache.2.refs_6_ = bf16[8,2048,512]{2,1,0:T(8,128)(2,1)S(1)} custom-call(s32[2]{0:T(128)S(1)} %pad_add_fusion.place.refs_0_, s32[2,8]{1,0:T(2,128)S(1)} %bitcast.49, s32[8]{0:T(128)S(1)} %copy-done.4, bf16[1,8,2048,1024]{3,2,1,0:T(8,128)(2,1)} %cache_ref.3), custom_call_target="tpu_custom_call" | custom-call | bytes 16777216 | tf_op jit(solution)/shard_map/fetch_cache/pallas_call | solution.py:135
  35.8 0.3 collective-permute-done.8
  36.3 3.7 %collective-permute-start.10 = (f16[40,1024]{1,0:T(8,128)(2,1)S(1)}, f16[40,1024]{1,0:T(8,128)(2,1)S(1)}, u32[]{:S(2)}, u32[]{:S(2)}) collective-permute-start(f16[40,1024]{1,0:T(8,128)(2,1)S(1)} %get-tuple-element.90), channel_id=1, source_target_pairs={{0,8},{2,10},{4,12},{6,14},{8,0},{10,2},{12,4},{14,6},{1,9},{3,11}... | collective-permute-start | bytes 245768 | tf_op jit(solution)/shard_map/ppermute | solution.py:40
  39.9 1.9 %collective-permute-start.11 = (f16[40,1024]{1,0:T(8,128)(2,1)S(1)}, f16[40,1024]{1,0:T(8,128)(2,1)S(1)}, u32[]{:S(2)}, u32[]{:S(2)}) collective-permute-start(f16[40,1024]{1,0:T(8,128)(2,1)S(1)} %get-tuple-element.89), channel_id=1, source_target_pairs={{0,12},{2,14},{4,8},{6,10},{8,4},{10,6},{12,0},{14,2},{1,13},{3,15... | collective-permute-start | bytes 245768 | tf_op jit(solution)/shard_map/ppermute | solution.py:40
  41.9 0.6 collective-permute-start.15
  42.5 1.4 %collective-permute-done.10 = f16[40,1024]{1,0:T(8,128)(2,1)S(1)} collective-permute-done((f16[40,1024]{1,0:T(8,128)(2,1)S(1)}, f16[40,1024]{1,0:T(8,128)(2,1)S(1)}, u32[]{:S(2)}, u32[]{:S(2)}) %collective-permute-start.10) | collective-permute-done | bytes 81952 | tf_op jit(solution)/shard_map/ppermute | solution.py:40
  44.0 2.4 %collective-permute-done.11 = f16[40,1024]{1,0:T(8,128)(2,1)S(1)} collective-permute-done((f16[40,1024]{1,0:T(8,128)(2,1)S(1)}, f16[40,1024]{1,0:T(8,128)(2,1)S(1)}, u32[]{:S(2)}, u32[]{:S(2)}) %collective-permute-start.11) | collective-permute-done | bytes 81952 | tf_op jit(solution)/shard_map/ppermute | solution.py:40
  46.4 0.8 collective-permute-done.9
  47.4 2.4 %collective-permute-start.13 = (bf16[40,1024]{1,0:T(8,128)(2,1)S(1)}, bf16[40,1024]{1,0:T(8,128)(2,1)S(1)}, u32[]{:S(2)}, u32[]{:S(2)}) collective-permute-start(bf16[40,1024]{1,0:T(8,128)(2,1)S(1)} %fusion.13), channel_id=1, source_target_pairs={{0,8},{2,10},{4,12},{6,14},{8,0},{10,2},{12,4},{14,6},{1,9},{3,11}... | collective-permute-start | bytes 245768 | tf_op jit(solution)/shard_map/ppermute | solution.py:40
  49.7 2.0 %collective-permute-start.14 = (bf16[40,1024]{1,0:T(8,128)(2,1)S(1)}, bf16[40,1024]{1,0:T(8,128)(2,1)S(1)}, u32[]{:S(2)}, u32[]{:S(2)}) collective-permute-start(bf16[40,1024]{1,0:T(8,128)(2,1)S(1)} %fusion.13), channel_id=1, source_target_pairs={{0,12},{2,14},{4,8},{6,10},{8,4},{10,6},{12,0},{14,2},{1,13},{3,15... | collective-permute-start | bytes 245768 | tf_op jit(solution)/shard_map/ppermute | solution.py:40
  51.7 5.5 %fetch_cache.3.refs_6_ = bf16[8,2048,512]{2,1,0:T(8,128)(2,1)S(1)} custom-call(s32[2]{0:T(128)S(1)} %pad_add_fusion.place.refs_0_, s32[2,8]{1,0:T(2,128)S(1)} %bitcast.50, s32[8]{0:T(128)S(1)} %copy-done.4, bf16[1,8,2048,1024]{3,2,1,0:T(8,128)(2,1)} %cache_ref.3), custom_call_target="tpu_custom_call" | custom-call | bytes 16777216 | tf_op jit(solution)/shard_map/fetch_cache/pallas_call | solution.py:135
  57.3 0.3 collective-permute-start.22
  57.8 1.3 %collective-permute-start.17 = (f16[40,1024]{1,0:T(8,128)(2,1)S(1)}, f16[40,1024]{1,0:T(8,128)(2,1)S(1)}, u32[]{:S(2)}, u32[]{:S(2)}) collective-permute-start(f16[40,1024]{1,0:T(8,128)(2,1)S(1)} %get-tuple-element.65), channel_id=1, source_target_pairs={{0,8},{2,10},{4,12},{6,14},{8,0},{10,2},{12,4},{14,6},{1,9},{3,11}... | collective-permute-start | bytes 245768 | tf_op jit(solution)/shard_map/ppermute | solution.py:40
  59.1 3.0 %collective-permute-start.18 = (f16[40,1024]{1,0:T(8,128)(2,1)S(1)}, f16[40,1024]{1,0:T(8,128)(2,1)S(1)}, u32[]{:S(2)}, u32[]{:S(2)}) collective-permute-start(f16[40,1024]{1,0:T(8,128)(2,1)S(1)} %get-tuple-element.66), channel_id=1, source_target_pairs={{0,12},{2,14},{4,8},{6,10},{8,4},{10,6},{12,0},{14,2},{1,13},{3,15... | collective-permute-start | bytes 245768 | tf_op jit(solution)/shard_map/ppermute | solution.py:40
  62.2 1.0 collective-permute-done.17
  63.2 3.5 %collective-permute-done.18 = f16[40,1024]{1,0:T(8,128)(2,1)S(1)} collective-permute-done((f16[40,1024]{1,0:T(8,128)(2,1)S(1)}, f16[40,1024]{1,0:T(8,128)(2,1)S(1)}, u32[]{:S(2)}, u32[]{:S(2)}) %collective-permute-start.18) | collective-permute-done | bytes 81952 | tf_op jit(solution)/shard_map/ppermute | solution.py:40
  66.8 2.7 %collective-permute-start.20 = (bf16[40,1024]{1,0:T(8,128)(2,1)S(1)}, bf16[40,1024]{1,0:T(8,128)(2,1)S(1)}, u32[]{:S(2)}, u32[]{:S(2)}) collective-permute-start(bf16[40,1024]{1,0:T(8,128)(2,1)S(1)} %fusion.6), channel_id=1, source_target_pairs={{0,8},{2,10},{4,12},{6,14},{8,0},{10,2},{12,4},{14,6},{1,9},{3,11}... | collective-permute-start | bytes 245768 | tf_op jit(solution)/shard_map/ppermute | solution.py:40
  69.5 1.6 %collective-permute-start.21 = (bf16[40,1024]{1,0:T(8,128)(2,1)S(1)}, bf16[40,1024]{1,0:T(8,128)(2,1)S(1)}, u32[]{:S(2)}, u32[]{:S(2)}) collective-permute-start(bf16[40,1024]{1,0:T(8,128)(2,1)S(1)} %fusion.6), channel_id=1, source_target_pairs={{0,12},{2,14},{4,8},{6,10},{8,4},{10,6},{12,0},{14,2},{1,13},{3,15... | collective-permute-start | bytes 245768 | tf_op jit(solution)/shard_map/ppermute | solution.py:40
  71.2 7.8 %attend.4 = bf16[4,64,1152]{2,1,0:T(8,128)(2,1)S(1)} custom-call(s32[2]{0:T(128)S(1)} %pad_add_fusion.place.refs_0_, s32[2,8]{1,0:T(2,128)S(1)} %copy-done.3, s32[2,8]{1,0:T(2,128)S(1)} %bitcast.51, s32[8]{0:T(128)S(1)} %copy-done.5, bf16[4,40,1024]{2,1,0:T(8,128)(2,1)S(1)} %pad_maximum_fusion.refs_4_, ...), custom_call_target="tpu_custom_call" | custom-call | flops 4294967296 | bytes 8388608 | tf_op jit(solution)/shard_map/attend/pallas_call | solution.py:448
  79.1 3.2 %collective-permute-start.23 = (bf16[4,40,1024]{2,1,0:T(8,128)(2,1)S(1)}, bf16[4,40,1024]{2,1,0:T(8,128)(2,1)S(1)}, u32[]{:S(2)}, u32[]{:S(2)}) collective-permute-start(bf16[4,40,1024]{2,1,0:T(8,128)(2,1)S(1)} %pad_maximum_fusion.1.refs_4_), channel_id=1, source_target_pairs={{0,2},{2,0},{4,6},{6,4},{8,10},{10,8},{12,14},{14,12},{1,3},{3,1},... | collective-permute-start | bytes 983048 | tf_op jit(solution)/shard_map/ppermute | solution.py:40
  82.3 8.3 %attend.5.refs_0_ = bf16[4,64,1152]{2,1,0:T(8,128)(2,1)S(1)} custom-call(s32[2]{0:T(128)S(1)} %pad_add_fusion.place.refs_0_, s32[2,8]{1,0:T(2,128)S(1)} %copy-done.3, s32[2,8]{1,0:T(2,128)S(1)} %bitcast.52, s32[8]{0:T(128)S(1)} %copy-done.5, bf16[4,40,1024]{2,1,0:T(8,128)(2,1)S(1)} %pad_maximum_fusion.refs_4_, ...), custom_call_target="tpu_custom_call" | custom-call | flops 4294967296 | bytes 8388608 | tf_op jit(solution)/shard_map/attend/pallas_call | solution.py:448
  90.6 8.0 %attend.6 = bf16[4,64,1152]{2,1,0:T(8,128)(2,1)S(1)} custom-call(s32[2]{0:T(128)S(1)} %pad_add_fusion.place.refs_0_, s32[2,8]{1,0:T(2,128)S(1)} %copy-done.3, s32[2,8]{1,0:T(2,128)S(1)} %bitcast.53, s32[8]{0:T(128)S(1)} %copy-done.5, bf16[4,40,1024]{2,1,0:T(8,128)(2,1)S(1)} %pad_maximum_fusion.1.refs_4_, ...), custom_call_target="tpu_custom_call" | custom-call | flops 4294967296 | bytes 8388608 | tf_op jit(solution)/shard_map/attend/pallas_call | solution.py:448
  98.6 5.9 %collective-permute-start.28 = (bf16[4,64,1152]{2,1,0:T(8,128)(2,1)S(1)}, bf16[4,64,1152]{2,1,0:T(8,128)(2,1)S(1)}, u32[]{:S(2)}, u32[]{:S(2)}) collective-permute-start(bf16[4,64,1152]{2,1,0:T(8,128)(2,1)S(1)} %attend.6), channel_id=1, source_target_pairs={{0,2},{2,0},{4,6},{6,4},{8,10},{10,8},{12,14},{14,12},{1,3},{3,1},... | collective-permute-start | bytes 1769480 | tf_op jit(solution)/shard_map/ppermute | solution.py:40
  104.4 1.4 %merge.2 = (bf16[64,1152]{1,0:T(8,128)(2,1)S(1)}, bf16[64,1152]{1,0:T(8,128)(2,1)S(1)}, bf16[64,1152]{1,0:T(8,128)(2,1)S(1)}, bf16[64,1152]{1,0:T(8,128)(2,1)S(1)}) custom-call(bf16[4,64,1152]{2,1,0:T(8,128)(2,1)S(1)} %attend.5.refs_0_, bf16[4,64,1152]{2,1,0:T(8,128)(2,1)S(1)} %collective-permute-done.24.refs_1_), custom_call_target="tpu_custom_call" | custom-call | tf_op jit(solution)/shard_map/merge/pallas_call | solution.py:265
  106.0 4.3 %collective-permute-start.27 = (bf16[64,1152]{1,0:T(8,128)(2,1)S(1)}, bf16[64,1152]{1,0:T(8,128)(2,1)S(1)}, u32[]{:S(2)}, u32[]{:S(2)}) collective-permute-start(bf16[64,1152]{1,0:T(8,128)(2,1)S(1)} %get-tuple-element.79), channel_id=1, source_target_pairs={{0,12},{2,14},{4,8},{6,10},{8,4},{10,6},{12,0},{14,2},{1,13},{3,15... | collective-permute-start | bytes 442376 | tf_op jit(solution)/shard_map/ppermute | solution.py:40
  110.3 8.3 %attend.7.refs_0_ = bf16[4,64,1152]{2,1,0:T(8,128)(2,1)S(1)} custom-call(s32[2]{0:T(128)S(1)} %pad_add_fusion.place.refs_0_, s32[2,8]{1,0:T(2,128)S(1)} %copy-done.3, s32[2,8]{1,0:T(2,128)S(1)} %bitcast.54, s32[8]{0:T(128)S(1)} %copy-done.5, bf16[4,40,1024]{2,1,0:T(8,128)(2,1)S(1)} %pad_maximum_fusion.1.refs_4_, ...), custom_call_target="tpu_custom_call" | custom-call | flops 4294967296 | bytes 8388608 | tf_op jit(solution)/shard_map/attend/pallas_call | solution.py:448
  118.6 1.4 %merge.3 = (bf16[64,1152]{1,0:T(8,128)(2,1)S(1)}, bf16[64,1152]{1,0:T(8,128)(2,1)S(1)}, bf16[64,1152]{1,0:T(8,128)(2,1)S(1)}, bf16[64,1152]{1,0:T(8,128)(2,1)S(1)}) custom-call(bf16[4,64,1152]{2,1,0:T(8,128)(2,1)S(1)} %attend.7.refs_0_, bf16[4,64,1152]{2,1,0:T(8,128)(2,1)S(1)} %collective-permute-done.28.refs_1_), custom_call_target="tpu_custom_call" | custom-call | tf_op jit(solution)/shard_map/merge/pallas_call | solution.py:265
  120.2 4.3 %collective-permute-start.31 = (bf16[64,1152]{1,0:T(8,128)(2,1)S(1)}, bf16[64,1152]{1,0:T(8,128)(2,1)S(1)}, u32[]{:S(2)}, u32[]{:S(2)}) collective-permute-start(bf16[64,1152]{1,0:T(8,128)(2,1)S(1)} %get-tuple-element.84), channel_id=1, source_target_pairs={{0,12},{2,14},{4,8},{6,10},{8,4},{10,6},{12,0},{14,2},{1,13},{3,15... | collective-permute-start | bytes 442376 | tf_op jit(solution)/shard_map/ppermute | solution.py:40
  124.5 2.2 %collective-permute-done.29.refs_5_ = bf16[64,1152]{1,0:T(8,128)(2,1)S(1)} collective-permute-done((bf16[64,1152]{1,0:T(8,128)(2,1)S(1)}, bf16[64,1152]{1,0:T(8,128)(2,1)S(1)}, u32[]{:S(2)}, u32[]{:S(2)}) %collective-permute-start.29) | collective-permute-done | bytes 147488 | tf_op jit(solution)/shard_map/ppermute | solution.py:40
  126.7 2.7 %collective-permute-done.30.refs_6_ = bf16[64,1152]{1,0:T(8,128)(2,1)S(1)} collective-permute-done((bf16[64,1152]{1,0:T(8,128)(2,1)S(1)}, bf16[64,1152]{1,0:T(8,128)(2,1)S(1)}, u32[]{:S(2)}, u32[]{:S(2)}) %collective-permute-start.30) | collective-permute-done | bytes 147488 | tf_op jit(solution)/shard_map/ppermute | solution.py:40
  129.4 2.4 %finish.1 = bf16[1,64,2048]{2,1,0:T(8,128)(2,1)} custom-call(s32[2]{0:T(128)S(1)} %pad_add_fusion.place.refs_0_, s32[2,8]{1,0:T(2,128)S(1)} %copy-done.3, bf16[64,1152]{1,0:T(8,128)(2,1)S(1)} %get-tuple-element.76.refs_0_, bf16[64,1152]{1,0:T(8,128)(2,1)S(1)} %collective-permute-done.25.refs_1_, bf16[64,1152]{1,0:T(8,128)(2,1)S(1)} %collective-permute-done.26.refs_2_, ...), custom_call_target="tpu_custom_call" | custom-call | tf_op jit(solution)/shard_map/finish/pallas_call | solution.py:490
  (52 shorter events, 1.5 us)
Async XLA Ops:
  0.0 4.3 %collective-permute-start = (bf16[1,64,5120]{2,1,0:T(8,128)(2,1)}, bf16[1,64,5120]{2,1,0:T(8,128)(2,1)S(1)}, u32[]{:S(2)}, u32[]{:S(2)}) collective-permute-start(bf16[1,64,5120]{2,1,0:T(8,128)(2,1)} %param.9), channel_id=1, source_target_pairs={{0,16},{1,17},{2,18},{3,19},{4,20},{5,21},{6,22},{7,23},{8,24},{9,... | collective-permute-start | bytes 1966088 | tf_op jit(solution)/shard_map/ppermute | solution.py:530
  5.0 7.4 %collective-permute-start.1 = (bf16[64,640]{1,0:T(8,128)(2,1)S(1)}, bf16[64,640]{1,0:T(8,128)(2,1)S(1)}, u32[]{:S(2)}, u32[]{:S(2)}) collective-permute-start(bf16[64,640]{1,0:T(8,128)(2,1)S(1)} %get-tuple-element.46), channel_id=1, source_target_pairs={{0,4},{2,6},{4,0},{6,2},{8,12},{10,14},{12,8},{14,10},{1,5},{3,7},... | collective-permute-start | bytes 245768 | tf_op jit(solution)/shard_map/ppermute | solution.py:40
  7.5 9.4 %collective-permute-start.2 = (bf16[64,640]{1,0:T(8,128)(2,1)S(1)}, bf16[64,640]{1,0:T(8,128)(2,1)S(1)}, u32[]{:S(2)}, u32[]{:S(2)}) collective-permute-start(bf16[64,640]{1,0:T(8,128)(2,1)S(1)} %get-tuple-element.47), channel_id=1, source_target_pairs={{0,8},{2,10},{4,12},{6,14},{8,0},{10,2},{12,4},{14,6},{1,9},{3,11}... | collective-permute-start | bytes 245768 | tf_op jit(solution)/shard_map/ppermute | solution.py:40
  10.1 12.6 %collective-permute-start.3 = (bf16[64,640]{1,0:T(8,128)(2,1)S(1)}, bf16[64,640]{1,0:T(8,128)(2,1)S(1)}, u32[]{:S(2)}, u32[]{:S(2)}) collective-permute-start(bf16[64,640]{1,0:T(8,128)(2,1)S(1)} %get-tuple-element.48), channel_id=1, source_target_pairs={{0,12},{2,14},{4,8},{6,10},{8,4},{10,6},{12,0},{14,2},{1,13},{3,15... | collective-permute-start | bytes 245768 | tf_op jit(solution)/shard_map/ppermute | solution.py:40
  10.1 12.7 %collective-permute-start.4 = (bf16[64,640]{1,0:T(8,128)(2,1)S(1)}, bf16[64,640]{1,0:T(8,128)(2,1)S(1)}, u32[]{:S(2)}, u32[]{:S(2)}) collective-permute-start(bf16[64,640]{1,0:T(8,128)(2,1)S(1)} %get-tuple-element.49), channel_id=1, source_target_pairs={{0,2},{2,0},{4,6},{6,4},{8,10},{10,8},{12,14},{14,12},{1,3},{3,1},... | collective-permute-start | bytes 245768 | tf_op jit(solution)/shard_map/ppermute | solution.py:40
  11.8 11.0 %collective-permute-start.5 = (bf16[64,640]{1,0:T(8,128)(2,1)S(1)}, bf16[64,640]{1,0:T(8,128)(2,1)S(1)}, u32[]{:S(2)}, u32[]{:S(2)}) collective-permute-start(bf16[64,640]{1,0:T(8,128)(2,1)S(1)} %get-tuple-element.50), channel_id=1, source_target_pairs={{0,6},{2,4},{4,2},{6,0},{8,14},{10,12},{12,10},{14,8},{1,7},{3,5},... | collective-permute-start | bytes 245768 | tf_op jit(solution)/shard_map/ppermute | solution.py:40
  12.4 12.4 %collective-permute-start.6 = (bf16[64,640]{1,0:T(8,128)(2,1)S(1)}, bf16[64,640]{1,0:T(8,128)(2,1)S(1)}, u32[]{:S(2)}, u32[]{:S(2)}) collective-permute-start(bf16[64,640]{1,0:T(8,128)(2,1)S(1)} %get-tuple-element.51), channel_id=1, source_target_pairs={{0,10},{2,8},{4,14},{6,12},{8,2},{10,0},{12,6},{14,4},{1,11},{3,9}... | collective-permute-start | bytes 245768 | tf_op jit(solution)/shard_map/ppermute | solution.py:40
  16.8 8.0 %collective-permute-start.7 = (bf16[64,640]{1,0:T(8,128)(2,1)S(1)}, bf16[64,640]{1,0:T(8,128)(2,1)S(1)}, u32[]{:S(2)}, u32[]{:S(2)}) collective-permute-start(bf16[64,640]{1,0:T(8,128)(2,1)S(1)} %get-tuple-element.52), channel_id=1, source_target_pairs={{0,14},{2,12},{4,10},{6,8},{8,6},{10,4},{12,2},{14,0},{1,15},{3,13... | collective-permute-start | bytes 245768 | tf_op jit(solution)/shard_map/ppermute | solution.py:40
  24.9 0.7 copy-start.2
  28.4 7.7 %collective-permute-start.8 = (f16[4,40,1024]{2,1,0:T(8,128)(2,1)S(1)}, f16[4,40,1024]{2,1,0:T(8,128)(2,1)S(1)}, u32[]{:S(2)}, u32[]{:S(2)}) collective-permute-start(f16[4,40,1024]{2,1,0:T(8,128)(2,1)S(1)} %bitcast.56), channel_id=1, source_target_pairs={{0,2},{2,0},{4,6},{6,4},{8,10},{10,8},{12,14},{14,12},{1,3},{3,1},... | collective-permute-start | bytes 983048 | tf_op jit(solution)/shard_map/ppermute | solution.py:40
  29.0 0.7 copy-start
  29.7 0.7 copy-start.4
  30.3 21.4 %copy-start.1 = (s32[2,8,1]{1,2,0:T(1,128)S(1)}, s32[2,8,1]{1,2,0:T(1,128)}, u32[]{:S(2)}) copy-start(s32[2,8,1]{1,2,0:T(1,128)} %param.15) | copy-start | bytes 196
  36.3 7.7 %collective-permute-start.10 = (f16[40,1024]{1,0:T(8,128)(2,1)S(1)}, f16[40,1024]{1,0:T(8,128)(2,1)S(1)}, u32[]{:S(2)}, u32[]{:S(2)}) collective-permute-start(f16[40,1024]{1,0:T(8,128)(2,1)S(1)} %get-tuple-element.90), channel_id=1, source_target_pairs={{0,8},{2,10},{4,12},{6,14},{8,0},{10,2},{12,4},{14,6},{1,9},{3,11}... | collective-permute-start | bytes 245768 | tf_op jit(solution)/shard_map/ppermute | solution.py:40
  39.9 6.4 %collective-permute-start.11 = (f16[40,1024]{1,0:T(8,128)(2,1)S(1)}, f16[40,1024]{1,0:T(8,128)(2,1)S(1)}, u32[]{:S(2)}, u32[]{:S(2)}) collective-permute-start(f16[40,1024]{1,0:T(8,128)(2,1)S(1)} %get-tuple-element.89), channel_id=1, source_target_pairs={{0,12},{2,14},{4,8},{6,10},{8,4},{10,6},{12,0},{14,2},{1,13},{3,15... | collective-permute-start | bytes 245768 | tf_op jit(solution)/shard_map/ppermute | solution.py:40
  41.9 5.3 %collective-permute-start.9 = (f16[40,1024]{1,0:T(8,128)(2,1)S(1)}, f16[40,1024]{1,0:T(8,128)(2,1)S(1)}, u32[]{:S(2)}, u32[]{:S(2)}) collective-permute-start(f16[40,1024]{1,0:T(8,128)(2,1)S(1)} %get-tuple-element.88), channel_id=1, source_target_pairs={{0,4},{2,6},{4,0},{6,2},{8,12},{10,14},{12,8},{14,10},{1,5},{3,7},... | collective-permute-start | bytes 245768 | tf_op jit(solution)/shard_map/ppermute | solution.py:40
  41.9 15.6 %collective-permute-start.15 = (f16[4,40,1024]{2,1,0:T(8,128)(2,1)S(1)}, f16[4,40,1024]{2,1,0:T(8,128)(2,1)S(1)}, u32[]{:S(2)}, u32[]{:S(2)}) collective-permute-start(f16[4,40,1024]{2,1,0:T(8,128)(2,1)S(1)} %bitcast.55), channel_id=1, source_target_pairs={{0,2},{2,0},{4,6},{6,4},{8,10},{10,8},{12,14},{14,12},{1,3},{3,1},... | collective-permute-start | bytes 983048 | tf_op jit(solution)/shard_map/ppermute | solution.py:40
  47.2 23.9 %copy-start.3 = (s32[2,8]{1,0:T(2,128)S(1)}, s32[2,8]{1,0:T(2,128)}, u32[]{:S(2)}) copy-start(s32[2,8]{1,0:T(2,128)} %lengths.3) | copy-start | bytes 196
  47.2 23.9 %copy-start.5 = (s32[8]{0:T(128)S(1)}, s32[8]{0:T(128)}, u32[]{:S(2)}) copy-start(s32[8]{0:T(128)} %refs_3_.7) | copy-start | bytes 100
  47.2 9.9 %collective-permute-start.12 = (bf16[40,1024]{1,0:T(8,128)(2,1)S(1)}, bf16[40,1024]{1,0:T(8,128)(2,1)S(1)}, u32[]{:S(2)}, u32[]{:S(2)}) collective-permute-start(bf16[40,1024]{1,0:T(8,128)(2,1)S(1)} %fusion.13), channel_id=1, source_target_pairs={{0,4},{2,6},{4,0},{6,2},{8,12},{10,14},{12,8},{14,10},{1,5},{3,7},... | collective-permute-start | bytes 245768 | tf_op jit(solution)/shard_map/ppermute | solution.py:40
  47.4 9.8 %collective-permute-start.13 = (bf16[40,1024]{1,0:T(8,128)(2,1)S(1)}, bf16[40,1024]{1,0:T(8,128)(2,1)S(1)}, u32[]{:S(2)}, u32[]{:S(2)}) collective-permute-start(bf16[40,1024]{1,0:T(8,128)(2,1)S(1)} %fusion.13), channel_id=1, source_target_pairs={{0,8},{2,10},{4,12},{6,14},{8,0},{10,2},{12,4},{14,6},{1,9},{3,11}... | collective-permute-start | bytes 245768 | tf_op jit(solution)/shard_map/ppermute | solution.py:40
  49.7 7.5 %collective-permute-start.14 = (bf16[40,1024]{1,0:T(8,128)(2,1)S(1)}, bf16[40,1024]{1,0:T(8,128)(2,1)S(1)}, u32[]{:S(2)}, u32[]{:S(2)}) collective-permute-start(bf16[40,1024]{1,0:T(8,128)(2,1)S(1)} %fusion.13), channel_id=1, source_target_pairs={{0,12},{2,14},{4,8},{6,10},{8,4},{10,6},{12,0},{14,2},{1,13},{3,15... | collective-permute-start | bytes 245768 | tf_op jit(solution)/shard_map/ppermute | solution.py:40
  57.3 13.9 %collective-permute-start.22 = (bf16[4,40,1024]{2,1,0:T(8,128)(2,1)S(1)}, bf16[4,40,1024]{2,1,0:T(8,128)(2,1)S(1)}, u32[]{:S(2)}, u32[]{:S(2)}) collective-permute-start(bf16[4,40,1024]{2,1,0:T(8,128)(2,1)S(1)} %pad_maximum_fusion.refs_4_), channel_id=1, source_target_pairs={{0,2},{2,0},{4,6},{6,4},{8,10},{10,8},{12,14},{14,12},{1,3},{3,1},... | collective-permute-start | bytes 983048 | tf_op jit(solution)/shard_map/ppermute | solution.py:40
  57.7 4.5 %collective-permute-start.16 = (f16[40,1024]{1,0:T(8,128)(2,1)S(1)}, f16[40,1024]{1,0:T(8,128)(2,1)S(1)}, u32[]{:S(2)}, u32[]{:S(2)}) collective-permute-start(f16[40,1024]{1,0:T(8,128)(2,1)S(1)} %get-tuple-element.64), channel_id=1, source_target_pairs={{0,4},{2,6},{4,0},{6,2},{8,12},{10,14},{12,8},{14,10},{1,5},{3,7},... | collective-permute-start | bytes 245768 | tf_op jit(solution)/shard_map/ppermute | solution.py:40
  57.8 5.4 %collective-permute-start.17 = (f16[40,1024]{1,0:T(8,128)(2,1)S(1)}, f16[40,1024]{1,0:T(8,128)(2,1)S(1)}, u32[]{:S(2)}, u32[]{:S(2)}) collective-permute-start(f16[40,1024]{1,0:T(8,128)(2,1)S(1)} %get-tuple-element.65), channel_id=1, source_target_pairs={{0,8},{2,10},{4,12},{6,14},{8,0},{10,2},{12,4},{14,6},{1,9},{3,11}... | collective-permute-start | bytes 245768 | tf_op jit(solution)/shard_map/ppermute | solution.py:40
  59.1 7.5 %collective-permute-start.18 = (f16[40,1024]{1,0:T(8,128)(2,1)S(1)}, f16[40,1024]{1,0:T(8,128)(2,1)S(1)}, u32[]{:S(2)}, u32[]{:S(2)}) collective-permute-start(f16[40,1024]{1,0:T(8,128)(2,1)S(1)} %get-tuple-element.66), channel_id=1, source_target_pairs={{0,12},{2,14},{4,8},{6,10},{8,4},{10,6},{12,0},{14,2},{1,13},{3,15... | collective-permute-start | bytes 245768 | tf_op jit(solution)/shard_map/ppermute | solution.py:40
  66.7 12.3 %collective-permute-start.19 = (bf16[40,1024]{1,0:T(8,128)(2,1)S(1)}, bf16[40,1024]{1,0:T(8,128)(2,1)S(1)}, u32[]{:S(2)}, u32[]{:S(2)}) collective-permute-start(bf16[40,1024]{1,0:T(8,128)(2,1)S(1)} %fusion.6), channel_id=1, source_target_pairs={{0,4},{2,6},{4,0},{6,2},{8,12},{10,14},{12,8},{14,10},{1,5},{3,7},... | collective-permute-start | bytes 245768 | tf_op jit(solution)/shard_map/ppermute | solution.py:40
  66.8 12.2 %collective-permute-start.20 = (bf16[40,1024]{1,0:T(8,128)(2,1)S(1)}, bf16[40,1024]{1,0:T(8,128)(2,1)S(1)}, u32[]{:S(2)}, u32[]{:S(2)}) collective-permute-start(bf16[40,1024]{1,0:T(8,128)(2,1)S(1)} %fusion.6), channel_id=1, source_target_pairs={{0,8},{2,10},{4,12},{6,14},{8,0},{10,2},{12,4},{14,6},{1,9},{3,11}... | collective-permute-start | bytes 245768 | tf_op jit(solution)/shard_map/ppermute | solution.py:40
  69.5 9.5 %collective-permute-start.21 = (bf16[40,1024]{1,0:T(8,128)(2,1)S(1)}, bf16[40,1024]{1,0:T(8,128)(2,1)S(1)}, u32[]{:S(2)}, u32[]{:S(2)}) collective-permute-start(bf16[40,1024]{1,0:T(8,128)(2,1)S(1)} %fusion.6), channel_id=1, source_target_pairs={{0,12},{2,14},{4,8},{6,10},{8,4},{10,6},{12,0},{14,2},{1,13},{3,15... | collective-permute-start | bytes 245768 | tf_op jit(solution)/shard_map/ppermute | solution.py:40
  79.1 11.5 %collective-permute-start.23 = (bf16[4,40,1024]{2,1,0:T(8,128)(2,1)S(1)}, bf16[4,40,1024]{2,1,0:T(8,128)(2,1)S(1)}, u32[]{:S(2)}, u32[]{:S(2)}) collective-permute-start(bf16[4,40,1024]{2,1,0:T(8,128)(2,1)S(1)} %pad_maximum_fusion.1.refs_4_), channel_id=1, source_target_pairs={{0,2},{2,0},{4,6},{6,4},{8,10},{10,8},{12,14},{14,12},{1,3},{3,1},... | collective-permute-start | bytes 983048 | tf_op jit(solution)/shard_map/ppermute | solution.py:40
  82.2 22.2 %collective-permute-start.24 = (bf16[4,64,1152]{2,1,0:T(8,128)(2,1)S(1)}, bf16[4,64,1152]{2,1,0:T(8,128)(2,1)S(1)}, u32[]{:S(2)}, u32[]{:S(2)}) collective-permute-start(bf16[4,64,1152]{2,1,0:T(8,128)(2,1)S(1)} %attend.4), channel_id=1, source_target_pairs={{0,2},{2,0},{4,6},{6,4},{8,10},{10,8},{12,14},{14,12},{1,3},{3,1},... | collective-permute-start | bytes 1769480 | tf_op jit(solution)/shard_map/ppermute | solution.py:40
  98.6 20.1 %collective-permute-start.28 = (bf16[4,64,1152]{2,1,0:T(8,128)(2,1)S(1)}, bf16[4,64,1152]{2,1,0:T(8,128)(2,1)S(1)}, u32[]{:S(2)}, u32[]{:S(2)}) collective-permute-start(bf16[4,64,1152]{2,1,0:T(8,128)(2,1)S(1)} %attend.6), channel_id=1, source_target_pairs={{0,2},{2,0},{4,6},{6,4},{8,10},{10,8},{12,14},{14,12},{1,3},{3,1},... | collective-permute-start | bytes 1769480 | tf_op jit(solution)/shard_map/ppermute | solution.py:40
  105.8 14.4 %collective-permute-start.25 = (bf16[64,1152]{1,0:T(8,128)(2,1)S(1)}, bf16[64,1152]{1,0:T(8,128)(2,1)S(1)}, u32[]{:S(2)}, u32[]{:S(2)}) collective-permute-start(bf16[64,1152]{1,0:T(8,128)(2,1)S(1)} %get-tuple-element.77), channel_id=1, source_target_pairs={{0,4},{2,6},{4,0},{6,2},{8,12},{10,14},{12,8},{14,10},{1,5},{3,7},... | collective-permute-start | bytes 442376 | tf_op jit(solution)/shard_map/ppermute | solution.py:40
  105.9 18.6 %collective-permute-start.26 = (bf16[64,1152]{1,0:T(8,128)(2,1)S(1)}, bf16[64,1152]{1,0:T(8,128)(2,1)S(1)}, u32[]{:S(2)}, u32[]{:S(2)}) collective-permute-start(bf16[64,1152]{1,0:T(8,128)(2,1)S(1)} %get-tuple-element.78), channel_id=1, source_target_pairs={{0,8},{2,10},{4,12},{6,14},{8,0},{10,2},{12,4},{14,6},{1,9},{3,11}... | collective-permute-start | bytes 442376 | tf_op jit(solution)/shard_map/ppermute | solution.py:40
  106.0 18.5 %collective-permute-start.27 = (bf16[64,1152]{1,0:T(8,128)(2,1)S(1)}, bf16[64,1152]{1,0:T(8,128)(2,1)S(1)}, u32[]{:S(2)}, u32[]{:S(2)}) collective-permute-start(bf16[64,1152]{1,0:T(8,128)(2,1)S(1)} %get-tuple-element.79), channel_id=1, source_target_pairs={{0,12},{2,14},{4,8},{6,10},{8,4},{10,6},{12,0},{14,2},{1,13},{3,15... | collective-permute-start | bytes 442376 | tf_op jit(solution)/shard_map/ppermute | solution.py:40
  120.0 6.6 %collective-permute-start.29 = (bf16[64,1152]{1,0:T(8,128)(2,1)S(1)}, bf16[64,1152]{1,0:T(8,128)(2,1)S(1)}, u32[]{:S(2)}, u32[]{:S(2)}) collective-permute-start(bf16[64,1152]{1,0:T(8,128)(2,1)S(1)} %get-tuple-element.82), channel_id=1, source_target_pairs={{0,4},{2,6},{4,0},{6,2},{8,12},{10,14},{12,8},{14,10},{1,5},{3,7},... | collective-permute-start | bytes 442376 | tf_op jit(solution)/shard_map/ppermute | solution.py:40
  120.1 9.3 %collective-permute-start.30 = (bf16[64,1152]{1,0:T(8,128)(2,1)S(1)}, bf16[64,1152]{1,0:T(8,128)(2,1)S(1)}, u32[]{:S(2)}, u32[]{:S(2)}) collective-permute-start(bf16[64,1152]{1,0:T(8,128)(2,1)S(1)} %get-tuple-element.83), channel_id=1, source_target_pairs={{0,8},{2,10},{4,12},{6,14},{8,0},{10,2},{12,4},{14,6},{1,9},{3,11}... | collective-permute-start | bytes 442376 | tf_op jit(solution)/shard_map/ppermute | solution.py:40
  120.2 9.2 %collective-permute-start.31 = (bf16[64,1152]{1,0:T(8,128)(2,1)S(1)}, bf16[64,1152]{1,0:T(8,128)(2,1)S(1)}, u32[]{:S(2)}, u32[]{:S(2)}) collective-permute-start(bf16[64,1152]{1,0:T(8,128)(2,1)S(1)} %get-tuple-element.84), channel_id=1, source_target_pairs={{0,12},{2,14},{4,8},{6,10},{8,4},{10,6},{12,0},{14,2},{1,13},{3,15... | collective-permute-start | bytes 442376 | tf_op jit(solution)/shard_map/ppermute | solution.py:40

commit v5 on v4

--- a/solution.py
+++ b/solution.py
@@ -13,8 +13,7 @@
 NEG = -1e30
 LOG2E = 1.4426950408889634
 CHUNK = 512
-LONG = 1024
-ROUND = 16
+ROUND = 32
 EXTRA = 128
 SLOT = 32
 BIG = 2.0 ** 100
@@ -40,22 +39,37 @@
         return lax.ppermute(value, "seq", pairs)
 
 
-def split_kernel(grid, depth, place, hidden_ref, handed_ref, *out_refs):
+class Facts:
+    def __init__(self, n, meta):
+        self.n, self.meta = n, meta
+        self.section, self.shard = meta[0], meta[1]
+
+    def length(self, block):
+        return self.meta[2 + self.section * self.n + block]
+
+    def prompt(self, block):
+        return self.meta[2 + (2 + self.section) * self.n + block]
+
+    def prompt_length(self, prompt):
+        return self.meta[2 + 4 * self.n + prompt]
+
+
+def split_kernel(grid, depth, meta, hidden_ref, handed_ref, *out_refs):
     for kx in range(grid.xs):
         for kz in range(grid.zs):
-            at = pl.multiple_of(grid.owner(place[1], kx, kz) * depth, HD)
+            at = pl.multiple_of(grid.owner(meta[1], kx, kz) * depth, HD)
             total = hidden_ref[0, :, pl.ds(at, depth)].astype(jnp.float32) + handed_ref[
                 0, :, pl.ds(at, depth)
             ].astype(jnp.float32)
             out_refs[kx * grid.zs + kz][...] = total.astype(jnp.bfloat16)
 
 
-def split(grid, place, hidden, handed, depth):
+def split(grid, meta, hidden, handed, depth):
     bl = hidden.shape[1]
     if depth % HD:
         total = (hidden[0].astype(jnp.float32) + handed[0].astype(jnp.float32)).astype(jnp.bfloat16)
         return [
-            lax.dynamic_slice_in_dim(total, grid.owner(place[1], kx, kz) * depth, depth, 1)
+            lax.dynamic_slice_in_dim(total, grid.owner(meta[1], kx, kz) * depth, depth, 1)
             for kx in range(grid.xs) for kz in range(grid.zs)
         ]
     whole = pl.BlockSpec(hidden.shape, lambda i, *m: (0, 0, 0))
@@ -70,7 +84,7 @@
         out_shape=[jax.ShapeDtypeStruct((bl, depth), jnp.bfloat16)] * grid.n,
         compiler_params=pltpu.CompilerParams(vmem_limit_bytes=16 * MIB),
         name="split",
-    )(place, hidden, handed)
+    )(meta, hidden, handed)
 
 
 def run_moves(moves):
@@ -110,17 +124,17 @@
     return [pltpu.with_memory_space_constraint(array, pltpu.VMEM) for array in out]
 
 
-def fetch_cache_kernel(chunk, width, first, place, prompts, prompt_lengths, cache_ref, kv_ref, sem):
+def fetch_cache_kernel(n, chunk, width, first, meta, cache_ref, kv_ref, sem):
     count, tile_len = kv_ref.shape[:2]
-    section, shard = place[0], place[1]
+    facts = Facts(n, meta)
     moves = []
     for p in range(count):
-        asked = prompts[section, 0] == p
-        for b in range(1, prompts.shape[1]):
-            asked = asked | (prompts[section, b] == p)
+        asked = facts.prompt(0) == p
+        for b in range(1, n):
+            asked = asked | (facts.prompt(b) == p)
         for c in range(tile_len // chunk):
             at = pl.ds(c * chunk, chunk)
-            needed = asked & (prompt_lengths[p] > shard * tile_len + c * chunk)
+            needed = asked & (facts.prompt_length(p) > facts.shard * tile_len + c * chunk)
             moves.append((needed, pltpu.make_async_copy(
                 cache_ref.at[0, p, at, pl.ds(first * width, width)], kv_ref.at[p, at],
                 sem.at[p, c],
@@ -128,14 +142,14 @@
     run_moves(moves)
 
 
-def fetch_cache(place, prompts, prompt_lengths, cache, width, first):
+def fetch_cache(n, meta, cache, width, first):
     count, tile_len = cache.shape[1:3]
     chunk = min(CHUNK, tile_len)
     shape = (count, tile_len, width)
     out = pl.pallas_call(
-        functools.partial(fetch_cache_kernel, chunk, width, first),
+        functools.partial(fetch_cache_kernel, n, chunk, width, first),
         grid_spec=pltpu.PrefetchScalarGridSpec(
-            num_scalar_prefetch=3,
+            num_scalar_prefetch=1,
             grid=(1,),
             in_specs=[pl.BlockSpec(memory_space=pltpu.HBM)],
             out_specs=pl.BlockSpec(memory_space=pltpu.VMEM),
@@ -147,21 +161,22 @@
             flops=0, bytes_accessed=2 * math.prod(shape), transcendentals=0
         ),
         name="fetch_cache",
-    )(place, prompts, prompt_lengths, pltpu.with_memory_space_constraint(cache, pltpu.HBM))
+    )(meta, pltpu.with_memory_space_constraint(cache, pltpu.HBM))
     return pltpu.with_memory_space_constraint(out, pltpu.VMEM)
 
 
-def project_kernel(grid, bl, share, place, lengths, *refs):
+def project_kernel(grid, bl, share, meta, *refs):
     x_refs, w_ref, refs = refs[:grid.n], refs[grid.n], refs[grid.n + 1:]
     out_refs, (xp_ref, starts) = refs[:-2], refs[-2:]
 
     @pl.when(pl.program_id(0) == 0)
     def _():
-        section, shard = place[0], place[1]
+        facts = Facts(grid.n, meta)
+        shard = facts.shard
         offset = jnp.int32(0)
         for b in range(grid.n):
             starts[b] = offset
-            offset = offset + lengths[section, b]
+            offset = offset + facts.length(b)
         lane = lax.broadcasted_iota(jnp.int32, (8, grid.n * bl), 1)
         target = jnp.full(lane.shape, -1, jnp.int32)
         owners = [
@@ -169,7 +184,7 @@
         ]
         for k, b in enumerate(owners):
             order = lane - k * bl
-            used = (order >= 0) & (order < lengths[section, b])
+            used = (order >= 0) & (order < facts.length(b))
             target = jnp.where(used, order + starts[b], target)
         row = lax.broadcasted_iota(jnp.int32, (share, grid.n * bl), 0)
         target = jnp.broadcast_to(target[:1], row.shape)
@@ -189,7 +204,7 @@
             out_ref[...] = result[kx * rows:(kx + 1) * rows]
 
 
-def project(grid, place, lengths, xs, w, bl, share, chunks):
+def project(grid, meta, xs, w, bl, share, chunks):
     k, cols = w.shape[1:]
     rows = grid.n * share
     tile = cols // chunks
@@ -197,7 +212,7 @@
     return pl.pallas_call(
         functools.partial(project_kernel, grid, bl, share),
         grid_spec=pltpu.PrefetchScalarGridSpec(
-            num_scalar_prefetch=2,
+            num_scalar_prefetch=1,
             grid=(chunks,),
             in_specs=[pl.BlockSpec((bl, k), lambda j, *m: (0, 0))] * grid.n
             + [pl.BlockSpec((1, k, tile), lambda j, *m: (0, 0, j))],
@@ -213,7 +228,7 @@
             transcendentals=0,
         ),
         name="project",
-    )(place, lengths, *xs, w)
+    )(meta, *xs, w)
 
 
 def encode(lse):
@@ -270,11 +285,11 @@
     )(*sources)
 
 
-def attend_kernel(grid, kx, bl, share, heads, tile_len, *refs):
-    place, lengths, prompts, prompt_lengths = refs[:4]
-    near_ref, far_refs = refs[4], refs[5:4 + grid.xs]
-    kv_ref, own_ref, out_ref, q32_ref, acc_ref, m_ref = refs[4 + grid.xs:]
-    shard = place[1]
+def attend_kernel(grid, kx, bl, share, first, heads, tile_len, meta, *refs):
+    near_ref, far_refs = refs[0], refs[1:grid.xs]
+    kv_ref, own_ref, out_ref, q32_ref, acc_ref, m_ref = refs[grid.xs:]
+    facts = Facts(grid.n, meta)
+    shard = facts.shard
     rows = grid.n * share
     for fx in range(grid.xs):
         for fz in range(grid.zs):
@@ -287,7 +302,7 @@
 
     def one(kz, carry):
         attend_block(
-            grid, kx, bl, heads, tile_len, kz, place, lengths, prompts, prompt_lengths,
+            grid, kx, bl, first, heads, tile_len, kz, facts,
             kv_ref, own_ref, out_ref, q32_ref, acc_ref, m_ref,
         )
         return carry
@@ -295,15 +310,14 @@
     lax.fori_loop(0, grid.zs, one, 0)
 
 
-def attend_block(grid, kx, bl, heads, tile_len, step, place, lengths, prompts, prompt_lengths,
+def attend_block(grid, kx, bl, first, heads, tile_len, step, facts,
                  kv_ref, own_ref, out_ref, q32_ref, acc_ref, m_ref):
-    section, shard = place[0], place[1]
-    block = grid.owner(shard, kx, step)
+    block = grid.owner(facts.shard, kx, step)
     offset = jnp.int32(0)
     for b in range(grid.n):
-        offset = offset + jnp.where(b < block, lengths[section, b], 0)
-    prompt = prompts[section, block]
-    valid = jnp.clip(prompt_lengths[prompt] - shard * tile_len, 0, tile_len)
+        offset = offset + jnp.where(b < block, facts.length(b), 0)
+    prompt = facts.prompt(block)
+    valid = jnp.clip(facts.prompt_length(prompt) - facts.shard * tile_len, 0, tile_len)
     c2 = LOG2E / math.sqrt(HD)
     chunk = min(CHUNK, tile_len)
     width = heads * GR * HD
@@ -358,56 +372,40 @@
 
         lax.fori_loop(0, (valid + chunk - 1) // chunk, one, 0)
 
-    length = lengths[section, block]
+    length = facts.length(block)
 
     @pl.when(valid == 0)
     def _():
         acc_ref[...] = jnp.zeros_like(acc_ref)
         m_ref[...] = jnp.full_like(m_ref, NEG)
 
-    long = min(LONG, tile_len)
-    for used in range(ROUND, bl + 1, ROUND):
-        @pl.when((valid == tile_len) & (length <= used) & (length > used - ROUND))
-        def _(used=used):
-            items = [(g, c) for g in range(heads) for c in range(tile_len // long)]
-            q = [group(g, used) for g in range(heads)]
-            peaks = [None] * heads
-            accs = [None] * heads
-            ahead = dot_nt(q[0], keys(0, 0, long))
-            for i, (g, c) in enumerate(items):
-                s = ahead
-                if i + 1 < len(items):
-                    ng, nc = items[i + 1]
-                    ahead = dot_nt(q[ng], keys(ng, nc * long, long))
-                if c == 0:
-                    peaks[g] = jnp.max(s, axis=1, keepdims=True)
-                p = jnp.exp2((s - peaks[g]) * c2).astype(jnp.bfloat16)
-                part = sums(p, vals(g, c * long, long))
-                accs[g] = part if c == 0 else accs[g] + part
-            for g in range(heads):
-                put(g, used, accs[g], peaks[g])
-
-    @pl.when((valid < tile_len) & (valid > 0))
-    def _():
-        def scores(g, at):
-            s = dot_nt(group(g, bl), keys(g, at, chunk))
-            here = lax.broadcasted_iota(jnp.int32, s.shape, 1) + at
-            return jnp.where(here < valid, s, NEG)
-
+    def single_pass(used, count):
+        items = [(g, c) for c in range(count) for g in range(heads)]
+        q = [group(g, used) for g in range(heads)]
+        peaks = [None] * heads
+        accs = [None] * heads
+        ahead = dot_nt(q[0], keys(0, 0, chunk))
+        for i, (g, c) in enumerate(items):
+            s = ahead
+            if i + 1 < len(items):
+                ng, nc = items[i + 1]
+                ahead = dot_nt(q[ng], keys(ng, nc * chunk, chunk))
+            if c == count - 1:
+                here = lax.broadcasted_iota(jnp.int32, s.shape, 1) + c * chunk
+                s = jnp.where(here < valid, s, NEG)
+            if c == 0:
+                peaks[g] = jnp.max(s, axis=1, keepdims=True)
+            p = jnp.exp2((s - peaks[g]) * c2).astype(jnp.bfloat16)
+            part = sums(p, vals(g, c * chunk, chunk))
+            accs[g] = part if c == 0 else accs[g] + part
         for g in range(heads):
-            s = scores(g, 0)
-            m = jnp.max(s, axis=1, keepdims=True)
-            p = jnp.exp2((s - m) * c2).astype(jnp.bfloat16)
-            put(g, bl, sums(p, vals(g, 0, chunk)), m)
-
-        def one(c, carry):
-            at = pl.multiple_of(c * chunk, chunk)
-            for g in range(heads):
-                p = jnp.exp2((scores(g, at) - m_ref[g][:, :1]) * c2).astype(jnp.bfloat16)
-                acc_ref[g] += sums(p, vals(g, at, chunk))
-            return carry
-
-        lax.fori_loop(1, (valid + chunk - 1) // chunk, one, 0)
+            put(g, used, accs[g], peaks[g])
+
+    for count in range(1, tile_len // chunk + 1):
+        for used in range(ROUND, bl + 1, ROUND):
+            some_keys = (valid > (count - 1) * chunk) & (valid <= count * chunk)
+            some_rows = (length > used - ROUND) & (length <= used)
+            pl.when(some_keys & some_rows)(functools.partial(single_pass, used, count))
 
     top = jnp.where(acc_ref[:, :, HD:] < BIG, 0.0, 1.0)
 
@@ -419,41 +417,42 @@
         @pl.when(step == 0)
         def _():
             for g in range(heads):
-                base = g * 2 * HD
+                base = (first + g) * 2 * HD
                 s = dot_nt(group(g, bl), own_ref[0, :, base:base + HD])
                 row = lax.broadcasted_iota(jnp.int32, s.shape, 0) % bl
                 col = lax.broadcasted_iota(jnp.int32, s.shape, 1)
                 update(g, s, col <= row, own_ref[0, :, base + HD:base + 2 * HD])
 
     lane = lax.broadcasted_iota(jnp.int32, (bl, EXTRA), 1)
-    lse_tile = jnp.zeros((bl, EXTRA), jnp.float32)
+    total_tile = jnp.zeros((bl, EXTRA), jnp.float32)
+    m_tile = jnp.zeros((bl, EXTRA), jnp.float32)
     for g in range(heads):
         total = acc_ref[g][:, HD:]
-        some = total > 0.0
-        safe = jnp.where(some, total, 1.0)
-        out = (acc_ref[g][:, :HD] / safe).astype(jnp.bfloat16)
-        lse = jnp.where(some, m_ref[g] * c2 + jnp.log2(safe), NEG)
+        out = (acc_ref[g][:, :HD] / jnp.where(total > 0.0, total, 1.0)).astype(jnp.bfloat16)
         for r in range(GR):
             h = g * GR + r
-            out_ref[step, :, h * HD:(h + 1) * HD] = out[r * bl:(r + 1) * bl]
-            lse_tile = jnp.where(lane == h, lse[r * bl:(r + 1) * bl], lse_tile)
-    out_ref[step, :, width:] = encode(lse_tile)
-
-
-def attend(grid, kx, place, lengths, prompts, prompt_lengths, near, fars, cache, own, first, heads):
+            at = slice(r * bl, (r + 1) * bl)
+            out_ref[step, :, h * HD:(h + 1) * HD] = out[at]
+            total_tile = jnp.where(lane == h, total[at], total_tile)
+            m_tile = jnp.where(lane == h, m_ref[g, at], m_tile)
+    some = total_tile > 0.0
+    lse = m_tile * c2 + jnp.log2(jnp.where(some, total_tile, 1.0))
+    out_ref[step, :, width:] = encode(jnp.where(some, lse, NEG))
+
+
+def attend(grid, kx, meta, near, fars, cache, own, first, heads):
     zs, share, cols = near.shape
     bl = own.shape[1]
     tile_len = cache.shape[1]
     width = heads * GR * HD + EXTRA
+    whole = pl.BlockSpec(memory_space=pltpu.VMEM)
     return pl.pallas_call(
-        functools.partial(attend_kernel, grid, kx, bl, share, heads, tile_len),
+        functools.partial(attend_kernel, grid, kx, bl, share, first, heads, tile_len),
         grid_spec=pltpu.PrefetchScalarGridSpec(
-            num_scalar_prefetch=4,
+            num_scalar_prefetch=1,
             grid=(1,),
-            in_specs=[pl.BlockSpec((zs, share, cols), lambda i, *m: (0, 0, 0))] * grid.xs
-            + [pl.BlockSpec(memory_space=pltpu.VMEM)]
-            + [pl.BlockSpec((1, bl, heads * 2 * HD), lambda i, *m: (0, 0, first // heads))],
-            out_specs=pl.BlockSpec((zs, bl, width), lambda i, *m: (0, 0, 0)),
+            in_specs=[whole] * (grid.xs + 2),
+            out_specs=whole,
             scratch_shapes=[
                 pltpu.VMEM((grid.n * share + bl + 8, cols), jnp.float32),
                 pltpu.VMEM((heads, GR * bl, 2 * HD), jnp.float32),
@@ -468,37 +467,40 @@
             transcendentals=zs * bl * heads * GR * tile_len,
         ),
         name="attend",
-    )(place, lengths, prompts, prompt_lengths, near, *fars, cache, own)
-
-
-def finish_kernel(chunks, zs, heads, bl, place, lengths, *refs):
-    out_ref = refs[-1]
-    length = lengths[place[0], place[1]]
+    )(meta, near, *fars, cache, own)
+
+
+def finish_kernel(n, heads, bl, done, meta, *refs):
+    sources, out_ref = refs[:-1], refs[-1]
+    pieces = sources[done:]
+    facts = Facts(n, meta)
+    length = facts.length(facts.shard)
     row = lax.broadcasted_iota(jnp.int32, (bl, HD), 0)
     width = heads * GR * HD
-    for c in range(chunks):
-        pieces = refs[c * zs:(c + 1) * zs]
-        parts, _ = merge(pieces, heads * GR)
-        for h in range(heads * GR):
-            at = c * width + h * HD
-            out_ref[0, :, at:at + HD] = jnp.where(row < length, parts[h], 0.0).astype(jnp.bfloat16)
-
-
-def finish(place, lengths, pieces, chunks, zs, heads):
+    for c in range(done):
+        out_ref[0, :, c * width:(c + 1) * width] = sources[c][0]
+    parts, _ = merge(pieces, heads * GR)
+    for h in range(heads * GR):
+        at = done * width + h * HD
+        out_ref[0, :, at:at + HD] = jnp.where(row < length, parts[h], 0.0).astype(jnp.bfloat16)
+
+
+def finish(n, meta, done, pieces, heads):
     bl = pieces[0].shape[0]
-    cols = chunks * heads * GR * HD
+    whole = pl.BlockSpec(memory_space=pltpu.VMEM)
+    sources = list(done) + list(pieces)
     return pl.pallas_call(
-        functools.partial(finish_kernel, chunks, zs, heads, bl),
+        functools.partial(finish_kernel, n, heads, bl, len(done)),
         grid_spec=pltpu.PrefetchScalarGridSpec(
-            num_scalar_prefetch=2,
+            num_scalar_prefetch=1,
             grid=(1,),
-            in_specs=[pl.BlockSpec(piece.shape, lambda i, *m: (0, 0)) for piece in pieces],
-            out_specs=pl.BlockSpec((1, bl, cols), lambda i, *m: (0, 0, 0)),
-        ),
-        out_shape=jax.ShapeDtypeStruct((1, bl, cols), jnp.bfloat16),
+            in_specs=[whole] * len(sources),
+            out_specs=whole,
+        ),
+        out_shape=jax.ShapeDtypeStruct((1, bl, (len(done) + 1) * heads * GR * HD), jnp.bfloat16),
         compiler_params=pltpu.CompilerParams(vmem_limit_bytes=16 * MIB),
         name="finish",
-    )(place, lengths, *pieces)
+    )(meta, *sources)
 
 
 def shards(
@@ -519,18 +521,20 @@
     heads = local_kv // chunks
     part_cols = heads * GR * HD
     place = jnp.stack([lax.axis_index("sec"), lax.axis_index("seq")]).astype(jnp.int32)
-    prompts = block_prompts[:, :, 0]
+    meta = jnp.concatenate(
+        [place, response_lengths.reshape(-1), block_prompts.reshape(-1), prompt_lengths]
+    )
 
     def after(value, done):
         return lax.optimization_barrier((value, done))[0]
 
     def fetched(c):
-        return fetch_cache(place, prompts, prompt_lengths, prompt_cache, heads * 2 * HD, c)
+        return fetch_cache(grid.n, meta, prompt_cache, heads * 2 * HD, c)
 
     handed = lax.ppermute(carried, "sec", [(0, 1)])
     depth = query_weight.shape[1]
     hidden = hidden_rows if depth % HD else fetch([hidden_rows])[0]
-    slices = split(grid, place, hidden, handed, depth)
+    slices = split(grid, meta, hidden, handed, depth)
     weight, own = fetch([query_weight, response_cache])
     x = [slices[0]] + [None] * (grid.n - 1)
     for kz in reversed(range(grid.zs)):
@@ -538,7 +542,7 @@
             k = kx * grid.zs + kz
             if k:
                 x[k] = grid.swap(slices[k], kx, kz)
-    part = project(grid, place, response_lengths, x, weight, bl, share, chunks)
+    part = project(grid, meta, x, weight, bl, share, chunks)
     part = [piece.reshape(grid.zs, share, part_cols) for piece in part]
     part = [part[c * grid.xs:(c + 1) * grid.xs] for c in range(chunks)]
 
@@ -566,8 +570,7 @@
 
     def call(c, kx, queries):
         return attend(
-            grid, kx, place, response_lengths, prompts, prompt_lengths, queries[0], queries[1:],
-            caches[c], own, c * heads, heads,
+            grid, kx, meta, queries[0], queries[1:], caches[c], own, c * heads, heads,
         )
 
     def call_far(c, queries):
@@ -605,11 +608,13 @@
         held = after(held, outs)
     merged = merge_column([held] + mets, heads * GR)
     pieces = send_z(merged)
-    if chunks > 1:
-        later[0] = after(later[0], merged)
-        held = call(1, 0, later)
-        pieces += send_z(merge_column([held] + later_mets, heads * GR))
-    return finish(place, response_lengths, pieces, chunks, grid.zs, heads)
+    if chunks == 1:
+        return finish(grid.n, meta, [], pieces, heads)
+    later[0] = after(later[0], merged)
+    held = call(1, 0, later)
+    done = finish(grid.n, meta, [], pieces, heads)
+    pieces = send_z(merge_column([held] + later_mets, heads * GR))
+    return finish(grid.n, meta, [done], pieces, heads)
 
 
 def solution(mesh):

time: 129 us -> 126 us (0.977); the launches traced: 132 us -> 125 us
  starting transfers between devices: 56.7 us -> 52.8 us
  Pallas kernels: 54.8 us -> 52 us
  waiting for transfers between devices: 17.2 us -> 15.5 us
  other arithmetic: 0.71 us -> 2 us
    ppermute x31, starting transfers between devices: 54.3 us -> 50.4 us  [swap(): return lax.ppermute(value, 'seq', pairs)]
    pallas_call x7 -> x8, Pallas kernels: 45.6 us -> 42.9 us  [the longest x4 30.5 us: attend(): pl.pallas_call(functools.partial(attend_kernel, grid, kx, bl, share, firs...]
    unnamed x12 -> x1, local copies, waits for them, and re-layouts: 2.03 us -> 0.58 us
    unnamed x0 -> x1, other arithmetic: none -> 1.37 us
  transfers between devices with their start and end apart: 32 -> 32, of which waited for: 11 -> 9; matrix products, arithmetic and copies ran while one was open for 0% -> 3% of each run, Pallas kernels for 37% -> 38%
where the time goes in v5:
time: 126 us; the launch traced here: 125 us
  starting transfers between devices  52.8 us (42%)
  Pallas kernels  52 us (41%)
  waiting for transfers between devices  15.5 us (12%)
  local copies, waits for them, and re-layouts  2.16 us (2%)
  other arithmetic  2 us (2%)
    ppermute x31, starting transfers between devices, swap(): return lax.ppermute(value, 'seq', pairs)  50.4 us
    pallas_call x4, Pallas kernels, attend(): pl.pallas_call(functools.partial(attend_kernel, grid, kx, bl, share, firs...  30.5 us
    ppermute x31, waiting for transfers between devices, swap(): return lax.ppermute(value, 'seq', pairs)  15.5 us
    pallas_call x2, Pallas kernels, fetch_cache(): pl.pallas_call(functools.partial(fetch_cache_kernel, n, chunk, width, fir...  9.65 us
    pallas_call x2, Pallas kernels, fetch(): pl.pallas_call(fetch_kernel, in_specs=[anywhere] * len(arrays), out_specs...  2.85 us
    pallas_call x2, Pallas kernels, merge_column(): pl.pallas_call(functools.partial(merge_kernel, zs, heads), out_shape=[jax...  2.83 us
    pallas_call x2, Pallas kernels, finish(): pl.pallas_call(functools.partial(finish_kernel, n, heads, bl, len(done)),...  2.75 us
    pallas_call x1, Pallas kernels, project(): pl.pallas_call(functools.partial(project_kernel, grid, bl, share), grid_s...  2.72 us
  transfers between devices with their start and end apart: 32, of which 9 were waited for; matrix products, arithmetic and copies ran while one was open for 3% of the time, Pallas kernels for 38%

profile of v5, /device:TPU:0, one launch (start us, length us, event | category | flops | bytes accessed | tf_op | source)
XLA Modules:
  0.0 124.7 jit_solution(13656919115084549875)
XLA Ops:
  0.0 2.4 %collective-permute-start = (bf16[1,64,5120]{2,1,0:T(8,128)(2,1)}, bf16[1,64,5120]{2,1,0:T(8,128)(2,1)S(1)}, u32[]{:S(2)}, u32[]{:S(2)}) collective-permute-start(bf16[1,64,5120]{2,1,0:T(8,128)(2,1)} %param.9), channel_id=1, source_target_pairs={{0,16},{1,17},{2,18},{3,19},{4,20},{5,21},{6,22},{7,23},{8,24},{9,... | collective-permute-start | bytes 1966088 | tf_op jit(solution)/shard_map/ppermute | solution.py:534
  3.0 1.4 %reduce.3 = s32[2,8]{1,0:T(2,128)S(1)} reduce(s32[2,8,1]{1,2,0:T(1,128)} %param.15, s32[]{:T(128)} %broadcast.41), dimensions={2}, to_apply=%param.15.reduce_sub_computation.3 | reduce | bytes 132 | tf_op args[7]
  4.4 0.8 reshape.38
  5.2 1.1 fetch.2.hidden_ref
  6.3 0.7 concatenate.3.meta
  7.0 0.7 split.1
  7.8 2.5 %collective-permute-start.1 = (bf16[64,640]{1,0:T(8,128)(2,1)S(1)}, bf16[64,640]{1,0:T(8,128)(2,1)S(1)}, u32[]{:S(2)}, u32[]{:S(2)}) collective-permute-start(bf16[64,640]{1,0:T(8,128)(2,1)S(1)} %get-tuple-element.46), channel_id=1, source_target_pairs={{0,4},{2,6},{4,0},{6,2},{8,12},{10,14},{12,8},{14,10},{1,5},{3,7},... | collective-permute-start | bytes 245768 | tf_op jit(solution)/shard_map/ppermute | solution.py:39
  10.2 2.6 %collective-permute-start.2 = (bf16[64,640]{1,0:T(8,128)(2,1)S(1)}, bf16[64,640]{1,0:T(8,128)(2,1)S(1)}, u32[]{:S(2)}, u32[]{:S(2)}) collective-permute-start(bf16[64,640]{1,0:T(8,128)(2,1)S(1)} %get-tuple-element.47), channel_id=1, source_target_pairs={{0,8},{2,10},{4,12},{6,14},{8,0},{10,2},{12,4},{14,6},{1,9},{3,11}... | collective-permute-start | bytes 245768 | tf_op jit(solution)/shard_map/ppermute | solution.py:39
  12.8 1.7 %collective-permute-start.4 = (bf16[64,640]{1,0:T(8,128)(2,1)S(1)}, bf16[64,640]{1,0:T(8,128)(2,1)S(1)}, u32[]{:S(2)}, u32[]{:S(2)}) collective-permute-start(bf16[64,640]{1,0:T(8,128)(2,1)S(1)} %get-tuple-element.49), channel_id=1, source_target_pairs={{0,2},{2,0},{4,6},{6,4},{8,10},{10,8},{12,14},{14,12},{1,3},{3,1},... | collective-permute-start | bytes 245768 | tf_op jit(solution)/shard_map/ppermute | solution.py:39
  14.5 0.6 collective-permute-start.5
  15.2 4.4 %collective-permute-start.6 = (bf16[64,640]{1,0:T(8,128)(2,1)S(1)}, bf16[64,640]{1,0:T(8,128)(2,1)S(1)}, u32[]{:S(2)}, u32[]{:S(2)}) collective-permute-start(bf16[64,640]{1,0:T(8,128)(2,1)S(1)} %get-tuple-element.51), channel_id=1, source_target_pairs={{0,10},{2,8},{4,14},{6,12},{8,2},{10,0},{12,6},{14,4},{1,11},{3,9}... | collective-permute-start | bytes 245768 | tf_op jit(solution)/shard_map/ppermute | solution.py:39
  19.6 4.9 %collective-permute-start.7 = (bf16[64,640]{1,0:T(8,128)(2,1)S(1)}, bf16[64,640]{1,0:T(8,128)(2,1)S(1)}, u32[]{:S(2)}, u32[]{:S(2)}) collective-permute-start(bf16[64,640]{1,0:T(8,128)(2,1)S(1)} %get-tuple-element.52), channel_id=1, source_target_pairs={{0,14},{2,12},{4,10},{6,8},{8,6},{10,4},{12,2},{14,0},{1,15},{3,13... | collective-permute-start | bytes 245768 | tf_op jit(solution)/shard_map/ppermute | solution.py:39
  24.5 1.8 %fetch.3 = (bf16[1,640,2048]{2,1,0:T(8,128)(2,1)S(1)}, bf16[1,64,1024]{2,1,0:T(8,128)(2,1)S(1)}) custom-call(bf16[1,640,2048]{2,1,0:T(8,128)(2,1)} %refs_0_.3, bf16[1,64,1024]{2,1,0:T(8,128)(2,1)} %refs_1_.1), custom_call_target="tpu_custom_call" | custom-call | bytes 2752512 | tf_op jit(solution)/shard_map/fetch/pallas_call | solution.py:114
  26.3 0.7 collective-permute-done.7.refs_7_
  27.0 2.7 %project.1 = (f32[160,1024]{1,0:T(8,128)S(1)}, f32[160,1024]{1,0:T(8,128)S(1)}, f32[160,1024]{1,0:T(8,128)S(1)}, f32[160,1024]{1,0:T(8,128)S(1)}) custom-call(s32[42]{0:T(128)S(1)} %concatenate.3.meta, bf16[64,640]{1,0:T(8,128)(2,1)S(1)} %get-tuple-element.45.refs_0_, bf16[64,640]{1,0:T(8,128)(2,1)S(1)} %collective-permute-done.1.refs_1_, ...), custom_call_target="tpu_custom_call" | custom-call | flops 838860800 | bytes 5242880 | tf_op jit(solution)/shard_map/project/pallas_call | solution.py:212
  29.8 1.7 %collective-permute-start.8 = (f16[4,40,1024]{2,1,0:T(8,128)(2,1)S(1)}, f16[4,40,1024]{2,1,0:T(8,128)(2,1)S(1)}, u32[]{:S(2)}, u32[]{:S(2)}) collective-permute-start(f16[4,40,1024]{2,1,0:T(8,128)(2,1)S(1)} %bitcast.50), channel_id=1, source_target_pairs={{0,2},{2,0},{4,6},{6,4},{8,10},{10,8},{12,14},{14,12},{1,3},{3,1},... | collective-permute-start | bytes 983048 | tf_op jit(solution)/shard_map/ppermute | solution.py:39
  31.5 4.8 %fetch_cache.2.refs_2_ = bf16[8,2048,512]{2,1,0:T(8,128)(2,1)S(1)} custom-call(s32[42]{0:T(128)S(1)} %concatenate.3.meta, bf16[1,8,2048,1024]{3,2,1,0:T(8,128)(2,1)} %cache_ref.3), custom_call_target="tpu_custom_call" | custom-call | bytes 16777216 | tf_op jit(solution)/shard_map/fetch_cache/pallas_call | solution.py:149
  37.1 2.5 %collective-permute-start.10 = (f16[40,1024]{1,0:T(8,128)(2,1)S(1)}, f16[40,1024]{1,0:T(8,128)(2,1)S(1)}, u32[]{:S(2)}, u32[]{:S(2)}) collective-permute-start(f16[40,1024]{1,0:T(8,128)(2,1)S(1)} %get-tuple-element.90), channel_id=1, source_target_pairs={{0,8},{2,10},{4,12},{6,14},{8,0},{10,2},{12,4},{14,6},{1,9},{3,11}... | collective-permute-start | bytes 245768 | tf_op jit(solution)/shard_map/ppermute | solution.py:39
  39.7 1.6 %collective-permute-start.11 = (f16[40,1024]{1,0:T(8,128)(2,1)S(1)}, f16[40,1024]{1,0:T(8,128)(2,1)S(1)}, u32[]{:S(2)}, u32[]{:S(2)}) collective-permute-start(f16[40,1024]{1,0:T(8,128)(2,1)S(1)} %get-tuple-element.89), channel_id=1, source_target_pairs={{0,12},{2,14},{4,8},{6,10},{8,4},{10,6},{12,0},{14,2},{1,13},{3,15... | collective-permute-start | bytes 245768 | tf_op jit(solution)/shard_map/ppermute | solution.py:39
  41.3 1.8 %collective-permute-start.15 = (f16[4,40,1024]{2,1,0:T(8,128)(2,1)S(1)}, f16[4,40,1024]{2,1,0:T(8,128)(2,1)S(1)}, u32[]{:S(2)}, u32[]{:S(2)}) collective-permute-start(f16[4,40,1024]{2,1,0:T(8,128)(2,1)S(1)} %bitcast.49), channel_id=1, source_target_pairs={{0,2},{2,0},{4,6},{6,4},{8,10},{10,8},{12,14},{14,12},{1,3},{3,1},... | collective-permute-start | bytes 983048 | tf_op jit(solution)/shard_map/ppermute | solution.py:39
  43.1 3.5 %collective-permute-done.11 = f16[40,1024]{1,0:T(8,128)(2,1)S(1)} collective-permute-done((f16[40,1024]{1,0:T(8,128)(2,1)S(1)}, f16[40,1024]{1,0:T(8,128)(2,1)S(1)}, u32[]{:S(2)}, u32[]{:S(2)}) %collective-permute-start.11) | collective-permute-done | bytes 81952 | tf_op jit(solution)/shard_map/ppermute | solution.py:39
  46.7 1.3 %collective-permute-done.9 = f16[40,1024]{1,0:T(8,128)(2,1)S(1)} collective-permute-done((f16[40,1024]{1,0:T(8,128)(2,1)S(1)}, f16[40,1024]{1,0:T(8,128)(2,1)S(1)}, u32[]{:S(2)}, u32[]{:S(2)}) %collective-permute-start.9) | collective-permute-done | bytes 81952 | tf_op jit(solution)/shard_map/ppermute | solution.py:39
  48.1 2.7 %collective-permute-start.13 = (bf16[40,1024]{1,0:T(8,128)(2,1)S(1)}, bf16[40,1024]{1,0:T(8,128)(2,1)S(1)}, u32[]{:S(2)}, u32[]{:S(2)}) collective-permute-start(bf16[40,1024]{1,0:T(8,128)(2,1)S(1)} %fusion.13), channel_id=1, source_target_pairs={{0,8},{2,10},{4,12},{6,14},{8,0},{10,2},{12,4},{14,6},{1,9},{3,11}... | collective-permute-start | bytes 245768 | tf_op jit(solution)/shard_map/ppermute | solution.py:39
  50.8 1.7 %collective-permute-start.14 = (bf16[40,1024]{1,0:T(8,128)(2,1)S(1)}, bf16[40,1024]{1,0:T(8,128)(2,1)S(1)}, u32[]{:S(2)}, u32[]{:S(2)}) collective-permute-start(bf16[40,1024]{1,0:T(8,128)(2,1)S(1)} %fusion.13), channel_id=1, source_target_pairs={{0,12},{2,14},{4,8},{6,10},{8,4},{10,6},{12,0},{14,2},{1,13},{3,15... | collective-permute-start | bytes 245768 | tf_op jit(solution)/shard_map/ppermute | solution.py:39
  52.5 4.8 %fetch_cache.3.refs_2_ = bf16[8,2048,512]{2,1,0:T(8,128)(2,1)S(1)} custom-call(s32[42]{0:T(128)S(1)} %concatenate.3.meta, bf16[1,8,2048,1024]{3,2,1,0:T(8,128)(2,1)} %cache_ref.3), custom_call_target="tpu_custom_call" | custom-call | bytes 16777216 | tf_op jit(solution)/shard_map/fetch_cache/pallas_call | solution.py:149
  57.4 1.2 collective-permute-start.22
  58.8 2.6 %collective-permute-start.17 = (f16[40,1024]{1,0:T(8,128)(2,1)S(1)}, f16[40,1024]{1,0:T(8,128)(2,1)S(1)}, u32[]{:S(2)}, u32[]{:S(2)}) collective-permute-start(f16[40,1024]{1,0:T(8,128)(2,1)S(1)} %get-tuple-element.65), channel_id=1, source_target_pairs={{0,8},{2,10},{4,12},{6,14},{8,0},{10,2},{12,4},{14,6},{1,9},{3,11}... | collective-permute-start | bytes 245768 | tf_op jit(solution)/shard_map/ppermute | solution.py:39
  61.4 1.8 %collective-permute-start.18 = (f16[40,1024]{1,0:T(8,128)(2,1)S(1)}, f16[40,1024]{1,0:T(8,128)(2,1)S(1)}, u32[]{:S(2)}, u32[]{:S(2)}) collective-permute-start(f16[40,1024]{1,0:T(8,128)(2,1)S(1)} %get-tuple-element.66), channel_id=1, source_target_pairs={{0,12},{2,14},{4,8},{6,10},{8,4},{10,6},{12,0},{14,2},{1,13},{3,15... | collective-permute-start | bytes 245768 | tf_op jit(solution)/shard_map/ppermute | solution.py:39
  63.2 1.7 %collective-permute-done.16 = f16[40,1024]{1,0:T(8,128)(2,1)S(1)} collective-permute-done((f16[40,1024]{1,0:T(8,128)(2,1)S(1)}, f16[40,1024]{1,0:T(8,128)(2,1)S(1)}, u32[]{:S(2)}, u32[]{:S(2)}) %collective-permute-start.16) | collective-permute-done | bytes 81952 | tf_op jit(solution)/shard_map/ppermute | solution.py:39
  64.9 3.2 %collective-permute-done.18 = f16[40,1024]{1,0:T(8,128)(2,1)S(1)} collective-permute-done((f16[40,1024]{1,0:T(8,128)(2,1)S(1)}, f16[40,1024]{1,0:T(8,128)(2,1)S(1)}, u32[]{:S(2)}, u32[]{:S(2)}) %collective-permute-start.18) | collective-permute-done | bytes 81952 | tf_op jit(solution)/shard_map/ppermute | solution.py:39
  68.1 2.2 %collective-permute-start.19 = (bf16[40,1024]{1,0:T(8,128)(2,1)S(1)}, bf16[40,1024]{1,0:T(8,128)(2,1)S(1)}, u32[]{:S(2)}, u32[]{:S(2)}) collective-permute-start(bf16[40,1024]{1,0:T(8,128)(2,1)S(1)} %fusion.6), channel_id=1, source_target_pairs={{0,4},{2,6},{4,0},{6,2},{8,12},{10,14},{12,8},{14,10},{1,5},{3,7},... | collective-permute-start | bytes 245768 | tf_op jit(solution)/shard_map/ppermute | solution.py:39
  71.0 1.8 %collective-permute-start.21 = (bf16[40,1024]{1,0:T(8,128)(2,1)S(1)}, bf16[40,1024]{1,0:T(8,128)(2,1)S(1)}, u32[]{:S(2)}, u32[]{:S(2)}) collective-permute-start(bf16[40,1024]{1,0:T(8,128)(2,1)S(1)} %fusion.6), channel_id=1, source_target_pairs={{0,12},{2,14},{4,8},{6,10},{8,4},{10,6},{12,0},{14,2},{1,13},{3,15... | collective-permute-start | bytes 245768 | tf_op jit(solution)/shard_map/ppermute | solution.py:39
  72.8 7.5 %attend.4 = bf16[4,64,1152]{2,1,0:T(8,128)(2,1)S(1)} custom-call(s32[42]{0:T(128)S(1)} %concatenate.3.meta, bf16[4,40,1024]{2,1,0:T(8,128)(2,1)S(1)} %pad_maximum_fusion.refs_0_, bf16[4,40,1024]{2,1,0:T(8,128)(2,1)S(1)} %collective-permute-done.22.refs_1_, bf16[8,2048,512]{2,1,0:T(8,128)(2,1)S(1)} %fetch_cache.3.refs_2_, ...), custom_call_target="tpu_custom_call" | custom-call | flops 4294967296 | bytes 8388608 | tf_op jit(solution)/shard_map/attend/pallas_call | solution.py:449
  80.7 1.7 %collective-permute-start.24 = (bf16[4,64,1152]{2,1,0:T(8,128)(2,1)S(1)}, bf16[4,64,1152]{2,1,0:T(8,128)(2,1)S(1)}, u32[]{:S(2)}, u32[]{:S(2)}) collective-permute-start(bf16[4,64,1152]{2,1,0:T(8,128)(2,1)S(1)} %attend.4), channel_id=1, source_target_pairs={{0,2},{2,0},{4,6},{6,4},{8,10},{10,8},{12,14},{14,12},{1,3},{3,1},... | collective-permute-start | bytes 1769480 | tf_op jit(solution)/shard_map/ppermute | solution.py:39
  82.4 7.6 %attend.5.refs_0_ = bf16[4,64,1152]{2,1,0:T(8,128)(2,1)S(1)} custom-call(s32[42]{0:T(128)S(1)} %concatenate.3.meta, bf16[4,40,1024]{2,1,0:T(8,128)(2,1)S(1)} %pad_maximum_fusion.refs_0_, bf16[4,40,1024]{2,1,0:T(8,128)(2,1)S(1)} %collective-permute-done.22.refs_1_, bf16[8,2048,512]{2,1,0:T(8,128)(2,1)S(1)} %fetch_cache.3.refs_2_, ...), custom_call_target="tpu_custom_call" | custom-call | flops 4294967296 | bytes 8388608 | tf_op jit(solution)/shard_map/attend/pallas_call | solution.py:449
  90.1 7.7 %attend.6 = bf16[4,64,1152]{2,1,0:T(8,128)(2,1)S(1)} custom-call(s32[42]{0:T(128)S(1)} %concatenate.3.meta, bf16[4,40,1024]{2,1,0:T(8,128)(2,1)S(1)} %pad_maximum_fusion.1.refs_0_, bf16[4,40,1024]{2,1,0:T(8,128)(2,1)S(1)} %collective-permute-done.23.refs_1_, bf16[8,2048,512]{2,1,0:T(8,128)(2,1)S(1)} %fetch_cache.2.refs_2_, ...), custom_call_target="tpu_custom_call" | custom-call | flops 4294967296 | bytes 8388608 | tf_op jit(solution)/shard_map/attend/pallas_call | solution.py:449
  98.5 1.4 %merge.2 = (bf16[64,1152]{1,0:T(8,128)(2,1)S(1)}, bf16[64,1152]{1,0:T(8,128)(2,1)S(1)}, bf16[64,1152]{1,0:T(8,128)(2,1)S(1)}, bf16[64,1152]{1,0:T(8,128)(2,1)S(1)}) custom-call(bf16[4,64,1152]{2,1,0:T(8,128)(2,1)S(1)} %attend.5.refs_0_, bf16[4,64,1152]{2,1,0:T(8,128)(2,1)S(1)} %collective-permute-done.24.refs_1_), custom_call_target="tpu_custom_call" | custom-call | tf_op jit(solution)/shard_map/merge/pallas_call | solution.py:280
  99.9 1.2 collective-permute-start.25
  101.1 1.6 %collective-permute-start.26 = (bf16[64,1152]{1,0:T(8,128)(2,1)S(1)}, bf16[64,1152]{1,0:T(8,128)(2,1)S(1)}, u32[]{:S(2)}, u32[]{:S(2)}) collective-permute-start(bf16[64,1152]{1,0:T(8,128)(2,1)S(1)} %get-tuple-element.78), channel_id=1, source_target_pairs={{0,8},{2,10},{4,12},{6,14},{8,0},{10,2},{12,4},{14,6},{1,9},{3,11}... | collective-permute-start | bytes 442376 | tf_op jit(solution)/shard_map/ppermute | solution.py:39
  102.6 1.7 %collective-permute-start.27 = (bf16[64,1152]{1,0:T(8,128)(2,1)S(1)}, bf16[64,1152]{1,0:T(8,128)(2,1)S(1)}, u32[]{:S(2)}, u32[]{:S(2)}) collective-permute-start(bf16[64,1152]{1,0:T(8,128)(2,1)S(1)} %get-tuple-element.79), channel_id=1, source_target_pairs={{0,12},{2,14},{4,8},{6,10},{8,4},{10,6},{12,0},{14,2},{1,13},{3,15... | collective-permute-start | bytes 442376 | tf_op jit(solution)/shard_map/ppermute | solution.py:39
  104.3 7.7 %attend.7.refs_0_ = bf16[4,64,1152]{2,1,0:T(8,128)(2,1)S(1)} custom-call(s32[42]{0:T(128)S(1)} %concatenate.3.meta, bf16[4,40,1024]{2,1,0:T(8,128)(2,1)S(1)} %pad_maximum_fusion.1.refs_0_, bf16[4,40,1024]{2,1,0:T(8,128)(2,1)S(1)} %collective-permute-done.23.refs_1_, bf16[8,2048,512]{2,1,0:T(8,128)(2,1)S(1)} %fetch_cache.2.refs_2_, ...), custom_call_target="tpu_custom_call" | custom-call | flops 4294967296 | bytes 8388608 | tf_op jit(solution)/shard_map/attend/pallas_call | solution.py:449
  112.0 1.4 %merge.3 = (bf16[64,1152]{1,0:T(8,128)(2,1)S(1)}, bf16[64,1152]{1,0:T(8,128)(2,1)S(1)}, bf16[64,1152]{1,0:T(8,128)(2,1)S(1)}, bf16[64,1152]{1,0:T(8,128)(2,1)S(1)}) custom-call(bf16[4,64,1152]{2,1,0:T(8,128)(2,1)S(1)} %attend.7.refs_0_, bf16[4,64,1152]{2,1,0:T(8,128)(2,1)S(1)} %collective-permute-done.28.refs_1_), custom_call_target="tpu_custom_call" | custom-call | tf_op jit(solution)/shard_map/merge/pallas_call | solution.py:280
  113.5 1.0 collective-permute-start.30
  114.5 3.4 %collective-permute-start.31 = (bf16[64,1152]{1,0:T(8,128)(2,1)S(1)}, bf16[64,1152]{1,0:T(8,128)(2,1)S(1)}, u32[]{:S(2)}, u32[]{:S(2)}) collective-permute-start(bf16[64,1152]{1,0:T(8,128)(2,1)S(1)} %get-tuple-element.84), channel_id=1, source_target_pairs={{0,12},{2,14},{4,8},{6,10},{8,4},{10,6},{12,0},{14,2},{1,13},{3,15... | collective-permute-start | bytes 442376 | tf_op jit(solution)/shard_map/ppermute | solution.py:39
  117.9 1.0 finish.2.refs_0_
  119.0 1.0 collective-permute-done.29.refs_2_
  120.0 3.0 %collective-permute-done.30.refs_3_ = bf16[64,1152]{1,0:T(8,128)(2,1)S(1)} collective-permute-done((bf16[64,1152]{1,0:T(8,128)(2,1)S(1)}, bf16[64,1152]{1,0:T(8,128)(2,1)S(1)}, u32[]{:S(2)}, u32[]{:S(2)}) %collective-permute-start.30) | collective-permute-done | bytes 147488 | tf_op jit(solution)/shard_map/ppermute | solution.py:39
  123.0 1.7 %finish.3 = bf16[1,64,2048]{2,1,0:T(8,128)(2,1)} custom-call(s32[42]{0:T(128)S(1)} %concatenate.3.meta, bf16[1,64,1024]{2,1,0:T(8,128)(2,1)S(1)} %finish.2.refs_0_, bf16[64,1152]{1,0:T(8,128)(2,1)S(1)} %get-tuple-element.81.refs_1_, bf16[64,1152]{1,0:T(8,128)(2,1)S(1)} %collective-permute-done.29.refs_2_, ...), custom_call_target="tpu_custom_call" | custom-call | tf_op jit(solution)/shard_map/finish/pallas_call | solution.py:492
  (45 shorter events, 3.9 us)
Async XLA Ops:
  0.0 7.0 %collective-permute-start = (bf16[1,64,5120]{2,1,0:T(8,128)(2,1)}, bf16[1,64,5120]{2,1,0:T(8,128)(2,1)S(1)}, u32[]{:S(2)}, u32[]{:S(2)}) collective-permute-start(bf16[1,64,5120]{2,1,0:T(8,128)(2,1)} %param.9), channel_id=1, source_target_pairs={{0,16},{1,17},{2,18},{3,19},{4,20},{5,21},{6,22},{7,23},{8,24},{9,... | collective-permute-start | bytes 1966088 | tf_op jit(solution)/shard_map/ppermute | solution.py:534
  7.8 7.4 %collective-permute-start.1 = (bf16[64,640]{1,0:T(8,128)(2,1)S(1)}, bf16[64,640]{1,0:T(8,128)(2,1)S(1)}, u32[]{:S(2)}, u32[]{:S(2)}) collective-permute-start(bf16[64,640]{1,0:T(8,128)(2,1)S(1)} %get-tuple-element.46), channel_id=1, source_target_pairs={{0,4},{2,6},{4,0},{6,2},{8,12},{10,14},{12,8},{14,10},{1,5},{3,7},... | collective-permute-start | bytes 245768 | tf_op jit(solution)/shard_map/ppermute | solution.py:39
  10.2 9.4 %collective-permute-start.2 = (bf16[64,640]{1,0:T(8,128)(2,1)S(1)}, bf16[64,640]{1,0:T(8,128)(2,1)S(1)}, u32[]{:S(2)}, u32[]{:S(2)}) collective-permute-start(bf16[64,640]{1,0:T(8,128)(2,1)S(1)} %get-tuple-element.47), channel_id=1, source_target_pairs={{0,8},{2,10},{4,12},{6,14},{8,0},{10,2},{12,4},{14,6},{1,9},{3,11}... | collective-permute-start | bytes 245768 | tf_op jit(solution)/shard_map/ppermute | solution.py:39
  12.8 13.5 %collective-permute-start.3 = (bf16[64,640]{1,0:T(8,128)(2,1)S(1)}, bf16[64,640]{1,0:T(8,128)(2,1)S(1)}, u32[]{:S(2)}, u32[]{:S(2)}) collective-permute-start(bf16[64,640]{1,0:T(8,128)(2,1)S(1)} %get-tuple-element.48), channel_id=1, source_target_pairs={{0,12},{2,14},{4,8},{6,10},{8,4},{10,6},{12,0},{14,2},{1,13},{3,15... | collective-permute-start | bytes 245768 | tf_op jit(solution)/shard_map/ppermute | solution.py:39
  12.8 13.5 %collective-permute-start.4 = (bf16[64,640]{1,0:T(8,128)(2,1)S(1)}, bf16[64,640]{1,0:T(8,128)(2,1)S(1)}, u32[]{:S(2)}, u32[]{:S(2)}) collective-permute-start(bf16[64,640]{1,0:T(8,128)(2,1)S(1)} %get-tuple-element.49), channel_id=1, source_target_pairs={{0,2},{2,0},{4,6},{6,4},{8,10},{10,8},{12,14},{14,12},{1,3},{3,1},... | collective-permute-start | bytes 245768 | tf_op jit(solution)/shard_map/ppermute | solution.py:39
  14.5 11.8 %collective-permute-start.5 = (bf16[64,640]{1,0:T(8,128)(2,1)S(1)}, bf16[64,640]{1,0:T(8,128)(2,1)S(1)}, u32[]{:S(2)}, u32[]{:S(2)}) collective-permute-start(bf16[64,640]{1,0:T(8,128)(2,1)S(1)} %get-tuple-element.50), channel_id=1, source_target_pairs={{0,6},{2,4},{4,2},{6,0},{8,14},{10,12},{12,10},{14,8},{1,7},{3,5},... | collective-permute-start | bytes 245768 | tf_op jit(solution)/shard_map/ppermute | solution.py:39
  15.2 11.1 %collective-permute-start.6 = (bf16[64,640]{1,0:T(8,128)(2,1)S(1)}, bf16[64,640]{1,0:T(8,128)(2,1)S(1)}, u32[]{:S(2)}, u32[]{:S(2)}) collective-permute-start(bf16[64,640]{1,0:T(8,128)(2,1)S(1)} %get-tuple-element.51), channel_id=1, source_target_pairs={{0,10},{2,8},{4,14},{6,12},{8,2},{10,0},{12,6},{14,4},{1,11},{3,9}... | collective-permute-start | bytes 245768 | tf_op jit(solution)/shard_map/ppermute | solution.py:39
  19.6 7.4 %collective-permute-start.7 = (bf16[64,640]{1,0:T(8,128)(2,1)S(1)}, bf16[64,640]{1,0:T(8,128)(2,1)S(1)}, u32[]{:S(2)}, u32[]{:S(2)}) collective-permute-start(bf16[64,640]{1,0:T(8,128)(2,1)S(1)} %get-tuple-element.52), channel_id=1, source_target_pairs={{0,14},{2,12},{4,10},{6,8},{8,6},{10,4},{12,2},{14,0},{1,15},{3,13... | collective-permute-start | bytes 245768 | tf_op jit(solution)/shard_map/ppermute | solution.py:39
  29.8 7.1 %collective-permute-start.8 = (f16[4,40,1024]{2,1,0:T(8,128)(2,1)S(1)}, f16[4,40,1024]{2,1,0:T(8,128)(2,1)S(1)}, u32[]{:S(2)}, u32[]{:S(2)}) collective-permute-start(f16[4,40,1024]{2,1,0:T(8,128)(2,1)S(1)} %bitcast.50), channel_id=1, source_target_pairs={{0,2},{2,0},{4,6},{6,4},{8,10},{10,8},{12,14},{14,12},{1,3},{3,1},... | collective-permute-start | bytes 983048 | tf_op jit(solution)/shard_map/ppermute | solution.py:39
  37.1 6.0 %collective-permute-start.10 = (f16[40,1024]{1,0:T(8,128)(2,1)S(1)}, f16[40,1024]{1,0:T(8,128)(2,1)S(1)}, u32[]{:S(2)}, u32[]{:S(2)}) collective-permute-start(f16[40,1024]{1,0:T(8,128)(2,1)S(1)} %get-tuple-element.90), channel_id=1, source_target_pairs={{0,8},{2,10},{4,12},{6,14},{8,0},{10,2},{12,4},{14,6},{1,9},{3,11}... | collective-permute-start | bytes 245768 | tf_op jit(solution)/shard_map/ppermute | solution.py:39
  39.7 7.0 %collective-permute-start.11 = (f16[40,1024]{1,0:T(8,128)(2,1)S(1)}, f16[40,1024]{1,0:T(8,128)(2,1)S(1)}, u32[]{:S(2)}, u32[]{:S(2)}) collective-permute-start(f16[40,1024]{1,0:T(8,128)(2,1)S(1)} %get-tuple-element.89), channel_id=1, source_target_pairs={{0,12},{2,14},{4,8},{6,10},{8,4},{10,6},{12,0},{14,2},{1,13},{3,15... | collective-permute-start | bytes 245768 | tf_op jit(solution)/shard_map/ppermute | solution.py:39
  41.2 6.7 %collective-permute-start.9 = (f16[40,1024]{1,0:T(8,128)(2,1)S(1)}, f16[40,1024]{1,0:T(8,128)(2,1)S(1)}, u32[]{:S(2)}, u32[]{:S(2)}) collective-permute-start(f16[40,1024]{1,0:T(8,128)(2,1)S(1)} %get-tuple-element.88), channel_id=1, source_target_pairs={{0,4},{2,6},{4,0},{6,2},{8,12},{10,14},{12,8},{14,10},{1,5},{3,7},... | collective-permute-start | bytes 245768 | tf_op jit(solution)/shard_map/ppermute | solution.py:39
  41.3 17.3 %collective-permute-start.15 = (f16[4,40,1024]{2,1,0:T(8,128)(2,1)S(1)}, f16[4,40,1024]{2,1,0:T(8,128)(2,1)S(1)}, u32[]{:S(2)}, u32[]{:S(2)}) collective-permute-start(f16[4,40,1024]{2,1,0:T(8,128)(2,1)S(1)} %bitcast.49), channel_id=1, source_target_pairs={{0,2},{2,0},{4,6},{6,4},{8,10},{10,8},{12,14},{14,12},{1,3},{3,1},... | collective-permute-start | bytes 983048 | tf_op jit(solution)/shard_map/ppermute | solution.py:39
  48.0 9.3 %collective-permute-start.12 = (bf16[40,1024]{1,0:T(8,128)(2,1)S(1)}, bf16[40,1024]{1,0:T(8,128)(2,1)S(1)}, u32[]{:S(2)}, u32[]{:S(2)}) collective-permute-start(bf16[40,1024]{1,0:T(8,128)(2,1)S(1)} %fusion.13), channel_id=1, source_target_pairs={{0,4},{2,6},{4,0},{6,2},{8,12},{10,14},{12,8},{14,10},{1,5},{3,7},... | collective-permute-start | bytes 245768 | tf_op jit(solution)/shard_map/ppermute | solution.py:39
  48.1 9.2 %collective-permute-start.13 = (bf16[40,1024]{1,0:T(8,128)(2,1)S(1)}, bf16[40,1024]{1,0:T(8,128)(2,1)S(1)}, u32[]{:S(2)}, u32[]{:S(2)}) collective-permute-start(bf16[40,1024]{1,0:T(8,128)(2,1)S(1)} %fusion.13), channel_id=1, source_target_pairs={{0,8},{2,10},{4,12},{6,14},{8,0},{10,2},{12,4},{14,6},{1,9},{3,11}... | collective-permute-start | bytes 245768 | tf_op jit(solution)/shard_map/ppermute | solution.py:39
  50.8 6.5 %collective-permute-start.14 = (bf16[40,1024]{1,0:T(8,128)(2,1)S(1)}, bf16[40,1024]{1,0:T(8,128)(2,1)S(1)}, u32[]{:S(2)}, u32[]{:S(2)}) collective-permute-start(bf16[40,1024]{1,0:T(8,128)(2,1)S(1)} %fusion.13), channel_id=1, source_target_pairs={{0,12},{2,14},{4,8},{6,10},{8,4},{10,6},{12,0},{14,2},{1,13},{3,15... | collective-permute-start | bytes 245768 | tf_op jit(solution)/shard_map/ppermute | solution.py:39
  57.4 15.4 %collective-permute-start.22 = (bf16[4,40,1024]{2,1,0:T(8,128)(2,1)S(1)}, bf16[4,40,1024]{2,1,0:T(8,128)(2,1)S(1)}, u32[]{:S(2)}, u32[]{:S(2)}) collective-permute-start(bf16[4,40,1024]{2,1,0:T(8,128)(2,1)S(1)} %pad_maximum_fusion.refs_0_), channel_id=1, source_target_pairs={{0,2},{2,0},{4,6},{6,4},{8,10},{10,8},{12,14},{14,12},{1,3},{3,1},... | collective-permute-start | bytes 983048 | tf_op jit(solution)/shard_map/ppermute | solution.py:39
  58.7 6.2 %collective-permute-start.16 = (f16[40,1024]{1,0:T(8,128)(2,1)S(1)}, f16[40,1024]{1,0:T(8,128)(2,1)S(1)}, u32[]{:S(2)}, u32[]{:S(2)}) collective-permute-start(f16[40,1024]{1,0:T(8,128)(2,1)S(1)} %get-tuple-element.64), channel_id=1, source_target_pairs={{0,4},{2,6},{4,0},{6,2},{8,12},{10,14},{12,8},{14,10},{1,5},{3,7},... | collective-permute-start | bytes 245768 | tf_op jit(solution)/shard_map/ppermute | solution.py:39
  58.8 6.1 %collective-permute-start.17 = (f16[40,1024]{1,0:T(8,128)(2,1)S(1)}, f16[40,1024]{1,0:T(8,128)(2,1)S(1)}, u32[]{:S(2)}, u32[]{:S(2)}) collective-permute-start(f16[40,1024]{1,0:T(8,128)(2,1)S(1)} %get-tuple-element.65), channel_id=1, source_target_pairs={{0,8},{2,10},{4,12},{6,14},{8,0},{10,2},{12,4},{14,6},{1,9},{3,11}... | collective-permute-start | bytes 245768 | tf_op jit(solution)/shard_map/ppermute | solution.py:39
  61.4 6.7 %collective-permute-start.18 = (f16[40,1024]{1,0:T(8,128)(2,1)S(1)}, f16[40,1024]{1,0:T(8,128)(2,1)S(1)}, u32[]{:S(2)}, u32[]{:S(2)}) collective-permute-start(f16[40,1024]{1,0:T(8,128)(2,1)S(1)} %get-tuple-element.66), channel_id=1, source_target_pairs={{0,12},{2,14},{4,8},{6,10},{8,4},{10,6},{12,0},{14,2},{1,13},{3,15... | collective-permute-start | bytes 245768 | tf_op jit(solution)/shard_map/ppermute | solution.py:39
  68.1 12.1 %collective-permute-start.19 = (bf16[40,1024]{1,0:T(8,128)(2,1)S(1)}, bf16[40,1024]{1,0:T(8,128)(2,1)S(1)}, u32[]{:S(2)}, u32[]{:S(2)}) collective-permute-start(bf16[40,1024]{1,0:T(8,128)(2,1)S(1)} %fusion.6), channel_id=1, source_target_pairs={{0,4},{2,6},{4,0},{6,2},{8,12},{10,14},{12,8},{14,10},{1,5},{3,7},... | collective-permute-start | bytes 245768 | tf_op jit(solution)/shard_map/ppermute | solution.py:39
  70.3 9.9 %collective-permute-start.20 = (bf16[40,1024]{1,0:T(8,128)(2,1)S(1)}, bf16[40,1024]{1,0:T(8,128)(2,1)S(1)}, u32[]{:S(2)}, u32[]{:S(2)}) collective-permute-start(bf16[40,1024]{1,0:T(8,128)(2,1)S(1)} %fusion.6), channel_id=1, source_target_pairs={{0,8},{2,10},{4,12},{6,14},{8,0},{10,2},{12,4},{14,6},{1,9},{3,11}... | collective-permute-start | bytes 245768 | tf_op jit(solution)/shard_map/ppermute | solution.py:39
  71.0 9.3 %collective-permute-start.21 = (bf16[40,1024]{1,0:T(8,128)(2,1)S(1)}, bf16[40,1024]{1,0:T(8,128)(2,1)S(1)}, u32[]{:S(2)}, u32[]{:S(2)}) collective-permute-start(bf16[40,1024]{1,0:T(8,128)(2,1)S(1)} %fusion.6), channel_id=1, source_target_pairs={{0,12},{2,14},{4,8},{6,10},{8,4},{10,6},{12,0},{14,2},{1,13},{3,15... | collective-permute-start | bytes 245768 | tf_op jit(solution)/shard_map/ppermute | solution.py:39
  80.3 9.7 %collective-permute-start.23 = (bf16[4,40,1024]{2,1,0:T(8,128)(2,1)S(1)}, bf16[4,40,1024]{2,1,0:T(8,128)(2,1)S(1)}, u32[]{:S(2)}, u32[]{:S(2)}) collective-permute-start(bf16[4,40,1024]{2,1,0:T(8,128)(2,1)S(1)} %pad_maximum_fusion.1.refs_0_), channel_id=1, source_target_pairs={{0,2},{2,0},{4,6},{6,4},{8,10},{10,8},{12,14},{14,12},{1,3},{3,1},... | collective-permute-start | bytes 983048 | tf_op jit(solution)/shard_map/ppermute | solution.py:39
  80.7 17.8 %collective-permute-start.24 = (bf16[4,64,1152]{2,1,0:T(8,128)(2,1)S(1)}, bf16[4,64,1152]{2,1,0:T(8,128)(2,1)S(1)}, u32[]{:S(2)}, u32[]{:S(2)}) collective-permute-start(bf16[4,64,1152]{2,1,0:T(8,128)(2,1)S(1)} %attend.4), channel_id=1, source_target_pairs={{0,2},{2,0},{4,6},{6,4},{8,10},{10,8},{12,14},{14,12},{1,3},{3,1},... | collective-permute-start | bytes 1769480 | tf_op jit(solution)/shard_map/ppermute | solution.py:39
  97.8 14.3 %collective-permute-start.28 = (bf16[4,64,1152]{2,1,0:T(8,128)(2,1)S(1)}, bf16[4,64,1152]{2,1,0:T(8,128)(2,1)S(1)}, u32[]{:S(2)}, u32[]{:S(2)}) collective-permute-start(bf16[4,64,1152]{2,1,0:T(8,128)(2,1)S(1)} %attend.6), channel_id=1, source_target_pairs={{0,2},{2,0},{4,6},{6,4},{8,10},{10,8},{12,14},{14,12},{1,3},{3,1},... | collective-permute-start | bytes 1769480 | tf_op jit(solution)/shard_map/ppermute | solution.py:39
  99.9 14.7 %collective-permute-start.25 = (bf16[64,1152]{1,0:T(8,128)(2,1)S(1)}, bf16[64,1152]{1,0:T(8,128)(2,1)S(1)}, u32[]{:S(2)}, u32[]{:S(2)}) collective-permute-start(bf16[64,1152]{1,0:T(8,128)(2,1)S(1)} %get-tuple-element.77), channel_id=1, source_target_pairs={{0,4},{2,6},{4,0},{6,2},{8,12},{10,14},{12,8},{14,10},{1,5},{3,7},... | collective-permute-start | bytes 442376 | tf_op jit(solution)/shard_map/ppermute | solution.py:39
  101.1 16.8 %collective-permute-start.26 = (bf16[64,1152]{1,0:T(8,128)(2,1)S(1)}, bf16[64,1152]{1,0:T(8,128)(2,1)S(1)}, u32[]{:S(2)}, u32[]{:S(2)}) collective-permute-start(bf16[64,1152]{1,0:T(8,128)(2,1)S(1)} %get-tuple-element.78), channel_id=1, source_target_pairs={{0,8},{2,10},{4,12},{6,14},{8,0},{10,2},{12,4},{14,6},{1,9},{3,11}... | collective-permute-start | bytes 442376 | tf_op jit(solution)/shard_map/ppermute | solution.py:39
  102.6 15.3 %collective-permute-start.27 = (bf16[64,1152]{1,0:T(8,128)(2,1)S(1)}, bf16[64,1152]{1,0:T(8,128)(2,1)S(1)}, u32[]{:S(2)}, u32[]{:S(2)}) collective-permute-start(bf16[64,1152]{1,0:T(8,128)(2,1)S(1)} %get-tuple-element.79), channel_id=1, source_target_pairs={{0,12},{2,14},{4,8},{6,10},{8,4},{10,6},{12,0},{14,2},{1,13},{3,15... | collective-permute-start | bytes 442376 | tf_op jit(solution)/shard_map/ppermute | solution.py:39
  113.5 6.5 %collective-permute-start.29 = (bf16[64,1152]{1,0:T(8,128)(2,1)S(1)}, bf16[64,1152]{1,0:T(8,128)(2,1)S(1)}, u32[]{:S(2)}, u32[]{:S(2)}) collective-permute-start(bf16[64,1152]{1,0:T(8,128)(2,1)S(1)} %get-tuple-element.82), channel_id=1, source_target_pairs={{0,4},{2,6},{4,0},{6,2},{8,12},{10,14},{12,8},{14,10},{1,5},{3,7},... | collective-permute-start | bytes 442376 | tf_op jit(solution)/shard_map/ppermute | solution.py:39
  113.5 9.4 %collective-permute-start.30 = (bf16[64,1152]{1,0:T(8,128)(2,1)S(1)}, bf16[64,1152]{1,0:T(8,128)(2,1)S(1)}, u32[]{:S(2)}, u32[]{:S(2)}) collective-permute-start(bf16[64,1152]{1,0:T(8,128)(2,1)S(1)} %get-tuple-element.83), channel_id=1, source_target_pairs={{0,8},{2,10},{4,12},{6,14},{8,0},{10,2},{12,4},{14,6},{1,9},{3,11}... | collective-permute-start | bytes 442376 | tf_op jit(solution)/shard_map/ppermute | solution.py:39
  114.5 8.4 %collective-permute-start.31 = (bf16[64,1152]{1,0:T(8,128)(2,1)S(1)}, bf16[64,1152]{1,0:T(8,128)(2,1)S(1)}, u32[]{:S(2)}, u32[]{:S(2)}) collective-permute-start(bf16[64,1152]{1,0:T(8,128)(2,1)S(1)} %get-tuple-element.84), channel_id=1, source_target_pairs={{0,12},{2,14},{4,8},{6,10},{8,4},{10,6},{12,0},{14,2},{1,13},{3,15... | collective-permute-start | bytes 442376 | tf_op jit(solution)/shard_map/ppermute | solution.py:39
